TPU v7x, 128 devices: a whole 4x4x4 slice. The times are simulated.
128 devices in a mesh: dp: 16 (over z, x_hi, core), head: 8 (over y, x_lo).
Axes of the slice: x: 4 (x_hi: 2, x_lo: 2; x = x_hi * 2 + x_lo), y: 4, z: 4, core: 2. Of those that a mesh axis runs over, the one named last changes fastest.
Arguments:
- query_rows: bfloat16 [24576, 2048], P(('dp', 'head')), may hold values from -9 to 9
- key_rows: bfloat16 [24576, 2048], P(('dp', 'head')), may hold values from -9 to 9
- value_rows: bfloat16 [24576, 2048], P(('dp', 'head')), may hold values from -6 to 6
- out_grad: bfloat16 [24576, 3072], P(('dp', 'head')), may hold values from -24 to 24
- out_weight: bfloat16 [2048, 3072], P('head'), may hold values from -0.109375 to 0.109375
- clip_len: int32 [32], replicated, may hold values from 256 to 1024, as said below
- clip_group: int32 [32], replicated, may hold values from 0 to 15, as said below
- clip_start: int32 [32], replicated, may hold values from 0 to 1280, as said below
Outputs:
- grad_query: bfloat16 [24576, 2048], P(('dp', 'head'))
- grad_key: bfloat16 [24576, 2048], P(('dp', 'head'))
- grad_value: bfloat16 [24576, 2048], P(('dp', 'head'))
- grad_weight: float32 [2048, 3072], P('head', 'dp')
Inputs may be any that keep to these rules, and one draw needn't show every extreme that they name: `clip_len`: clip 2 g starts in group g and stays there, with 6 to 8 units of 128 rows; clip 2 g + 1 has 2 to 4 units; some clip 2 g has 1024 rows and some clip 2 g + 1 has 512 rows. clip_group[2 g] = g and clip_group[2 g + 1] = (g + r) modulo the number of data groups, with one r common to all groups, 1 <= r <= half the number of data groups. `clip_start`: the two clips of a group lie in index order without intersection inside its 1536 rows, each start a multiple of 128.
All inputs are finite; a program needn't handle non-finite values.
Results may differ from a plain program's by a relative error of at most 0.029.
Values may be sent and summed in bfloat16 or wider, within the bound.
No kernel may reach another device: no remote copies, remote signals or barrier semaphores. Data moves between devices by JAX's collectives and lax.ppermute only.
A program may use at most 128 MiB of HBM per device.

v0:
```python
import functools

import jax
import jax.numpy as jnp
from jax import lax
from jax.experimental import pallas as pl
from jax.experimental.pallas import tpu as pltpu
from jax.sharding import PartitionSpec as P

D = 3072
HD = 128
FEAT = 256
ROWS = 192
GROUP = 1536
HOME = 1024
MOVE = 512
HOME_MIN = 768
MOVE_MIN = 256
QB = 256
SCALE = HD ** (-0.5)
EXP2_SCALE = SCALE * 1.4426950408889634
NEG_BIG = -1e30
NN = (((1,), (0,)), ((), ()))
NT = (((1,), (1,)), ((), ()))
VMEM = pl.BlockSpec(memory_space=pltpu.VMEM)
SMEM = pl.BlockSpec(memory_space=pltpu.SMEM)
PARAMS = pltpu.CompilerParams(vmem_limit_bytes=56 * 1024 * 1024)


def dot(a, b, dims=NN):
    return lax.dot_general(a, b, dims, preferred_element_type=jnp.float32)


def flip(x):
    return x.astype(jnp.float32).T.astype(x.dtype)


def shifted(x, axis, distance):
    n = lax.axis_size(axis)
    return lax.ppermute(x, axis, [((i - distance) % n, i) for i in range(n)])


def swapped(x):
    return lax.ppermute(x, "head", [(i, i ^ 1) for i in range(8)])


def columns(which, head):
    return pl.ds(pl.multiple_of(which * FEAT + head * HD, HD), HD)


def forward_clip(read, length, rows, sure, prob_ref, att_ref, att_first):
    def one_head(head, _):
        k = read(1, head, 0, rows)
        v_t = flip(read(2, head, 0, rows))

        def block(step, _):
            first = pl.multiple_of(step * QB, QB)
            q = read(0, head, first, QB)
            scores = dot(k, q, NT)
            key = lax.broadcasted_iota(jnp.int32, (rows - sure, QB), 0) + sure
            scores = jnp.concatenate(
                [scores[:sure], jnp.where(key < length, scores[sure:], NEG_BIG)], axis=0
            )
            peak = jnp.max(scores, axis=0, keepdims=True)
            unnorm = jnp.exp2((scores - peak) * EXP2_SCALE)
            total = jnp.sum(unnorm, axis=0, keepdims=True)
            query = lax.broadcasted_iota(jnp.int32, (1, QB), 1) + first
            prob = (unnorm * jnp.where(query < length, 1.0 / total, 0.0)).astype(jnp.bfloat16)
            prob_ref[head, :, pl.ds(first, QB)] = prob
            att = dot(v_t, prob).T.astype(jnp.bfloat16)
            there = pl.ds(pl.multiple_of(att_first + first, 128), QB)
            att_ref[there, columns(0, head)] = att
            return 0

        return lax.fori_loop(0, rows // QB, block, 0)

    lax.fori_loop(0, 2, one_head, 0)


def forward_home_kernel(meta_ref, qkv_ref, att_ref, prob_ref):
    home_first, home_len = meta_ref[0], meta_ref[1]

    def read(which, head, first, count):
        start = pl.multiple_of(home_first + first, 128)
        return qkv_ref[pl.ds(start, count), columns(which, head)]

    forward_clip(read, home_len, HOME, HOME_MIN, prob_ref, att_ref, 0)


def forward_home(meta, qkv):
    return pl.pallas_call(
        forward_home_kernel,
        out_shape=(
            jax.ShapeDtypeStruct((HOME, FEAT), jnp.bfloat16),
            jax.ShapeDtypeStruct((2, HOME, HOME), jnp.bfloat16),
        ),
        in_specs=[SMEM, VMEM],
        out_specs=(VMEM, VMEM),
        compiler_params=PARAMS,
        cost_estimate=pl.CostEstimate(
            flops=6_000_000_000, bytes_accessed=8_000_000, transcendentals=2_100_000
        ),
        name="forward_home",
    )(meta, qkv)


def forward_move_kernel(meta_ref, move_ref, home_att_ref, att_ref, prob_ref):
    home_len, arrive_len = meta_ref[1], meta_ref[2]

    def read(which, head, first, count):
        return move_ref[pl.ds(first, count), columns(which, head)]

    att_ref[:HOME, :] = home_att_ref[...]
    att_ref[HOME:, :] = jnp.zeros((GROUP - HOME, FEAT), jnp.bfloat16)
    forward_clip(read, arrive_len, MOVE, MOVE_MIN, prob_ref, att_ref, home_len)


def forward_move(meta, moved, home_att):
    return pl.pallas_call(
        forward_move_kernel,
        out_shape=(
            jax.ShapeDtypeStruct((GROUP, FEAT), jnp.bfloat16),
            jax.ShapeDtypeStruct((2, MOVE, MOVE), jnp.bfloat16),
        ),
        in_specs=[SMEM, VMEM, VMEM],
        out_specs=(VMEM, VMEM),
        compiler_params=PARAMS,
        cost_estimate=pl.CostEstimate(
            flops=1_500_000_000, bytes_accessed=3_000_000, transcendentals=500_000
        ),
        name="forward_move",
    )(meta, moved, home_att)


def grad_att_kernel(count, weight_ref, *refs):
    blocks = refs[:count]
    out_ref, acc = refs[-2:]
    step = pl.program_id(0)

    @pl.when(step == 0)
    def _():
        acc[...] = jnp.zeros_like(acc)

    dy = jnp.concatenate([block[...] for block in blocks], axis=0)
    acc[...] += dot(dy, weight_ref[...], NT)

    @pl.when(step == pl.num_programs(0) - 1)
    def _():
        out_ref[...] = acc[...].astype(jnp.bfloat16)


def grad_att(weight, blocks):
    count = len(blocks)
    total = sum(block.shape[0] for block in blocks)
    wide = D // 4
    return pl.pallas_call(
        functools.partial(grad_att_kernel, count),
        grid=(4,),
        out_shape=jax.ShapeDtypeStruct((total, FEAT), jnp.bfloat16),
        in_specs=[
            pl.BlockSpec((FEAT, wide), lambda j: (0, j)),
            *[pl.BlockSpec((block.shape[0], wide), lambda j: (0, j)) for block in blocks],
        ],
        out_specs=pl.BlockSpec((total, FEAT), lambda j: (0, 0)),
        scratch_shapes=[pltpu.VMEM((total, FEAT), jnp.float32)],
        compiler_params=PARAMS,
        cost_estimate=pl.CostEstimate(
            flops=total * 3_000_000, bytes_accessed=total * 6_500, transcendentals=0
        ),
        name="grad_att",
    )(weight, *blocks)


def place_rows(att_ref, first_ref, rows):
    picked, at = [], 0
    for count in rows:
        first = pl.multiple_of(first_ref[at], 32)
        picked.append(att_ref[pl.ds(first, count), :])
        at += 1
    return flip(jnp.concatenate(picked, axis=0))


def grad_weight_kernel(pieces, first_ref, att_ref, *refs):
    blocks = refs[:-2]
    out_ref, att_t = refs[-2:]

    @pl.when(pl.program_id(0) == 0)
    def _():
        att_t[...] = place_rows(att_ref, first_ref, pieces)

    dy = jnp.concatenate([block[...] for block in blocks], axis=0)
    out_ref[0] = dot(att_t[...], dy)


def grad_weight_part(firsts, att, blocks, pieces):
    total = sum(pieces)
    wide = D // 4
    return pl.pallas_call(
        functools.partial(grad_weight_kernel, pieces),
        grid=(4,),
        out_shape=jax.ShapeDtypeStruct((4, FEAT, wide), jnp.float32),
        in_specs=[
            SMEM,
            pl.BlockSpec((GROUP, FEAT), lambda j: (0, 0)),
            *[pl.BlockSpec((block.shape[0], wide), lambda j: (0, j)) for block in blocks],
        ],
        out_specs=pl.BlockSpec((1, FEAT, wide), lambda j: (j, 0, 0)),
        scratch_shapes=[pltpu.VMEM((FEAT, total), jnp.bfloat16)],
        compiler_params=PARAMS,
        cost_estimate=pl.CostEstimate(
            flops=total * 2_500_000, bytes_accessed=total * 8_000, transcendentals=0
        ),
        name="grad_weight",
    )(firsts, att, *blocks)


def grad_weight_last_kernel(first_ref, att_ref, *refs):
    blocks = refs[:3]
    sum_ref, out_ref, att_t = refs[3:]

    @pl.when(pl.program_id(0) == 0)
    def _():
        att_t[...] = place_rows(att_ref, first_ref, (ROWS,))

    dy = jnp.concatenate([block[...] for block in blocks], axis=0)
    part = sum_ref[0] + dot(att_t[...], dy)
    cut = D // 16
    for xh in range(2):
        for core in range(2):
            at = (2 * xh + core) * cut
            out_ref[core, 0, :, xh * cut : (xh + 1) * cut] = part[:, at : at + cut].astype(
                jnp.bfloat16
            )


def grad_weight_last(firsts, att, blocks, running):
    wide = D // 4
    return pl.pallas_call(
        grad_weight_last_kernel,
        grid=(4,),
        out_shape=jax.ShapeDtypeStruct((2, 4, FEAT, wide // 2), jnp.bfloat16),
        in_specs=[
            SMEM,
            pl.BlockSpec((GROUP, FEAT), lambda j: (0, 0)),
            *[pl.BlockSpec((block.shape[0], wide), lambda j: (0, j)) for block in blocks],
            pl.BlockSpec((1, FEAT, wide), lambda j: (j, 0, 0)),
        ],
        out_specs=pl.BlockSpec((2, 1, FEAT, wide // 2), lambda j: (0, j, 0, 0)),
        scratch_shapes=[pltpu.VMEM((FEAT, ROWS), jnp.bfloat16)],
        compiler_params=PARAMS,
        cost_estimate=pl.CostEstimate(
            flops=600_000_000, bytes_accessed=6_000_000, transcendentals=0
        ),
        name="grad_weight_last",
    )(firsts, att, *blocks, running)


def backward_clip(read, rows, prob_ref, row_first, ga_ref, att_ref, out_ref, key_acc, value_acc):
    def one_head(head, _):
        k_t = flip(read(1, head, 0, rows))
        v = read(2, head, 0, rows)
        key_acc[:rows, :] = jnp.zeros((rows, HD), jnp.float32)
        value_acc[:rows, :] = jnp.zeros((rows, HD), jnp.float32)

        def block(step, _):
            first = pl.multiple_of(step * QB, QB)
            there = pl.ds(pl.multiple_of(row_first + first, 128), QB)
            q = read(0, head, first, QB)
            prob = prob_ref[head, :, pl.ds(first, QB)]
            grad_att = ga_ref[there, columns(0, head)]
            attended = att_ref[there, columns(0, head)]
            product = grad_att.astype(jnp.float32) * attended.astype(jnp.float32)
            row_dot = jnp.sum(product.T, axis=0, keepdims=True)
            grad_prob = dot(v, grad_att, NT)
            grad_score = (prob.astype(jnp.float32) * (grad_prob - row_dot)).astype(jnp.bfloat16)
            value_acc[:rows, :] += dot(prob, grad_att)
            key_acc[:rows, :] += dot(grad_score, q)
            grad_query = (dot(k_t, grad_score) * SCALE).T.astype(jnp.bfloat16)
            out_ref[there, columns(0, head)] = grad_query
            return 0

        lax.fori_loop(0, rows // QB, block, 0)
        whole = pl.ds(pl.multiple_of(row_first, 128), rows)
        out_ref[whole, columns(1, head)] = (key_acc[:rows, :] * SCALE).astype(jnp.bfloat16)
        out_ref[whole, columns(2, head)] = value_acc[:rows, :].astype(jnp.bfloat16)
        return 0

    lax.fori_loop(0, 2, one_head, 0)


def backward_kernel(
    meta_ref, qkv_ref, move_ref, att_ref, home_prob_ref, move_prob_ref,
    near_ref, far_ref, last_ref, out_ref, ga_ref, key_acc, value_acc,
):
    home_first, home_len = meta_ref[0], meta_ref[1]
    half = ROWS // 2
    for i in range(4):
        first = pl.multiple_of(meta_ref[4 + i], half)
        ga_ref[pl.ds(first, ROWS), :] = near_ref[i * ROWS : (i + 1) * ROWS, :]
    for i in range(6):
        first = pl.multiple_of(meta_ref[8 + i], half)
        ga_ref[pl.ds(first, half), :] = far_ref[i * half : (i + 1) * half, :]
    ga_ref[pl.ds(pl.multiple_of(meta_ref[14], half), ROWS), :] = last_ref[...]

    def read_home(which, head, first, count):
        start = pl.multiple_of(home_first + first, 128)
        return qkv_ref[pl.ds(start, count), columns(which, head)]

    def read_move(which, head, first, count):
        return move_ref[pl.ds(first, count), columns(which, head)]

    out_ref[HOME:, :] = jnp.zeros((GROUP - HOME, 3 * FEAT), jnp.bfloat16)
    backward_clip(
        read_home, HOME, home_prob_ref, 0, ga_ref, att_ref, out_ref, key_acc, value_acc
    )
    backward_clip(
        read_move, MOVE, move_prob_ref, home_len, ga_ref, att_ref, out_ref, key_acc, value_acc
    )


def backward(meta, qkv, moved, att, home_prob, move_prob, near, far, last):
    return pl.pallas_call(
        backward_kernel,
        out_shape=jax.ShapeDtypeStruct((GROUP, 3 * FEAT), jnp.bfloat16),
        in_specs=[SMEM] + [VMEM] * 8,
        out_specs=VMEM,
        scratch_shapes=[
            pltpu.VMEM((GROUP, FEAT), jnp.bfloat16),
            pltpu.VMEM((HOME, HD), jnp.float32),
            pltpu.VMEM((HOME, HD), jnp.float32),
        ],
        compiler_params=PARAMS,
        cost_estimate=pl.CostEstimate(
            flops=10_000_000_000, bytes_accessed=12_000_000, transcendentals=0
        ),
        name="backward",
    )(meta, qkv, moved, att, home_prob, move_prob, near, far, last)


def pick(x, index):
    return lax.dynamic_index_in_dim(x, index, 0, keepdims=False)


def summed_over_groups(parts):
    group_id = lax.axis_index("dp")
    z, xh, core = group_id // 4, group_id // 2 % 2, group_id % 2
    got = lax.ppermute(pick(parts, 1 - core), "dp", [(i, i ^ 1) for i in range(16)])
    both = (pick(parts, core).astype(jnp.float32) + got.astype(jnp.float32)).astype(jnp.bfloat16)
    total = pick(both, z).astype(jnp.float32)
    for distance in (1, 2, 3):
        sent = pick(both, (z + distance) % 4)
        total = total + shifted(sent, "dp", 4 * distance).astype(jnp.float32)
    low, high = total[:, : D // 16], total[:, D // 16 :]
    sent = jnp.where(xh == 0, high, low).astype(jnp.bfloat16)
    got = lax.ppermute(sent, "dp", [(i, i ^ 2) for i in range(16)])
    return jnp.where(xh == 0, low, high) + got.astype(jnp.float32)


def arriving(distance, outgoing, qkv, meta):
    moved = shifted(outgoing, "dp", distance)
    home_att, home_prob = forward_home(meta, qkv)
    return moved, home_att, home_prob


def local(query_rows, key_rows, value_rows, out_grad, out_weight, clip_len, clip_group, clip_start):
    groups = lax.axis_size("dp")
    group_id = lax.axis_index("dp")
    me = lax.axis_index("head")
    rotate_by = jnp.mod(clip_group[1] - clip_group[0], groups)
    source_group = jnp.mod(group_id - rotate_by, groups)
    half, third = ROWS // 2, ROWS // 3

    up, down = ((me + 6) % 8) * ROWS, ((me + 2) % 8) * ROWS
    far_a = ((me + 4) % 8) * ROWS
    far_b, far_c = (((me + 2) % 8) ^ 1) * ROWS, (((me + 6) % 8) ^ 1) * ROWS
    far_d = (((me + 4) % 8) ^ 1) * ROWS
    meta = jnp.stack(
        [
            clip_start[2 * group_id],
            clip_len[2 * group_id],
            clip_len[2 * source_group + 1],
            jnp.int32(0),
            me * ROWS,
            (me ^ 1) * ROWS,
            up,
            down,
            far_a,
            far_c,
            far_a + half,
            far_b,
            far_b + half,
            far_c + half,
            far_d,
        ]
    ).astype(jnp.int32)

    dy_x = swapped(out_grad)
    dy_up = shifted(out_grad, "head", 2)
    dy_down = shifted(out_grad, "head", -2)

    packed = jnp.concatenate(
        [x.reshape(ROWS, 8, FEAT) for x in (query_rows, key_rows, value_rows)], axis=2
    )
    qkv = lax.all_to_all(packed, "head", split_axis=1, concat_axis=0, tiled=False)
    qkv = qkv.reshape(GROUP, 3 * FEAT)
    padded = jnp.concatenate([qkv, jnp.zeros((MOVE // 2, 3 * FEAT), jnp.bfloat16)], axis=0)
    outgoing = lax.dynamic_slice_in_dim(padded, clip_start[2 * group_id + 1], MOVE, 0)

    moved, home_att, home_prob = lax.switch(
        rotate_by - 1,
        [functools.partial(arriving, d) for d in range(1, groups // 2 + 1)],
        outgoing, qkv, meta,
    )

    moved, dy_x, dy_up, dy_down = lax.optimization_barrier((moved, dy_x, dy_up, dy_down))
    got_up = shifted(jnp.concatenate([dy_up[:half], dy_x[:half]]), "head", 2)
    got_down = shifted(jnp.concatenate([dy_down[half:], dy_x[:half]]), "head", -2)
    got_x = swapped(jnp.concatenate([dy_down[half:], dy_up[half:]]))
    att, move_prob = forward_move(meta, moved, home_att)
    near_blocks = [out_grad, dy_x, dy_up, dy_down]
    near = grad_att(out_weight, near_blocks)

    last_blocks = [
        shifted(got_up[half : half + third], "head", 2),
        swapped(jnp.concatenate([got_up[third:half], got_down[: 2 * third - half]])),
        shifted(got_x[half - third : half], "head", -2),
    ]
    far_blocks = [got_up, got_down, got_x]
    far = grad_att(out_weight, far_blocks)
    part = grad_weight_part(
        meta[4:14], att, near_blocks + far_blocks, (ROWS,) * 4 + (half,) * 6
    )
    last = grad_att(out_weight, last_blocks)
    grads = backward(meta, qkv, moved, att, home_prob, move_prob, near, far, last)
    parts = grad_weight_last(meta[14:], att, last_blocks, part)
    grad_weight = summed_over_groups(parts) * ((GROUP * groups) ** (-0.5))

    back = lax.all_to_all(
        grads.reshape(8, ROWS, 3 * FEAT), "head", split_axis=0, concat_axis=1, tiled=False
    )
    outs = [
        back[:, :, i * FEAT : (i + 1) * FEAT].reshape(ROWS, 8 * FEAT) for i in range(3)
    ]
    return (*outs, grad_weight)


def solution(mesh):
    rows = P(("dp", "head"), None)
    in_specs = (rows, rows, rows, rows, P("head", None), P(), P(), P())
    out_specs = (rows, rows, rows, P("head", "dp"))
    return jax.shard_map(local, mesh=mesh, in_specs=in_specs, out_specs=out_specs, check_vma=False)
```

profile of v0, /device:TPU:0, one launch (start us, length us, event | category | flops | bytes accessed | tf_op | source)
XLA Modules:
  0.0 193.0 jit_solution(7838955089719255051)
XLA Ops:
  5.6 5.6 %all-to-all-start = ((bf16[1,192,8,768]{3,1,0,2:T(8,128)(2,1)}), bf16[1,192,8,768]{3,1,0,2:T(8,128)(2,1)S(1)}, u32[]{:S(2)}, u32[]{:S(2)}) async-start(bf16[1,192,8,768]{3,1,0,2:T(8,128)(2,1)} %copy.21), calls=%async_computation | async-start | bytes 4718592 | tf_op jit(solution)/shard_map/all_to_all | solution.py:404
  11.2 2.0 %collective-permute-start.8 = (bf16[192,3072]{1,0:T(8,128)(2,1)}, bf16[192,3072]{1,0:T(8,128)(2,1)}, u32[]{:S(2)}, u32[]{:S(2)}) collective-permute-start(bf16[192,3072]{1,0:T(8,128)(2,1)} %refs_0_.3), channel_id=1, source_target_pairs={{0,1},{1,0},{2,3},{3,2},{4,5},{5,4},{6,7},{7,6},{8,9},{9,8},{10,11... | collective-permute-start | bytes 3538952 | tf_op jit(solution)/shard_map/ppermute | solution.py:44
  21.0 2.0 %stack.49.meta_ref = s32[15]{0:T(128)S(1)} concatenate(s32[1]{0:T(128)} %get-tuple-element.134, s32[1]{0:T(128)} %get-tuple-element.139, s32[1]{0:T(128)} %get-tuple-element.140, s32[1]{0:T(128)} %constant.129.clone.1, s32[1]{0:T(128)} %bitcast.1, s32[1]{0:T(128)} %bitcast.2, s32[1]{0:T(128)} %bitcast.3, s32[1]{0:T(128)} %bitcast.4, s32[1]{0:T(128)} %bitcast.5, s32[1]{0:T(128)} %bitcast.6, ...), dimensions={0} | concatenate | bytes 120 | tf_op jit(solution)/shard_map/stack | solution.py:377
  23.0 19.5 %all-to-all-done = bf16[1,192,8,768]{3,1,0,2:T(8,128)(2,1)S(1)} async-done(((bf16[1,192,8,768]{3,1,0,2:T(8,128)(2,1)}), bf16[1,192,8,768]{3,1,0,2:T(8,128)(2,1)S(1)}, u32[]{:S(2)}, u32[]{:S(2)}) %all-to-all-start) | async-done | bytes 2359328 | tf_op jit(solution)/shard_map/all_to_all | solution.py:404
  42.9 34.4 %conditional.1 = (bf16[512,768]{1,0:T(8,128)(2,1)}, bf16[1024,256]{1,0:T(8,128)(2,1)}, bf16[2,1024,1024]{2,1,0:T(8,128)(2,1)}) conditional(s32[]{:T(128)} %clamp.3, (bf16[512,768]{1,0:T(8,128)(2,1)S(1)}, s32[15]{0:T(128)S(1)}, bf16[1536,768]{1,0:T(8,128)(2,1)S(1)}) %tuple.67, (bf16[512,768]{1,0:T(8,128)(2,1)S(1)}, ...), branch_computations={%region_0.1_spmd, %region_1.2_spmd, %region_2.3_spmd, %region_3.4_... | conditional | flops 6000000000 | bytes 11145792 | solution.py:409
  43.0 10.9 %forward_home.12 = (bf16[1024,256]{1,0:T(8,128)(2,1)}, bf16[2,1024,1024]{2,1,0:T(8,128)(2,1)}) custom-call(s32[15]{0:T(128)S(1)} %get-tuple-element.69.meta_ref, bf16[1536,768]{1,0:T(8,128)(2,1)S(1)} %get-tuple-element.70.qkv_ref), custom_call_target="tpu_custom_call" | custom-call | flops 6000000000 | bytes 8000000 | tf_op jit(solution)/shard_map/cond/branch_4_fun/forward_home/pallas_call | solution.py:91
  53.9 23.4 %collective-permute-done.4 = bf16[512,768]{1,0:T(8,128)(2,1)} collective-permute-done((bf16[512,768]{1,0:T(8,128)(2,1)S(1)}, bf16[512,768]{1,0:T(8,128)(2,1)}, u32[]{:S(2)}, u32[]{:S(2)}) %collective-permute-start.4) | collective-permute-done | bytes 786464 | tf_op jit(solution)/shard_map/cond/branch_4_fun/ppermute | solution.py:40
  80.0 1.9 pad_maximum_fusion.2
  85.1 1.8 collective-permute-start.13
  87.6 5.6 %forward_move.1 = (bf16[1536,256]{1,0:T(8,128)(2,1)}, bf16[2,512,512]{2,1,0:T(8,128)(2,1)}) custom-call(s32[15]{0:T(128)S(1)} %stack.49.meta_ref, bf16[512,768]{1,0:T(8,128)(2,1)} %get-tuple-element.102.move_ref, bf16[1024,256]{1,0:T(8,128)(2,1)} %get-tuple-element.103.home_att_ref), custom_call_target="tpu_custom_call" | custom-call | flops 1500000000 | bytes 3000000 | tf_op jit(solution)/shard_map/forward_move/pallas_call | solution.py:119
  93.2 5.2 %grad_att.3.near_ref = bf16[768,256]{1,0:T(8,128)(2,1)} custom-call(bf16[256,3072]{1,0:T(8,128)(2,1)} %weight_ref.5, bf16[192,3072]{1,0:T(8,128)(2,1)} %refs_0_.3, bf16[192,3072]{1,0:T(8,128)(2,1)} %collective-permute-done.8.refs_1_, bf16[192,3072]{1,0:T(8,128)(2,1)} %copy-done.3, bf16[192,3072]{1,0:T(8,128)(2,1)} %collective-permute-done.10.refs_3_), custom_call_target="tpu_custom_call" | custom-call | flops 2304000000 | bytes 4992000 | tf_op jit(solution)/shard_map/grad_att/pallas_call | solution.py:156
  98.4 8.8 %collective-permute-done.11.refs_0_.refs_4_ = bf16[192,3072]{1,0:T(8,128)(2,1)} collective-permute-done((bf16[192,3072]{1,0:T(8,128)(2,1)}, bf16[192,3072]{1,0:T(8,128)(2,1)}, u32[]{:S(2)}, u32[]{:S(2)}) %collective-permute-start.11) | collective-permute-done | bytes 1179680 | tf_op jit(solution)/shard_map/ppermute | solution.py:40
  113.3 3.2 %collective-permute-start.16 = (bf16[64,3072]{1,0:T(8,128)(2,1)S(1)}, bf16[64,3072]{1,0:T(8,128)(2,1)S(1)}, u32[]{:S(2)}, u32[]{:S(2)}) collective-permute-start(bf16[64,3072]{1,0:T(8,128)(2,1)S(1)} %slice.67), channel_id=1, source_target_pairs={{2,0},{3,1},{4,2},{5,3},{6,4},{7,5},{0,6},{1,7},{10,8},{11,9},{12,... | collective-permute-start | bytes 1179656 | tf_op jit(solution)/shard_map/ppermute | solution.py:40
  116.4 4.7 %grad_att.4.far_ref = bf16[576,256]{1,0:T(8,128)(2,1)} custom-call(bf16[256,3072]{1,0:T(8,128)(2,1)} %weight_ref.5, bf16[192,3072]{1,0:T(8,128)(2,1)} %collective-permute-done.11.refs_0_.refs_4_, bf16[192,3072]{1,0:T(8,128)(2,1)} %collective-permute-done.12.refs_1_.refs_5_, bf16[192,3072]{1,0:T(8,128)(2,1)} %collective-permute-done.13.refs_2_.refs_6_), custom_call_target="tpu_custom_call" | custom-call | flops 1728000000 | bytes 3744000 | tf_op jit(solution)/shard_map/grad_att/pallas_call | solution.py:156
  121.2 7.7 %grad_weight.1.refs_3_ = f32[4,256,768]{2,1,0:T(8,128)} custom-call(s32[10]{0:T(128)} %stack.50.first_ref, bf16[1536,256]{1,0:T(8,128)(2,1)} %get-tuple-element.104.att_ref, bf16[192,3072]{1,0:T(8,128)(2,1)} %refs_0_.3, bf16[192,3072]{1,0:T(8,128)(2,1)} %collective-permute-done.8.refs_1_, bf16[192,3072]{1,0:T(8,128)(2,1)} %copy-done.3, ...), custom_call_target="tpu_custom_call" | custom-call | flops 3360000000 | bytes 10752000 | tf_op jit(solution)/shard_map/grad_weight/pallas_call | solution.py:198
  130.5 5.2 %grad_weight_last.1 = bf16[2,4,256,384]{3,2,1,0:T(8,128)(2,1)} custom-call(s32[1]{0:T(128)} %bitcast.11.first_ref, bf16[1536,256]{1,0:T(8,128)(2,1)} %get-tuple-element.104.att_ref, bf16[64,3072]{1,0:T(8,128)(2,1)} %copy-done, bf16[64,3072]{1,0:T(8,128)(2,1)} %copy-done.1, bf16[64,3072]{1,0:T(8,128)(2,1)} %copy-done.2, f32[4,256,768]{2,1,0:T(8,128)} %grad_weight.1.refs_3_), custom_call_target="tpu_custom_call" | custom-call | flops 600000000 | bytes 6000000 | tf_op jit(solution)/shard_map/grad_weight_last/pallas_call | solution.py:238
  137.2 3.9 %grad_att.5.last_ref = bf16[192,256]{1,0:T(8,128)(2,1)} custom-call(bf16[256,3072]{1,0:T(8,128)(2,1)} %weight_ref.5, bf16[64,3072]{1,0:T(8,128)(2,1)} %copy-done, bf16[64,3072]{1,0:T(8,128)(2,1)} %copy-done.1, bf16[64,3072]{1,0:T(8,128)(2,1)} %copy-done.2), custom_call_target="tpu_custom_call" | custom-call | flops 576000000 | bytes 1248000 | tf_op jit(solution)/shard_map/grad_att/pallas_call | solution.py:156
  141.0 12.2 %backward.1 = bf16[1536,768]{1,0:T(8,128)(2,1)} custom-call(s32[15]{0:T(128)S(1)} %stack.49.meta_ref, bf16[1536,768]{1,0:T(8,128)(2,1)S(1)} %bitcast.66, bf16[512,768]{1,0:T(8,128)(2,1)} %get-tuple-element.102.move_ref, bf16[1536,256]{1,0:T(8,128)(2,1)} %get-tuple-element.104.att_ref, bf16[2,1024,1024]{2,1,0:T(8,128)(2,1)S(1)} %copy-done.8, ...), custom_call_target="tpu_custom_call" | custom-call | flops 10000000000 | bytes 12000000 | tf_op jit(solution)/shard_map/backward/pallas_call | solution.py:322
  153.3 3.6 %all-to-all-start.1 = ((bf16[8,192,1,768]{3,1,2,0:T(8,128)(2,1)}), bf16[8,192,1,768]{3,1,2,0:T(8,128)(2,1)S(1)}, u32[]{:S(2)}, u32[]{:S(2)}) async-start(bf16[8,192,1,768]{3,1,2,0:T(8,128)(2,1)} %bitcast.71), calls=%async_computation.1 | async-start | bytes 4718592 | tf_op jit(solution)/shard_map/all_to_all | solution.py:438
  159.3 2.3 %collective-permute-start.20 = (bf16[256,384]{1,0:T(8,128)(2,1)}, bf16[256,384]{1,0:T(8,128)(2,1)}, u32[]{:S(2)}, u32[]{:S(2)}) collective-permute-start(bf16[256,384]{1,0:T(8,128)(2,1)} %get-tuple-element.128), channel_id=1, source_target_pairs={{32,0},{40,8},{48,16},{56,24},{64,32},{72,40},{80,48},{88,56},{96,... | collective-permute-start | bytes 589832 | tf_op jit(solution)/shard_map/ppermute | solution.py:40
  162.9 8.1 %collective-permute-done.20 = bf16[256,384]{1,0:T(8,128)(2,1)} collective-permute-done((bf16[256,384]{1,0:T(8,128)(2,1)}, bf16[256,384]{1,0:T(8,128)(2,1)}, u32[]{:S(2)}, u32[]{:S(2)}) %collective-permute-start.20) | collective-permute-done | bytes 196640 | tf_op jit(solution)/shard_map/ppermute | solution.py:40
  171.0 3.4 %collective-permute-done.18 = bf16[256,384]{1,0:T(8,128)(2,1)} collective-permute-done((bf16[256,384]{1,0:T(8,128)(2,1)S(1)}, bf16[256,384]{1,0:T(8,128)(2,1)}, u32[]{:S(2)}, u32[]{:S(2)}) %collective-permute-start.18) | collective-permute-done | bytes 196640 | tf_op jit(solution)/shard_map/ppermute | solution.py:40
  175.7 2.5 %collective-permute-start.21 = (bf16[256,192]{1,0:T(8,128)(2,1)S(1)}, bf16[256,192]{1,0:T(8,128)(2,1)S(1)}, u32[]{:S(2)}, u32[]{:S(2)}) collective-permute-start(bf16[256,192]{1,0:T(8,128)(2,1)S(1)} %select_convert_fusion), channel_id=1, source_target_pairs={{0,16},{8,24},{16,0},{24,8},{32,48},{40,56},{48,32},{56,40},{64,80... | collective-permute-start | bytes 294920 | tf_op jit(solution)/shard_map/ppermute | solution.py:355
  178.2 10.6 %collective-permute-done.21 = bf16[256,192]{1,0:T(8,128)(2,1)S(1)} collective-permute-done((bf16[256,192]{1,0:T(8,128)(2,1)S(1)}, bf16[256,192]{1,0:T(8,128)(2,1)S(1)}, u32[]{:S(2)}, u32[]{:S(2)}) %collective-permute-start.21) | collective-permute-done | bytes 98336 | tf_op jit(solution)/shard_map/ppermute | solution.py:355
  (67 shorter events, 34.5 us)
Async XLA Ops:
  0.6 2.8 %copy-start.4 = (bf16[192,2048]{1,0:T(8,128)(2,1)S(1)}, bf16[192,2048]{1,0:T(8,128)(2,1)}, u32[]{:S(2)}) copy-start(bf16[192,2048]{1,0:T(8,128)(2,1)} %param.16) | copy-start | bytes 2359300
  5.6 10.9 %copy-start.5 = (s32[32]{0:T(128)S(1)}, s32[32]{0:T(128)}, u32[]{:S(2)}) copy-start(s32[32]{0:T(128)} %param.22) | copy-start | bytes 388
  5.6 12.8 %copy-start.6 = (s32[32]{0:T(128)S(1)}, s32[32]{0:T(128)}, u32[]{:S(2)}) copy-start(s32[32]{0:T(128)} %param.23) | copy-start | bytes 388
  5.6 12.9 %copy-start.7 = (s32[32]{0:T(128)S(1)}, s32[32]{0:T(128)}, u32[]{:S(2)}) copy-start(s32[32]{0:T(128)} %param.21) | copy-start | bytes 388
  5.6 37.0 %all-to-all-start = ((bf16[1,192,8,768]{3,1,0,2:T(8,128)(2,1)}), bf16[1,192,8,768]{3,1,0,2:T(8,128)(2,1)S(1)}, u32[]{:S(2)}, u32[]{:S(2)}) async-start(bf16[1,192,8,768]{3,1,0,2:T(8,128)(2,1)} %copy.21), calls=%async_computation | async-start | bytes 4718592 | tf_op jit(solution)/shard_map/all_to_all | solution.py:404
  11.2 66.1 %collective-permute-start.8 = (bf16[192,3072]{1,0:T(8,128)(2,1)}, bf16[192,3072]{1,0:T(8,128)(2,1)}, u32[]{:S(2)}, u32[]{:S(2)}) collective-permute-start(bf16[192,3072]{1,0:T(8,128)(2,1)} %refs_0_.3), channel_id=1, source_target_pairs={{0,1},{1,0},{2,3},{3,2},{4,5},{5,4},{6,7},{7,6},{8,9},{9,8},{10,11... | collective-permute-start | bytes 3538952 | tf_op jit(solution)/shard_map/ppermute | solution.py:44
  13.2 64.1 %collective-permute-start.9 = (bf16[192,3072]{1,0:T(8,128)(2,1)}, bf16[192,3072]{1,0:T(8,128)(2,1)S(1)}, u32[]{:S(2)}, u32[]{:S(2)}) collective-permute-start(bf16[192,3072]{1,0:T(8,128)(2,1)} %refs_0_.3), channel_id=1, source_target_pairs={{6,0},{7,1},{0,2},{1,3},{2,4},{3,5},{4,6},{5,7},{14,8},{15,9},{8,1... | collective-permute-start | bytes 3538952 | tf_op jit(solution)/shard_map/ppermute | solution.py:40
  14.7 62.6 %collective-permute-start.10 = (bf16[192,3072]{1,0:T(8,128)(2,1)}, bf16[192,3072]{1,0:T(8,128)(2,1)}, u32[]{:S(2)}, u32[]{:S(2)}) collective-permute-start(bf16[192,3072]{1,0:T(8,128)(2,1)} %refs_0_.3), channel_id=1, source_target_pairs={{2,0},{3,1},{4,2},{5,3},{6,4},{7,5},{0,6},{1,7},{10,8},{11,9},{12,... | collective-permute-start | bytes 3538952 | tf_op jit(solution)/shard_map/ppermute | solution.py:40
  42.9 34.4 %collective-permute-start.4 = (bf16[512,768]{1,0:T(8,128)(2,1)S(1)}, bf16[512,768]{1,0:T(8,128)(2,1)}, u32[]{:S(2)}, u32[]{:S(2)}) collective-permute-start(bf16[512,768]{1,0:T(8,128)(2,1)S(1)} %get-tuple-element.68), channel_id=1, source_target_pairs={{88,0},{96,8},{104,16},{112,24},{120,32},{0,40},{8,48},{16,56},{24... | collective-permute-start | bytes 2359304 | tf_op jit(solution)/shard_map/cond/branch_4_fun/ppermute | solution.py:40
  77.3 2.7 %copy-start.3 = (bf16[192,3072]{1,0:T(8,128)(2,1)}, bf16[192,3072]{1,0:T(8,128)(2,1)S(1)}, u32[]{:S(2)}) copy-start(bf16[192,3072]{1,0:T(8,128)(2,1)S(1)} %collective-permute-done.9.refs_2_) | copy-start | bytes 3538948
  81.9 25.2 %collective-permute-start.11 = (bf16[192,3072]{1,0:T(8,128)(2,1)}, bf16[192,3072]{1,0:T(8,128)(2,1)}, u32[]{:S(2)}, u32[]{:S(2)}) collective-permute-start(bf16[192,3072]{1,0:T(8,128)(2,1)} %get-tuple-element.132), channel_id=1, source_target_pairs={{6,0},{7,1},{0,2},{1,3},{2,4},{3,5},{4,6},{5,7},{14,8},{15,9},{8,1... | collective-permute-start | bytes 3538952 | tf_op jit(solution)/shard_map/ppermute | solution.py:40
  83.4 27.3 %collective-permute-start.12 = (bf16[192,3072]{1,0:T(8,128)(2,1)}, bf16[192,3072]{1,0:T(8,128)(2,1)}, u32[]{:S(2)}, u32[]{:S(2)}) collective-permute-start(bf16[192,3072]{1,0:T(8,128)(2,1)} %get-tuple-element.131), channel_id=1, source_target_pairs={{2,0},{3,1},{4,2},{5,3},{6,4},{7,5},{0,6},{1,7},{10,8},{11,9},{12,... | collective-permute-start | bytes 3538952 | tf_op jit(solution)/shard_map/ppermute | solution.py:40
  85.1 27.1 %collective-permute-start.13 = (bf16[192,3072]{1,0:T(8,128)(2,1)S(1)}, bf16[192,3072]{1,0:T(8,128)(2,1)}, u32[]{:S(2)}, u32[]{:S(2)}) collective-permute-start(bf16[192,3072]{1,0:T(8,128)(2,1)S(1)} %get-tuple-element.130), channel_id=1, source_target_pairs={{0,1},{1,0},{2,3},{3,2},{4,5},{5,4},{6,7},{7,6},{8,9},{9,8},{10,11... | collective-permute-start | bytes 3538952 | tf_op jit(solution)/shard_map/ppermute | solution.py:44
  108.2 20.7 %collective-permute-start.14 = (bf16[64,3072]{1,0:T(8,128)(2,1)S(1)}, bf16[64,3072]{1,0:T(8,128)(2,1)S(1)}, u32[]{:S(2)}, u32[]{:S(2)}) collective-permute-start(bf16[64,3072]{1,0:T(8,128)(2,1)S(1)} %slice.64), channel_id=1, source_target_pairs={{6,0},{7,1},{0,2},{1,3},{2,4},{3,5},{4,6},{5,7},{14,8},{15,9},{8,1... | collective-permute-start | bytes 1179656 | tf_op jit(solution)/shard_map/ppermute | solution.py:40
  111.7 17.2 %collective-permute-start.15 = (bf16[64,3072]{1,0:T(8,128)(2,1)S(1)}, bf16[64,3072]{1,0:T(8,128)(2,1)S(1)}, u32[]{:S(2)}, u32[]{:S(2)}) collective-permute-start(bf16[64,3072]{1,0:T(8,128)(2,1)S(1)} %pad_maximum_fusion.3), channel_id=1, source_target_pairs={{0,1},{1,0},{2,3},{3,2},{4,5},{5,4},{6,7},{7,6},{8,9},{9,8},{10,11... | collective-permute-start | bytes 1179656 | tf_op jit(solution)/shard_map/ppermute | solution.py:44
  113.3 15.6 %collective-permute-start.16 = (bf16[64,3072]{1,0:T(8,128)(2,1)S(1)}, bf16[64,3072]{1,0:T(8,128)(2,1)S(1)}, u32[]{:S(2)}, u32[]{:S(2)}) collective-permute-start(bf16[64,3072]{1,0:T(8,128)(2,1)S(1)} %slice.67), channel_id=1, source_target_pairs={{2,0},{3,1},{4,2},{5,3},{6,4},{7,5},{0,6},{1,7},{10,8},{11,9},{12,... | collective-permute-start | bytes 1179656 | tf_op jit(solution)/shard_map/ppermute | solution.py:40
  128.9 0.9 copy-start.1
  135.7 5.3 %copy-start.8 = (bf16[2,1024,1024]{2,1,0:T(8,128)(2,1)S(1)}, bf16[2,1024,1024]{2,1,0:T(8,128)(2,1)}, u32[]{:S(2)}) copy-start(bf16[2,1024,1024]{2,1,0:T(8,128)(2,1)} %get-tuple-element.105.home_prob_ref) | copy-start | bytes 12582916
  137.1 19.9 %collective-permute-start.17 = (bf16[4,256,384]{2,1,0:T(8,128)(2,1)S(1)}, bf16[4,256,384]{2,1,0:T(8,128)(2,1)}, u32[]{:S(2)}, u32[]{:S(2)}) collective-permute-start(bf16[4,256,384]{2,1,0:T(8,128)(2,1)S(1)} %dynamic-slice_bitcast_fusion), channel_id=1, source_target_pairs={{0,8},{8,0},{16,24},{24,16},{32,40},{40,32},{48,56},{56,48},{64,72... | collective-permute-start | bytes 2359304 | tf_op jit(solution)/shard_map/ppermute | solution.py:347
  153.3 36.6 %all-to-all-start.1 = ((bf16[8,192,1,768]{3,1,2,0:T(8,128)(2,1)}), bf16[8,192,1,768]{3,1,2,0:T(8,128)(2,1)S(1)}, u32[]{:S(2)}, u32[]{:S(2)}) async-start(bf16[8,192,1,768]{3,1,2,0:T(8,128)(2,1)} %bitcast.71), calls=%async_computation.1 | async-start | bytes 4718592 | tf_op jit(solution)/shard_map/all_to_all | solution.py:438
  159.3 11.7 %collective-permute-start.20 = (bf16[256,384]{1,0:T(8,128)(2,1)}, bf16[256,384]{1,0:T(8,128)(2,1)}, u32[]{:S(2)}, u32[]{:S(2)}) collective-permute-start(bf16[256,384]{1,0:T(8,128)(2,1)} %get-tuple-element.128), channel_id=1, source_target_pairs={{32,0},{40,8},{48,16},{56,24},{64,32},{72,40},{80,48},{88,56},{96,... | collective-permute-start | bytes 589832 | tf_op jit(solution)/shard_map/ppermute | solution.py:40
  161.6 9.4 %collective-permute-start.19 = (bf16[256,384]{1,0:T(8,128)(2,1)S(1)}, bf16[256,384]{1,0:T(8,128)(2,1)}, u32[]{:S(2)}, u32[]{:S(2)}) collective-permute-start(bf16[256,384]{1,0:T(8,128)(2,1)S(1)} %get-tuple-element.129), channel_id=1, source_target_pairs={{64,0},{72,8},{80,16},{88,24},{96,32},{104,40},{112,48},{120,56},{... | collective-permute-start | bytes 589832 | tf_op jit(solution)/shard_map/ppermute | solution.py:40
  162.4 12.0 %collective-permute-start.18 = (bf16[256,384]{1,0:T(8,128)(2,1)S(1)}, bf16[256,384]{1,0:T(8,128)(2,1)}, u32[]{:S(2)}, u32[]{:S(2)}) collective-permute-start(bf16[256,384]{1,0:T(8,128)(2,1)S(1)} %get-tuple-element.127), channel_id=1, source_target_pairs={{96,0},{104,8},{112,16},{120,24},{0,32},{8,40},{16,48},{24,56},{32... | collective-permute-start | bytes 589832 | tf_op jit(solution)/shard_map/ppermute | solution.py:40
  175.7 13.1 %collective-permute-start.21 = (bf16[256,192]{1,0:T(8,128)(2,1)S(1)}, bf16[256,192]{1,0:T(8,128)(2,1)S(1)}, u32[]{:S(2)}, u32[]{:S(2)}) collective-permute-start(bf16[256,192]{1,0:T(8,128)(2,1)S(1)} %select_convert_fusion), channel_id=1, source_target_pairs={{0,16},{8,24},{16,0},{24,8},{32,48},{40,56},{48,32},{56,40},{64,80... | collective-permute-start | bytes 294920 | tf_op jit(solution)/shard_map/ppermute | solution.py:355
  (2 other events, 1.5 us)
where the time goes:
time: 194 us; the launch traced here: 193 us
  waiting for transfers between devices  73.9 us (38%)
  Pallas kernels  55.4 us (29%)
  starting transfers between devices  31.1 us (16%)
  local copies, waits for them, and re-layouts  23.2 us (12%)
  other arithmetic  5.05 us (3%)
  between operations  4.29 us (2%)
    ppermute x10, waiting for transfers between devices, shifted(): return lax.ppermute(x, axis, [((i - distance) % n, i) for i in range(n)])  43.7 us
    all_to_all x1, waiting for transfers between devices, local(): lax.all_to_all(packed, 'head', split_axis=1, concat_axis=0, tiled=False)  19.5 us
    ppermute x10, starting transfers between devices, shifted(): return lax.ppermute(x, axis, [((i - distance) % n, i) for i in range(n)])  14.8 us
    pallas_call x3, Pallas kernels, grad_att(): pl.pallas_call(functools.partial(grad_att_kernel, count), grid=(4,), out_...  13.8 us
    pallas_call x1, Pallas kernels, backward(): pl.pallas_call(backward_kernel, out_shape=jax.ShapeDtypeStruct((GROUP, 3...  12.2 us
    pallas_call x1, Pallas kernels, forward_home(): pl.pallas_call(forward_home_kernel, out_shape=(jax.ShapeDtypeStruct((HOME...  10.9 us
    ppermute x1, waiting for transfers between devices, summed_over_groups(): got = lax.ppermute(sent, 'dp', [(i, i ^ 2) for i in range(16)])  10.6 us
    pallas_call x1, Pallas kernels, grad_weight_part(): pl.pallas_call(functools.partial(grad_weight_kernel, pieces), grid=(4,),...  7.66 us
  transfers between devices with their start and end apart: 17, of which 6 were waited for; matrix products, arithmetic and copies ran while one was open for 7% of the time, Pallas kernels for 26%

commit v1 on v0

--- a/solution.py
+++ b/solution.py
@@ -24,7 +24,7 @@
 NT = (((1,), (1,)), ((), ()))
 VMEM = pl.BlockSpec(memory_space=pltpu.VMEM)
 SMEM = pl.BlockSpec(memory_space=pltpu.SMEM)
-PARAMS = pltpu.CompilerParams(vmem_limit_bytes=56 * 1024 * 1024)
+PARAMS = pltpu.CompilerParams(vmem_limit_bytes=32 * 1024 * 1024)
 
 
 def dot(a, b, dims=NN):
@@ -33,6 +33,23 @@
 
 def flip(x):
     return x.astype(jnp.float32).T.astype(x.dtype)
+
+
+def apart_kernel(packed_ref, *outs):
+    for i, out in enumerate(outs):
+        out[...] = packed_ref[0, :, i * FEAT : (i + 1) * FEAT]
+
+
+def apart(packed):
+    return pl.pallas_call(
+        apart_kernel,
+        grid=(8,),
+        out_shape=(jax.ShapeDtypeStruct((ROWS, 8 * FEAT), jnp.bfloat16),) * 3,
+        in_specs=[pl.BlockSpec((1, ROWS, 3 * FEAT), lambda i: (i, 0, 0))],
+        out_specs=(pl.BlockSpec((ROWS, FEAT), lambda i: (0, i)),) * 3,
+        compiler_params=PARAMS,
+        name="apart",
+    )(packed)
 
 
 def shifted(x, axis, distance):
@@ -126,7 +143,7 @@
         out_specs=(VMEM, VMEM),
         compiler_params=PARAMS,
         cost_estimate=pl.CostEstimate(
-            flops=1_500_000_000, bytes_accessed=3_000_000, transcendentals=500_000
+            flops=150_000_000, bytes_accessed=300_000, transcendentals=50_000
         ),
         name="forward_move",
     )(meta, moved, home_att)
@@ -165,7 +182,7 @@
         scratch_shapes=[pltpu.VMEM((total, FEAT), jnp.float32)],
         compiler_params=PARAMS,
         cost_estimate=pl.CostEstimate(
-            flops=total * 3_000_000, bytes_accessed=total * 6_500, transcendentals=0
+            flops=total * 300_000, bytes_accessed=total * 650, transcendentals=0
         ),
         name="grad_att",
     )(weight, *blocks)
@@ -208,51 +225,10 @@
         scratch_shapes=[pltpu.VMEM((FEAT, total), jnp.bfloat16)],
         compiler_params=PARAMS,
         cost_estimate=pl.CostEstimate(
-            flops=total * 2_500_000, bytes_accessed=total * 8_000, transcendentals=0
+            flops=total * 250_000, bytes_accessed=total * 800, transcendentals=0
         ),
         name="grad_weight",
     )(firsts, att, *blocks)
-
-
-def grad_weight_last_kernel(first_ref, att_ref, *refs):
-    blocks = refs[:3]
-    sum_ref, out_ref, att_t = refs[3:]
-
-    @pl.when(pl.program_id(0) == 0)
-    def _():
-        att_t[...] = place_rows(att_ref, first_ref, (ROWS,))
-
-    dy = jnp.concatenate([block[...] for block in blocks], axis=0)
-    part = sum_ref[0] + dot(att_t[...], dy)
-    cut = D // 16
-    for xh in range(2):
-        for core in range(2):
-            at = (2 * xh + core) * cut
-            out_ref[core, 0, :, xh * cut : (xh + 1) * cut] = part[:, at : at + cut].astype(
-                jnp.bfloat16
-            )
-
-
-def grad_weight_last(firsts, att, blocks, running):
-    wide = D // 4
-    return pl.pallas_call(
-        grad_weight_last_kernel,
-        grid=(4,),
-        out_shape=jax.ShapeDtypeStruct((2, 4, FEAT, wide // 2), jnp.bfloat16),
-        in_specs=[
-            SMEM,
-            pl.BlockSpec((GROUP, FEAT), lambda j: (0, 0)),
-            *[pl.BlockSpec((block.shape[0], wide), lambda j: (0, j)) for block in blocks],
-            pl.BlockSpec((1, FEAT, wide), lambda j: (j, 0, 0)),
-        ],
-        out_specs=pl.BlockSpec((2, 1, FEAT, wide // 2), lambda j: (0, j, 0, 0)),
-        scratch_shapes=[pltpu.VMEM((FEAT, ROWS), jnp.bfloat16)],
-        compiler_params=PARAMS,
-        cost_estimate=pl.CostEstimate(
-            flops=600_000_000, bytes_accessed=6_000_000, transcendentals=0
-        ),
-        name="grad_weight_last",
-    )(firsts, att, *blocks, running)
 
 
 def backward_clip(read, rows, prob_ref, row_first, ga_ref, att_ref, out_ref, key_acc, value_acc):
@@ -290,7 +266,8 @@
 
 def backward_kernel(
     meta_ref, qkv_ref, move_ref, att_ref, home_prob_ref, move_prob_ref,
-    near_ref, far_ref, last_ref, out_ref, ga_ref, key_acc, value_acc,
+    near_ref, far_ref, weight_ref, last_a, last_b, last_c, sum_ref,
+    out_ref, send_ref, keep_ref, ga_ref, key_acc, value_acc,
 ):
     home_first, home_len = meta_ref[0], meta_ref[1]
     half = ROWS // 2
@@ -300,7 +277,25 @@
     for i in range(6):
         first = pl.multiple_of(meta_ref[8 + i], half)
         ga_ref[pl.ds(first, half), :] = far_ref[i * half : (i + 1) * half, :]
-    ga_ref[pl.ds(pl.multiple_of(meta_ref[14], half), ROWS), :] = last_ref[...]
+    dy = jnp.concatenate([last_a[...], last_b[...], last_c[...]], axis=0)
+    last = dot(dy, weight_ref[...], NT).astype(jnp.bfloat16)
+    last_rows = pl.ds(pl.multiple_of(meta_ref[14], half), ROWS)
+    ga_ref[last_rows, :] = last
+
+    att_t = flip(att_ref[last_rows, :])
+    wide, cut = D // 4, D // 16
+    for z in range(4):
+        whole = sum_ref[z] + dot(att_t, dy[:, z * wide : (z + 1) * wide])
+        by_core = [
+            jnp.concatenate(
+                [whole[:, (2 * xh + core) * cut : (2 * xh + core + 1) * cut] for xh in range(2)],
+                axis=1,
+            ).astype(jnp.bfloat16)
+            for core in range(2)
+        ]
+        first_core = meta_ref[15] == 0
+        keep_ref[z] = jnp.where(first_core, by_core[0], by_core[1])
+        send_ref[z] = jnp.where(first_core, by_core[1], by_core[0])
 
     def read_home(which, head, first, count):
         start = pl.multiple_of(home_first + first, 128)
@@ -318,12 +313,16 @@
     )
 
 
-def backward(meta, qkv, moved, att, home_prob, move_prob, near, far, last):
+def backward(meta, qkv, moved, att, home_prob, move_prob, near, far, weight, last_blocks, part):
     return pl.pallas_call(
         backward_kernel,
-        out_shape=jax.ShapeDtypeStruct((GROUP, 3 * FEAT), jnp.bfloat16),
-        in_specs=[SMEM] + [VMEM] * 8,
-        out_specs=VMEM,
+        out_shape=(
+            jax.ShapeDtypeStruct((GROUP, 3 * FEAT), jnp.bfloat16),
+            jax.ShapeDtypeStruct((4, FEAT, D // 8), jnp.bfloat16),
+            jax.ShapeDtypeStruct((4, FEAT, D // 8), jnp.bfloat16),
+        ),
+        in_specs=[SMEM] + [VMEM] * 12,
+        out_specs=(VMEM, VMEM, VMEM),
         scratch_shapes=[
             pltpu.VMEM((GROUP, FEAT), jnp.bfloat16),
             pltpu.VMEM((HOME, HD), jnp.float32),
@@ -334,18 +333,18 @@
             flops=10_000_000_000, bytes_accessed=12_000_000, transcendentals=0
         ),
         name="backward",
-    )(meta, qkv, moved, att, home_prob, move_prob, near, far, last)
+    )(meta, qkv, moved, att, home_prob, move_prob, near, far, weight, *last_blocks, part)
 
 
 def pick(x, index):
     return lax.dynamic_index_in_dim(x, index, 0, keepdims=False)
 
 
-def summed_over_groups(parts):
+def summed_over_groups(send, keep):
     group_id = lax.axis_index("dp")
-    z, xh, core = group_id // 4, group_id // 2 % 2, group_id % 2
-    got = lax.ppermute(pick(parts, 1 - core), "dp", [(i, i ^ 1) for i in range(16)])
-    both = (pick(parts, core).astype(jnp.float32) + got.astype(jnp.float32)).astype(jnp.bfloat16)
+    z, xh = group_id // 4, group_id // 2 % 2
+    got = lax.ppermute(send, "dp", [(i, i ^ 1) for i in range(16)])
+    both = (keep.astype(jnp.float32) + got.astype(jnp.float32)).astype(jnp.bfloat16)
     total = pick(both, z).astype(jnp.float32)
     for distance in (1, 2, 3):
         sent = pick(both, (z + distance) % 4)
@@ -356,10 +355,11 @@
     return jnp.where(xh == 0, low, high) + got.astype(jnp.float32)
 
 
-def arriving(distance, outgoing, qkv, meta):
+def arriving(distance, outgoing, qkv, meta, weight, *blocks):
     moved = shifted(outgoing, "dp", distance)
     home_att, home_prob = forward_home(meta, qkv)
-    return moved, home_att, home_prob
+    near = grad_att(weight, blocks)
+    return moved, home_att, home_prob, near
 
 
 def local(query_rows, key_rows, value_rows, out_grad, out_weight, clip_len, clip_group, clip_start):
@@ -391,6 +391,7 @@
             far_b + half,
             far_c + half,
             far_d,
+            group_id % 2,
         ]
     ).astype(jnp.int32)
 
@@ -406,41 +407,38 @@
     padded = jnp.concatenate([qkv, jnp.zeros((MOVE // 2, 3 * FEAT), jnp.bfloat16)], axis=0)
     outgoing = lax.dynamic_slice_in_dim(padded, clip_start[2 * group_id + 1], MOVE, 0)
 
-    moved, home_att, home_prob = lax.switch(
-        rotate_by - 1,
-        [functools.partial(arriving, d) for d in range(1, groups // 2 + 1)],
-        outgoing, qkv, meta,
-    )
-
-    moved, dy_x, dy_up, dy_down = lax.optimization_barrier((moved, dy_x, dy_up, dy_down))
     got_up = shifted(jnp.concatenate([dy_up[:half], dy_x[:half]]), "head", 2)
     got_down = shifted(jnp.concatenate([dy_down[half:], dy_x[:half]]), "head", -2)
     got_x = swapped(jnp.concatenate([dy_down[half:], dy_up[half:]]))
-    att, move_prob = forward_move(meta, moved, home_att)
+
     near_blocks = [out_grad, dy_x, dy_up, dy_down]
-    near = grad_att(out_weight, near_blocks)
-
+    moved, home_att, home_prob, near = lax.switch(
+        rotate_by - 1,
+        [functools.partial(arriving, d) for d in range(1, groups // 2 + 1)],
+        outgoing, qkv, meta, out_weight, *near_blocks,
+    )
+
+    moved, got_up, got_down, got_x = lax.optimization_barrier((moved, got_up, got_down, got_x))
     last_blocks = [
         shifted(got_up[half : half + third], "head", 2),
         swapped(jnp.concatenate([got_up[third:half], got_down[: 2 * third - half]])),
         shifted(got_x[half - third : half], "head", -2),
     ]
     far_blocks = [got_up, got_down, got_x]
+    att, move_prob = forward_move(meta, moved, home_att)
     far = grad_att(out_weight, far_blocks)
     part = grad_weight_part(
         meta[4:14], att, near_blocks + far_blocks, (ROWS,) * 4 + (half,) * 6
     )
-    last = grad_att(out_weight, last_blocks)
-    grads = backward(meta, qkv, moved, att, home_prob, move_prob, near, far, last)
-    parts = grad_weight_last(meta[14:], att, last_blocks, part)
-    grad_weight = summed_over_groups(parts) * ((GROUP * groups) ** (-0.5))
-
-    back = lax.all_to_all(
-        grads.reshape(8, ROWS, 3 * FEAT), "head", split_axis=0, concat_axis=1, tiled=False
-    )
-    outs = [
-        back[:, :, i * FEAT : (i + 1) * FEAT].reshape(ROWS, 8 * FEAT) for i in range(3)
-    ]
+    grads, send, keep = backward(
+        meta, qkv, moved, att, home_prob, move_prob, near, far, out_weight, last_blocks, part
+    )
+    grad_weight = summed_over_groups(send, keep) * ((GROUP * groups) ** (-0.5))
+    outs = apart(
+        lax.all_to_all(
+            grads.reshape(8, ROWS, 3 * FEAT), "head", split_axis=0, concat_axis=0, tiled=True
+        )
+    )
     return (*outs, grad_weight)
 
 

time: 194 us -> 167 us (0.86)
  waiting for transfers between devices: 73.9 us -> 61.1 us
  Pallas kernels: 55.4 us -> 44.8 us
  local copies, waits for them, and re-layouts: 23.2 us -> 15 us
  starting transfers between devices: 31.1 us -> 33.6 us
    ppermute x10, waiting for transfers between devices: 43.7 us -> 23 us  [shifted(): return lax.ppermute(x, axis, [((i - distance) % n, i) for i in range(n)])]
    ppermute x3, waiting for transfers between devices: 0.01 us -> 15.1 us  [swapped(): return lax.ppermute(x, 'head', [(i, i ^ 1) for i in range(8)])]
    all_to_all x1, waiting for transfers between devices: 19.5 us -> 9.28 us  [local(): lax.all_to_all(packed, 'head', split_axis=1, concat_axis=0, tiled=False)]
    pallas_call x3 -> x2, Pallas kernels: 13.8 us -> 7.74 us  [grad_att(): pl.pallas_call(functools.partial(grad_att_kernel, count), grid=(4,), out_...]
    ppermute x1, starting transfers between devices: 0.09 us -> 5.44 us  [summed_over_groups(): got = lax.ppermute(send, 'dp', [(i, i ^ 1) for i in range(16)])]
    pallas_call x1, Pallas kernels: 7.66 us -> 4.49 us  [grad_weight_part(): pl.pallas_call(functools.partial(grad_weight_kernel, pieces), grid=(4,),...]
    reshape x3 -> x0, local copies, waits for them, and re-layouts: 2.91 us -> none  [local(): back[:, :, i * FEAT:(i + 1) * FEAT].reshape(ROWS, 8 * FEAT)]
    ppermute x3, starting transfers between devices: 4.45 us -> 7.21 us  [swapped(): return lax.ppermute(x, 'head', [(i, i ^ 1) for i in range(8)])]
  transfers between devices with their start and end apart: 17 -> 17, of which waited for: 6 -> 9; matrix products, arithmetic and copies ran while one was open for 7% -> 10% of each run, Pallas kernels for 26% -> 17%
where the time goes in v1:
time: 167 us; the launch traced here: 165 us
  waiting for transfers between devices  61.1 us (37%)
  Pallas kernels  44.8 us (27%)
  starting transfers between devices  33.6 us (20%)
  local copies, waits for them, and re-layouts  15 us (9%)
  other arithmetic  5.63 us (3%)
  between operations  4.45 us (3%)
    ppermute x10, waiting for transfers between devices, shifted(): return lax.ppermute(x, axis, [((i - distance) % n, i) for i in range(n)])  23 us
    ppermute x3, waiting for transfers between devices, swapped(): return lax.ppermute(x, 'head', [(i, i ^ 1) for i in range(8)])  15.1 us
    pallas_call x1, Pallas kernels, backward(): pl.pallas_call(backward_kernel, out_shape=(jax.ShapeDtypeStruct((GROUP, 3...  13.1 us
    ppermute x10, starting transfers between devices, shifted(): return lax.ppermute(x, axis, [((i - distance) % n, i) for i in range(n)])  12.8 us
    ppermute x1, waiting for transfers between devices, summed_over_groups(): got = lax.ppermute(sent, 'dp', [(i, i ^ 2) for i in range(16)])  12.4 us
    pallas_call x1, Pallas kernels, forward_home(): pl.pallas_call(forward_home_kernel, out_shape=(jax.ShapeDtypeStruct((HOME...  12.1 us
    all_to_all x1, waiting for transfers between devices, local(): lax.all_to_all(packed, 'head', split_axis=1, concat_axis=0, tiled=False)  9.28 us
    pallas_call x2, Pallas kernels, grad_att(): pl.pallas_call(functools.partial(grad_att_kernel, count), grid=(4,), out_...  7.74 us
  transfers between devices with their start and end apart: 17, of which 9 were waited for; matrix products, arithmetic and copies ran while one was open for 10% of the time, Pallas kernels for 17%

profile of v1, /device:TPU:0, one launch (start us, length us, event | category | flops | bytes accessed | tf_op | source)
XLA Modules:
  0.0 164.6 jit_solution(9457936123910727400)
XLA Ops:
  2.3 3.0 %collective-permute-start.10 = (bf16[192,3072]{1,0:T(8,128)(2,1)}, bf16[192,3072]{1,0:T(8,128)(2,1)S(1)}, u32[]{:S(2)}, u32[]{:S(2)}) collective-permute-start(bf16[192,3072]{1,0:T(8,128)(2,1)} %refs_0_.1), channel_id=1, source_target_pairs={{2,0},{3,1},{4,2},{5,3},{6,4},{7,5},{0,6},{1,7},{10,8},{11,9},{12,... | collective-permute-start | bytes 3538952 | tf_op jit(solution)/shard_map/ppermute | solution.py:57
  8.4 1.9 %copy.17 = bf16[1,192,8,768]{3,1,0,2:T(8,128)(2,1)} copy(bf16[1,192,8,768]{3,2,1,0:T(8,128)(2,1)S(1)} %maximum_bitcast_fusion) | data formatting | bytes 4718592 | tf_op jit(solution)/shard_map/broadcast_in_dim | solution.py:405
  10.2 4.5 %all-to-all-start = ((bf16[1,192,8,768]{3,1,0,2:T(8,128)(2,1)}), bf16[1,192,8,768]{3,1,0,2:T(8,128)(2,1)}, u32[]{:S(2)}, u32[]{:S(2)}) async-start(bf16[1,192,8,768]{3,1,0,2:T(8,128)(2,1)} %copy.17), calls=%async_computation | async-start | bytes 4718592 | tf_op jit(solution)/shard_map/all_to_all | solution.py:405
  14.7 15.1 %collective-permute-done.8.refs_1_ = bf16[192,3072]{1,0:T(8,128)(2,1)S(1)} collective-permute-done((bf16[192,3072]{1,0:T(8,128)(2,1)}, bf16[192,3072]{1,0:T(8,128)(2,1)S(1)}, u32[]{:S(2)}, u32[]{:S(2)}) %collective-permute-start.8) | collective-permute-done | bytes 1179680 | tf_op jit(solution)/shard_map/ppermute | solution.py:61
  29.9 2.2 %collective-permute-done.10.refs_3_ = bf16[192,3072]{1,0:T(8,128)(2,1)S(1)} collective-permute-done((bf16[192,3072]{1,0:T(8,128)(2,1)}, bf16[192,3072]{1,0:T(8,128)(2,1)S(1)}, u32[]{:S(2)}, u32[]{:S(2)}) %collective-permute-start.10) | collective-permute-done | bytes 1179680 | tf_op jit(solution)/shard_map/ppermute | solution.py:57
  32.1 3.6 %collective-permute-done.9.refs_2_ = bf16[192,3072]{1,0:T(8,128)(2,1)S(1)} collective-permute-done((bf16[192,3072]{1,0:T(8,128)(2,1)}, bf16[192,3072]{1,0:T(8,128)(2,1)S(1)}, u32[]{:S(2)}, u32[]{:S(2)}) %collective-permute-start.9) | collective-permute-done | bytes 1179680 | tf_op jit(solution)/shard_map/ppermute | solution.py:57
  35.8 2.1 %pad_maximum_fusion.2 = (bf16[192,3072]{1,0:T(8,128)(2,1)}, bf16[192,3072]{1,0:T(8,128)(2,1)}, bf16[192,3072]{1,0:T(8,128)(2,1)}) fusion(bf16[96,3072]{1,0:T(8,128)(2,1)S(1)} %slice.54, bf16[96,3072]{1,0:T(8,128)(2,1)S(1)} %get-tuple-element.256, bf16[96,3072]{1,0:T(8,128)(2,1)S(1)} %slice.53, bf16[96,3072]{1,0:T(8,128)(2,1)S(1)} %get-tuple-element.257), kind=kLoop, calls=%fused_computation.5 | loop fusion | flops 5898240 | bytes 5898240 | tf_op jit(solution)/shard_map/concatenate | solution.py:412
  37.9 3.2 %collective-permute-start.12 = (bf16[192,3072]{1,0:T(8,128)(2,1)}, bf16[192,3072]{1,0:T(8,128)(2,1)S(1)}, u32[]{:S(2)}, u32[]{:S(2)}) collective-permute-start(bf16[192,3072]{1,0:T(8,128)(2,1)} %get-tuple-element.262), channel_id=1, source_target_pairs={{2,0},{3,1},{4,2},{5,3},{6,4},{7,5},{0,6},{1,7},{10,8},{11,9},{12,... | collective-permute-start | bytes 3538952 | tf_op jit(solution)/shard_map/ppermute | solution.py:57
  41.1 4.0 %collective-permute-start.13 = (bf16[192,3072]{1,0:T(8,128)(2,1)}, bf16[192,3072]{1,0:T(8,128)(2,1)S(1)}, u32[]{:S(2)}, u32[]{:S(2)}) collective-permute-start(bf16[192,3072]{1,0:T(8,128)(2,1)} %get-tuple-element.261), channel_id=1, source_target_pairs={{0,1},{1,0},{2,3},{3,2},{4,5},{5,4},{6,7},{7,6},{8,9},{9,8},{10,11... | collective-permute-start | bytes 3538952 | tf_op jit(solution)/shard_map/ppermute | solution.py:61
  49.7 2.0 %stack.53.meta_ref = s32[16]{0:T(128)S(1)} concatenate(s32[1]{0:T(128)} %get-tuple-element.265, s32[1]{0:T(128)} %get-tuple-element.270, s32[1]{0:T(128)} %get-tuple-element.271, s32[1]{0:T(128)} %constant.122.clone.1, s32[1]{0:T(128)} %bitcast.1, s32[1]{0:T(128)} %bitcast.2, s32[1]{0:T(128)} %bitcast.3, s32[1]{0:T(128)} %bitcast.4, s32[1]{0:T(128)} %bitcast.5, s32[1]{0:T(128)} %bitcast.6, ...), dimensions={0} | concatenate | bytes 128 | tf_op jit(solution)/shard_map/stack | solution.py:377
  51.7 9.3 %all-to-all-done = bf16[1,192,8,768]{3,1,0,2:T(8,128)(2,1)} async-done(((bf16[1,192,8,768]{3,1,0,2:T(8,128)(2,1)}), bf16[1,192,8,768]{3,1,0,2:T(8,128)(2,1)}, u32[]{:S(2)}, u32[]{:S(2)}) %all-to-all-start) | async-done | bytes 2359328 | tf_op jit(solution)/shard_map/all_to_all | solution.py:405
  63.0 23.9 %conditional.1 = (bf16[512,768]{1,0:T(8,128)(2,1)}, bf16[1024,256]{1,0:T(8,128)(2,1)}, bf16[2,1024,1024]{2,1,0:T(8,128)(2,1)}, bf16[768,256]{1,0:T(8,128)(2,1)S(1)}) conditional(s32[]{:T(128)} %clamp.3, (bf16[512,768]{1,0:T(8,128)(2,1)S(1)}, s32[16]{0:T(128)S(1)}, bf16[1536,768]{1,0:T(8,128)(2,1)}, ...), branch_computations={%region_0.1_spmd, %region_1.2_spmd, %region_2.3_spmd, %region_3.4_... | conditional | flops 6230400000 | bytes 11645000 | solution.py:415
  63.0 4.1 %grad_att.11 = bf16[768,256]{1,0:T(8,128)(2,1)S(1)} custom-call(bf16[256,3072]{1,0:T(8,128)(2,1)S(1)} %get-tuple-element.153.weight_ref, bf16[192,3072]{1,0:T(8,128)(2,1)} %get-tuple-element.154.refs_0_, bf16[192,3072]{1,0:T(8,128)(2,1)} %get-tuple-element.155.refs_1_, bf16[192,3072]{1,0:T(8,128)(2,1)S(1)} %get-tuple-element.156.refs_2_, ...), custom_call_target="tpu_custom_call" | custom-call | flops 230400000 | bytes 499200 | tf_op jit(solution)/shard_map/cond/branch_2_fun/grad_att/pallas_call | solution.py:173
  67.1 12.1 %forward_home.10 = (bf16[1024,256]{1,0:T(8,128)(2,1)}, bf16[2,1024,1024]{2,1,0:T(8,128)(2,1)}) custom-call(s32[16]{0:T(128)S(1)} %get-tuple-element.149.meta_ref, bf16[1536,768]{1,0:T(8,128)(2,1)} %get-tuple-element.150.qkv_ref), custom_call_target="tpu_custom_call" | custom-call | flops 6000000000 | bytes 8000000 | tf_op jit(solution)/shard_map/cond/branch_2_fun/forward_home/pallas_call | solution.py:108
  79.2 7.7 %collective-permute-done.2 = bf16[512,768]{1,0:T(8,128)(2,1)} collective-permute-done((bf16[512,768]{1,0:T(8,128)(2,1)S(1)}, bf16[512,768]{1,0:T(8,128)(2,1)}, u32[]{:S(2)}, u32[]{:S(2)}) %collective-permute-start.2) | collective-permute-done | bytes 786464 | tf_op jit(solution)/shard_map/cond/branch_2_fun/ppermute | solution.py:57
  94.2 4.3 %forward_move.1 = (bf16[1536,256]{1,0:T(8,128)(2,1)S(1)}, bf16[2,512,512]{2,1,0:T(8,128)(2,1)S(1)}) custom-call(s32[16]{0:T(128)S(1)} %stack.53.meta_ref, bf16[512,768]{1,0:T(8,128)(2,1)} %get-tuple-element.229.move_ref, bf16[1024,256]{1,0:T(8,128)(2,1)} %get-tuple-element.230.home_att_ref), custom_call_target="tpu_custom_call" | custom-call | flops 150000000 | bytes 300000 | tf_op jit(solution)/shard_map/forward_move/pallas_call | solution.py:136
  98.6 3.6 %grad_att.17.far_ref = bf16[576,256]{1,0:T(8,128)(2,1)S(1)} custom-call(bf16[256,3072]{1,0:T(8,128)(2,1)} %weight_ref.3, bf16[192,3072]{1,0:T(8,128)(2,1)S(1)} %collective-permute-done.11.refs_0_.refs_4_, bf16[192,3072]{1,0:T(8,128)(2,1)S(1)} %collective-permute-done.12.refs_1_.refs_5_, bf16[192,3072]{1,0:T(8,128)(2,1)S(1)} %collective-permute-done.13.refs_2_.refs_6_), custom_call_target="tpu_custom_call" | custom-call | flops 172800000 | bytes 374400 | tf_op jit(solution)/shard_map/grad_att/pallas_call | solution.py:173
  102.3 4.5 %grad_weight.1.sum_ref = f32[4,256,768]{2,1,0:T(8,128)S(1)} custom-call(s32[10]{0:T(128)S(1)} %stack.54.first_ref, bf16[1536,256]{1,0:T(8,128)(2,1)S(1)} %get-tuple-element.231.att_ref, bf16[192,3072]{1,0:T(8,128)(2,1)S(1)} %copy-done.10, bf16[192,3072]{1,0:T(8,128)(2,1)S(1)} %copy-done.7, bf16[192,3072]{1,0:T(8,128)(2,1)S(1)} %copy-done.5, ...), custom_call_target="tpu_custom_call" | custom-call | flops 336000000 | bytes 1075200 | tf_op jit(solution)/shard_map/grad_weight/pallas_call | solution.py:215
  106.9 13.1 %backward.1 = (bf16[1536,768]{1,0:T(8,128)(2,1)S(1)}, bf16[4,256,384]{2,1,0:T(8,128)(2,1)}, bf16[4,256,384]{2,1,0:T(8,128)(2,1)S(1)}) custom-call(s32[16]{0:T(128)S(1)} %stack.53.meta_ref, bf16[1536,768]{1,0:T(8,128)(2,1)} %bitcast.16.qkv_ref, bf16[512,768]{1,0:T(8,128)(2,1)} %get-tuple-element.229.move_ref, ...), custom_call_target="tpu_custom_call" | custom-call | flops 10000000000 | bytes 12000000 | tf_op jit(solution)/shard_map/backward/pallas_call | solution.py:317
  121.4 5.4 %collective-permute-start.17 = (bf16[4,256,384]{2,1,0:T(8,128)(2,1)}, bf16[4,256,384]{2,1,0:T(8,128)(2,1)}, u32[]{:S(2)}, u32[]{:S(2)}) collective-permute-start(bf16[4,256,384]{2,1,0:T(8,128)(2,1)} %get-tuple-element.243), channel_id=1, source_target_pairs={{0,8},{8,0},{16,24},{24,16},{32,40},{40,32},{48,56},{56,48},{64,72... | collective-permute-start | bytes 2359304 | tf_op jit(solution)/shard_map/ppermute | solution.py:346
  126.9 3.6 %all-to-all-start.1 = ((bf16[8,192,768]{2,1,0:T(8,128)(2,1)}), bf16[8,192,768]{2,1,0:T(8,128)(2,1)S(1)}, u32[]{:S(2)}, u32[]{:S(2)}) async-start(bf16[8,192,768]{2,1,0:T(8,128)(2,1)} %bitcast.37), calls=%async_computation.1 | async-start | bytes 4718592 | tf_op jit(solution)/shard_map/all_to_all | solution.py:438
  136.2 9.0 %collective-permute-done.18 = bf16[256,384]{1,0:T(8,128)(2,1)S(1)} collective-permute-done((bf16[256,384]{1,0:T(8,128)(2,1)S(1)}, bf16[256,384]{1,0:T(8,128)(2,1)S(1)}, u32[]{:S(2)}, u32[]{:S(2)}) %collective-permute-start.18) | collective-permute-done | bytes 196640 | tf_op jit(solution)/shard_map/ppermute | solution.py:57
  147.0 12.4 %collective-permute-done.21 = bf16[256,192]{1,0:T(8,128)(2,1)S(1)} collective-permute-done((bf16[256,192]{1,0:T(8,128)(2,1)S(1)}, bf16[256,192]{1,0:T(8,128)(2,1)S(1)}, u32[]{:S(2)}, u32[]{:S(2)}) %collective-permute-start.21) | collective-permute-done | bytes 98336 | tf_op jit(solution)/shard_map/ppermute | solution.py:354
  161.6 3.0 %apart.1 = (bf16[192,2048]{1,0:T(8,128)(2,1)}, bf16[192,2048]{1,0:T(8,128)(2,1)}, bf16[192,2048]{1,0:T(8,128)(2,1)}) custom-call(bf16[8,192,768]{2,1,0:T(8,128)(2,1)S(1)} %all-to-all-done.1.packed_ref), custom_call_target="tpu_custom_call" | custom-call | tf_op jit(solution)/shard_map/apart/pallas_call | solution.py:44
  (81 shorter events, 26.4 us)
Async XLA Ops:
  0.6 7.4 %copy-start.12 = (bf16[192,2048]{1,0:T(8,128)(2,1)S(1)}, bf16[192,2048]{1,0:T(8,128)(2,1)}, u32[]{:S(2)}) copy-start(bf16[192,2048]{1,0:T(8,128)(2,1)} %param.18) | copy-start | bytes 2359300
  0.6 29.2 %collective-permute-start.8 = (bf16[192,3072]{1,0:T(8,128)(2,1)}, bf16[192,3072]{1,0:T(8,128)(2,1)S(1)}, u32[]{:S(2)}, u32[]{:S(2)}) collective-permute-start(bf16[192,3072]{1,0:T(8,128)(2,1)} %refs_0_.1), channel_id=1, source_target_pairs={{0,1},{1,0},{2,3},{3,2},{4,5},{5,4},{6,7},{7,6},{8,9},{9,8},{10,11... | collective-permute-start | bytes 3538952 | tf_op jit(solution)/shard_map/ppermute | solution.py:61
  2.3 29.7 %collective-permute-start.10 = (bf16[192,3072]{1,0:T(8,128)(2,1)}, bf16[192,3072]{1,0:T(8,128)(2,1)S(1)}, u32[]{:S(2)}, u32[]{:S(2)}) collective-permute-start(bf16[192,3072]{1,0:T(8,128)(2,1)} %refs_0_.1), channel_id=1, source_target_pairs={{2,0},{3,1},{4,2},{5,3},{6,4},{7,5},{0,6},{1,7},{10,8},{11,9},{12,... | collective-permute-start | bytes 3538952 | tf_op jit(solution)/shard_map/ppermute | solution.py:57
  5.3 30.3 %collective-permute-start.9 = (bf16[192,3072]{1,0:T(8,128)(2,1)}, bf16[192,3072]{1,0:T(8,128)(2,1)S(1)}, u32[]{:S(2)}, u32[]{:S(2)}) collective-permute-start(bf16[192,3072]{1,0:T(8,128)(2,1)} %refs_0_.1), channel_id=1, source_target_pairs={{6,0},{7,1},{0,2},{1,3},{2,4},{3,5},{4,6},{5,7},{14,8},{15,9},{8,1... | collective-permute-start | bytes 3538952 | tf_op jit(solution)/shard_map/ppermute | solution.py:57
  10.2 50.8 %all-to-all-start = ((bf16[1,192,8,768]{3,1,0,2:T(8,128)(2,1)}), bf16[1,192,8,768]{3,1,0,2:T(8,128)(2,1)}, u32[]{:S(2)}, u32[]{:S(2)}) async-start(bf16[1,192,8,768]{3,1,0,2:T(8,128)(2,1)} %copy.17), calls=%async_computation | async-start | bytes 4718592 | tf_op jit(solution)/shard_map/all_to_all | solution.py:405
  29.8 5.9 %copy-start.6 = (bf16[192,3072]{1,0:T(8,128)(2,1)}, bf16[192,3072]{1,0:T(8,128)(2,1)S(1)}, u32[]{:S(2)}) copy-start(bf16[192,3072]{1,0:T(8,128)(2,1)S(1)} %collective-permute-done.8.refs_1_) | copy-start | bytes 3538948
  32.0 5.8 %copy-start.8 = (bf16[192,3072]{1,0:T(8,128)(2,1)}, bf16[192,3072]{1,0:T(8,128)(2,1)S(1)}, u32[]{:S(2)}) copy-start(bf16[192,3072]{1,0:T(8,128)(2,1)S(1)} %collective-permute-done.10.refs_3_) | copy-start | bytes 3538948
  35.7 9.4 %copy-start.15 = (s32[32]{0:T(128)S(1)}, s32[32]{0:T(128)}, u32[]{:S(2)}) copy-start(s32[32]{0:T(128)} %param.22) | copy-start | bytes 388
  35.7 11.4 %copy-start.16 = (s32[32]{0:T(128)S(1)}, s32[32]{0:T(128)}, u32[]{:S(2)}) copy-start(s32[32]{0:T(128)} %param.23) | copy-start | bytes 388
  35.8 11.4 %copy-start.17 = (s32[32]{0:T(128)S(1)}, s32[32]{0:T(128)}, u32[]{:S(2)}) copy-start(s32[32]{0:T(128)} %param.21) | copy-start | bytes 388
  37.9 49.0 %collective-permute-start.11 = (bf16[192,3072]{1,0:T(8,128)(2,1)}, bf16[192,3072]{1,0:T(8,128)(2,1)S(1)}, u32[]{:S(2)}, u32[]{:S(2)}) collective-permute-start(bf16[192,3072]{1,0:T(8,128)(2,1)} %get-tuple-element.263), channel_id=1, source_target_pairs={{6,0},{7,1},{0,2},{1,3},{2,4},{3,5},{4,6},{5,7},{14,8},{15,9},{8,1... | collective-permute-start | bytes 3538952 | tf_op jit(solution)/shard_map/ppermute | solution.py:57
  37.9 49.0 %collective-permute-start.12 = (bf16[192,3072]{1,0:T(8,128)(2,1)}, bf16[192,3072]{1,0:T(8,128)(2,1)S(1)}, u32[]{:S(2)}, u32[]{:S(2)}) collective-permute-start(bf16[192,3072]{1,0:T(8,128)(2,1)} %get-tuple-element.262), channel_id=1, source_target_pairs={{2,0},{3,1},{4,2},{5,3},{6,4},{7,5},{0,6},{1,7},{10,8},{11,9},{12,... | collective-permute-start | bytes 3538952 | tf_op jit(solution)/shard_map/ppermute | solution.py:57
  41.1 45.8 %collective-permute-start.13 = (bf16[192,3072]{1,0:T(8,128)(2,1)}, bf16[192,3072]{1,0:T(8,128)(2,1)S(1)}, u32[]{:S(2)}, u32[]{:S(2)}) collective-permute-start(bf16[192,3072]{1,0:T(8,128)(2,1)} %get-tuple-element.261), channel_id=1, source_target_pairs={{0,1},{1,0},{2,3},{3,2},{4,5},{5,4},{6,7},{7,6},{8,9},{9,8},{10,11... | collective-permute-start | bytes 3538952 | tf_op jit(solution)/shard_map/ppermute | solution.py:61
  63.0 23.9 %collective-permute-start.2 = (bf16[512,768]{1,0:T(8,128)(2,1)S(1)}, bf16[512,768]{1,0:T(8,128)(2,1)}, u32[]{:S(2)}, u32[]{:S(2)}) collective-permute-start(bf16[512,768]{1,0:T(8,128)(2,1)S(1)} %get-tuple-element.148), channel_id=1, source_target_pairs={{104,0},{112,8},{120,16},{0,24},{8,32},{16,40},{24,48},{32,56},{40... | collective-permute-start | bytes 2359304 | tf_op jit(solution)/shard_map/cond/branch_2_fun/ppermute | solution.py:57
  86.9 5.5 %copy-start.13 = (bf16[768,256]{1,0:T(8,128)(2,1)}, bf16[768,256]{1,0:T(8,128)(2,1)S(1)}, u32[]{:S(2)}) copy-start(bf16[768,256]{1,0:T(8,128)(2,1)S(1)} %get-tuple-element.234.near_ref) | copy-start | bytes 1179652
  88.5 18.3 %collective-permute-start.15 = (bf16[64,3072]{1,0:T(8,128)(2,1)}, bf16[64,3072]{1,0:T(8,128)(2,1)}, u32[]{:S(2)}, u32[]{:S(2)}) collective-permute-start(bf16[64,3072]{1,0:T(8,128)(2,1)} %pad_maximum_fusion.3), channel_id=1, source_target_pairs={{0,1},{1,0},{2,3},{3,2},{4,5},{5,4},{6,7},{7,6},{8,9},{9,8},{10,11... | collective-permute-start | bytes 1179656 | tf_op jit(solution)/shard_map/ppermute | solution.py:61
  90.1 16.7 %collective-permute-start.14 = (bf16[64,3072]{1,0:T(8,128)(2,1)}, bf16[64,3072]{1,0:T(8,128)(2,1)}, u32[]{:S(2)}, u32[]{:S(2)}) collective-permute-start(bf16[64,3072]{1,0:T(8,128)(2,1)} %slice.46), channel_id=1, source_target_pairs={{6,0},{7,1},{0,2},{1,3},{2,4},{3,5},{4,6},{5,7},{14,8},{15,9},{8,1... | collective-permute-start | bytes 1179656 | tf_op jit(solution)/shard_map/ppermute | solution.py:57
  92.4 14.4 %collective-permute-start.16 = (bf16[64,3072]{1,0:T(8,128)(2,1)}, bf16[64,3072]{1,0:T(8,128)(2,1)}, u32[]{:S(2)}, u32[]{:S(2)}) collective-permute-start(bf16[64,3072]{1,0:T(8,128)(2,1)} %slice.49), channel_id=1, source_target_pairs={{2,0},{3,1},{4,2},{5,3},{6,4},{7,5},{0,6},{1,7},{10,8},{11,9},{12,... | collective-permute-start | bytes 1179656 | tf_op jit(solution)/shard_map/ppermute | solution.py:57
  121.4 9.1 %collective-permute-start.17 = (bf16[4,256,384]{2,1,0:T(8,128)(2,1)}, bf16[4,256,384]{2,1,0:T(8,128)(2,1)}, u32[]{:S(2)}, u32[]{:S(2)}) collective-permute-start(bf16[4,256,384]{2,1,0:T(8,128)(2,1)} %get-tuple-element.243), channel_id=1, source_target_pairs={{0,8},{8,0},{16,24},{24,16},{32,40},{40,32},{48,56},{56,48},{64,72... | collective-permute-start | bytes 2359304 | tf_op jit(solution)/shard_map/ppermute | solution.py:346
  126.9 34.8 %all-to-all-start.1 = ((bf16[8,192,768]{2,1,0:T(8,128)(2,1)}), bf16[8,192,768]{2,1,0:T(8,128)(2,1)S(1)}, u32[]{:S(2)}, u32[]{:S(2)}) async-start(bf16[8,192,768]{2,1,0:T(8,128)(2,1)} %bitcast.37), calls=%async_computation.1 | async-start | bytes 4718592 | tf_op jit(solution)/shard_map/all_to_all | solution.py:438
  132.9 12.3 %collective-permute-start.18 = (bf16[256,384]{1,0:T(8,128)(2,1)S(1)}, bf16[256,384]{1,0:T(8,128)(2,1)S(1)}, u32[]{:S(2)}, u32[]{:S(2)}) collective-permute-start(bf16[256,384]{1,0:T(8,128)(2,1)S(1)} %get-tuple-element.258), channel_id=1, source_target_pairs={{96,0},{104,8},{112,16},{120,24},{0,32},{8,40},{16,48},{24,56},{32... | collective-permute-start | bytes 589832 | tf_op jit(solution)/shard_map/ppermute | solution.py:57
  132.9 12.2 %collective-permute-start.19 = (bf16[256,384]{1,0:T(8,128)(2,1)S(1)}, bf16[256,384]{1,0:T(8,128)(2,1)S(1)}, u32[]{:S(2)}, u32[]{:S(2)}) collective-permute-start(bf16[256,384]{1,0:T(8,128)(2,1)S(1)} %get-tuple-element.260), channel_id=1, source_target_pairs={{64,0},{72,8},{80,16},{88,24},{96,32},{104,40},{112,48},{120,56},{... | collective-permute-start | bytes 589832 | tf_op jit(solution)/shard_map/ppermute | solution.py:57
  134.8 11.0 %collective-permute-start.20 = (bf16[256,384]{1,0:T(8,128)(2,1)S(1)}, bf16[256,384]{1,0:T(8,128)(2,1)S(1)}, u32[]{:S(2)}, u32[]{:S(2)}) collective-permute-start(bf16[256,384]{1,0:T(8,128)(2,1)S(1)} %get-tuple-element.259), channel_id=1, source_target_pairs={{32,0},{40,8},{48,16},{56,24},{64,32},{72,40},{80,48},{88,56},{96,... | collective-permute-start | bytes 589832 | tf_op jit(solution)/shard_map/ppermute | solution.py:57
  146.9 12.5 %collective-permute-start.21 = (bf16[256,192]{1,0:T(8,128)(2,1)S(1)}, bf16[256,192]{1,0:T(8,128)(2,1)S(1)}, u32[]{:S(2)}, u32[]{:S(2)}) collective-permute-start(bf16[256,192]{1,0:T(8,128)(2,1)S(1)} %select_convert_fusion), channel_id=1, source_target_pairs={{0,16},{8,24},{16,0},{24,8},{32,48},{40,56},{48,32},{56,40},{64,80... | collective-permute-start | bytes 294920 | tf_op jit(solution)/shard_map/ppermute | solution.py:354
  (12 other events, 36.6 us)

commit v2 on v1

--- a/solution.py
+++ b/solution.py
@@ -16,6 +16,7 @@
 MOVE = 512
 HOME_MIN = 768
 MOVE_MIN = 256
+FAR_PIECES = (96, 128, 96, 128, 64, 64)
 QB = 256
 SCALE = HD ** (-0.5)
 EXP2_SCALE = SCALE * 1.4426950408889634
@@ -37,16 +38,17 @@
 
 def apart_kernel(packed_ref, *outs):
     for i, out in enumerate(outs):
-        out[...] = packed_ref[0, :, i * FEAT : (i + 1) * FEAT]
+        for j in range(4):
+            out[:, j * FEAT : (j + 1) * FEAT] = packed_ref[j, :, i * FEAT : (i + 1) * FEAT]
 
 
 def apart(packed):
     return pl.pallas_call(
         apart_kernel,
-        grid=(8,),
+        grid=(2,),
         out_shape=(jax.ShapeDtypeStruct((ROWS, 8 * FEAT), jnp.bfloat16),) * 3,
-        in_specs=[pl.BlockSpec((1, ROWS, 3 * FEAT), lambda i: (i, 0, 0))],
-        out_specs=(pl.BlockSpec((ROWS, FEAT), lambda i: (0, i)),) * 3,
+        in_specs=[pl.BlockSpec((4, ROWS, 3 * FEAT), lambda i: (i, 0, 0))],
+        out_specs=(pl.BlockSpec((ROWS, 4 * FEAT), lambda i: (0, i)),) * 3,
         compiler_params=PARAMS,
         name="apart",
     )(packed)
@@ -197,86 +199,104 @@
     return flip(jnp.concatenate(picked, axis=0))
 
 
-def grad_weight_kernel(pieces, first_ref, att_ref, *refs):
-    blocks = refs[:-2]
-    out_ref, att_t = refs[-2:]
-
-    @pl.when(pl.program_id(0) == 0)
+def middle_kernel(pieces, n_far, first_ref, weight_ref, att_ref, *refs):
+    blocks = refs[:-4]
+    grad_att_ref, out_ref, att_t, acc = refs[-4:]
+    step = pl.program_id(0)
+
+    @pl.when(step == 0)
     def _():
         att_t[...] = place_rows(att_ref, first_ref, pieces)
-
-    dy = jnp.concatenate([block[...] for block in blocks], axis=0)
-    out_ref[0] = dot(att_t[...], dy)
-
-
-def grad_weight_part(firsts, att, blocks, pieces):
+        acc[...] = jnp.zeros_like(acc)
+
+    dy = [block[...] for block in blocks]
+    acc[...] += dot(jnp.concatenate(dy[-n_far:], axis=0), weight_ref[...], NT)
+    out_ref[0] = dot(att_t[...], jnp.concatenate(dy, axis=0))
+
+    @pl.when(step == pl.num_programs(0) - 1)
+    def _():
+        grad_att_ref[...] = acc[...].astype(jnp.bfloat16)
+
+
+def middle(firsts, weight, att, near, far, pieces):
+    blocks = near + far
     total = sum(pieces)
+    far_rows = sum(block.shape[0] for block in far)
     wide = D // 4
     return pl.pallas_call(
-        functools.partial(grad_weight_kernel, pieces),
+        functools.partial(middle_kernel, pieces, len(far)),
         grid=(4,),
-        out_shape=jax.ShapeDtypeStruct((4, FEAT, wide), jnp.float32),
+        out_shape=(
+            jax.ShapeDtypeStruct((far_rows, FEAT), jnp.bfloat16),
+            jax.ShapeDtypeStruct((4, FEAT, wide), jnp.float32),
+        ),
         in_specs=[
             SMEM,
+            pl.BlockSpec((FEAT, wide), lambda j: (0, j)),
             pl.BlockSpec((GROUP, FEAT), lambda j: (0, 0)),
             *[pl.BlockSpec((block.shape[0], wide), lambda j: (0, j)) for block in blocks],
         ],
-        out_specs=pl.BlockSpec((1, FEAT, wide), lambda j: (j, 0, 0)),
-        scratch_shapes=[pltpu.VMEM((FEAT, total), jnp.bfloat16)],
+        out_specs=(
+            pl.BlockSpec((far_rows, FEAT), lambda j: (0, 0)),
+            pl.BlockSpec((1, FEAT, wide), lambda j: (j, 0, 0)),
+        ),
+        scratch_shapes=[
+            pltpu.VMEM((FEAT, total), jnp.bfloat16),
+            pltpu.VMEM((far_rows, FEAT), jnp.float32),
+        ],
         compiler_params=PARAMS,
         cost_estimate=pl.CostEstimate(
-            flops=total * 250_000, bytes_accessed=total * 800, transcendentals=0
-        ),
-        name="grad_weight",
-    )(firsts, att, *blocks)
+            flops=total * 500_000, bytes_accessed=total * 800, transcendentals=0
+        ),
+        name="middle",
+    )(firsts, weight, att, *blocks)
 
 
 def backward_clip(read, rows, prob_ref, row_first, ga_ref, att_ref, out_ref, key_acc, value_acc):
-    def one_head(head, _):
-        k_t = flip(read(1, head, 0, rows))
-        v = read(2, head, 0, rows)
-        key_acc[:rows, :] = jnp.zeros((rows, HD), jnp.float32)
-        value_acc[:rows, :] = jnp.zeros((rows, HD), jnp.float32)
-
-        def block(step, _):
-            first = pl.multiple_of(step * QB, QB)
-            there = pl.ds(pl.multiple_of(row_first + first, 128), QB)
+    k_t = [flip(read(1, head, 0, rows)) for head in range(2)]
+    key_acc[:rows, :] = jnp.zeros((rows, FEAT), jnp.float32)
+    value_acc[:rows, :] = jnp.zeros((rows, FEAT), jnp.float32)
+
+    def block(step, _):
+        first = pl.multiple_of(step * QB, QB)
+        there = pl.ds(pl.multiple_of(row_first + first, 128), QB)
+        for head in range(2):
+            side = slice(head * HD, (head + 1) * HD)
             q = read(0, head, first, QB)
+            v = read(2, head, 0, rows)
             prob = prob_ref[head, :, pl.ds(first, QB)]
-            grad_att = ga_ref[there, columns(0, head)]
-            attended = att_ref[there, columns(0, head)]
-            product = grad_att.astype(jnp.float32) * attended.astype(jnp.float32)
+            grad_att = ga_ref[there, side]
+            product = grad_att.astype(jnp.float32) * att_ref[there, side].astype(jnp.float32)
             row_dot = jnp.sum(product.T, axis=0, keepdims=True)
             grad_prob = dot(v, grad_att, NT)
             grad_score = (prob.astype(jnp.float32) * (grad_prob - row_dot)).astype(jnp.bfloat16)
-            value_acc[:rows, :] += dot(prob, grad_att)
-            key_acc[:rows, :] += dot(grad_score, q)
-            grad_query = (dot(k_t, grad_score) * SCALE).T.astype(jnp.bfloat16)
-            out_ref[there, columns(0, head)] = grad_query
-            return 0
-
-        lax.fori_loop(0, rows // QB, block, 0)
-        whole = pl.ds(pl.multiple_of(row_first, 128), rows)
-        out_ref[whole, columns(1, head)] = (key_acc[:rows, :] * SCALE).astype(jnp.bfloat16)
-        out_ref[whole, columns(2, head)] = value_acc[:rows, :].astype(jnp.bfloat16)
+            value_acc[:rows, side] += dot(prob, grad_att)
+            key_acc[:rows, side] += dot(grad_score, q)
+            grad_query = (dot(k_t[head], grad_score) * SCALE).T.astype(jnp.bfloat16)
+            out_ref[there, side] = grad_query
         return 0
 
-    lax.fori_loop(0, 2, one_head, 0)
+    lax.fori_loop(0, rows // QB, block, 0)
+    whole = pl.ds(pl.multiple_of(row_first, 128), rows)
+    out_ref[whole, FEAT : 2 * FEAT] = (key_acc[:rows, :] * SCALE).astype(jnp.bfloat16)
+    out_ref[whole, 2 * FEAT :] = value_acc[:rows, :].astype(jnp.bfloat16)
 
 
 def backward_kernel(
     meta_ref, qkv_ref, move_ref, att_ref, home_prob_ref, move_prob_ref,
     near_ref, far_ref, weight_ref, last_a, last_b, last_c, sum_ref,
-    out_ref, send_ref, keep_ref, ga_ref, key_acc, value_acc,
+    grads_ref, send_ref, keep_ref, out_ref, ga_ref, key_acc, value_acc, done,
 ):
     home_first, home_len = meta_ref[0], meta_ref[1]
     half = ROWS // 2
     for i in range(4):
         first = pl.multiple_of(meta_ref[4 + i], half)
         ga_ref[pl.ds(first, ROWS), :] = near_ref[i * ROWS : (i + 1) * ROWS, :]
-    for i in range(6):
-        first = pl.multiple_of(meta_ref[8 + i], half)
-        ga_ref[pl.ds(first, half), :] = far_ref[i * half : (i + 1) * half, :]
+    at = 0
+    for i, count in enumerate(FAR_PIECES):
+        first = pl.multiple_of(meta_ref[8 + i], 32)
+        ga_ref[pl.ds(first, count), :] = far_ref[at : at + count, :]
+        at += count
     dy = jnp.concatenate([last_a[...], last_b[...], last_c[...]], axis=0)
     last = dot(dy, weight_ref[...], NT).astype(jnp.bfloat16)
     last_rows = pl.ds(pl.multiple_of(meta_ref[14], half), ROWS)
@@ -308,25 +328,37 @@
     backward_clip(
         read_home, HOME, home_prob_ref, 0, ga_ref, att_ref, out_ref, key_acc, value_acc
     )
+    start = pltpu.make_async_copy(
+        out_ref.at[:HOME_MIN, :], grads_ref.at[:HOME_MIN, :], done.at[0]
+    )
+    start.start()
     backward_clip(
         read_move, MOVE, move_prob_ref, home_len, ga_ref, att_ref, out_ref, key_acc, value_acc
     )
+    end = pltpu.make_async_copy(
+        out_ref.at[HOME_MIN:, :], grads_ref.at[HOME_MIN:, :], done.at[1]
+    )
+    end.start()
+    start.wait()
+    end.wait()
 
 
 def backward(meta, qkv, moved, att, home_prob, move_prob, near, far, weight, last_blocks, part):
     return pl.pallas_call(
         backward_kernel,
         out_shape=(
-            jax.ShapeDtypeStruct((GROUP, 3 * FEAT), jnp.bfloat16),
+            pltpu.HBM((GROUP, 3 * FEAT), jnp.bfloat16),
             jax.ShapeDtypeStruct((4, FEAT, D // 8), jnp.bfloat16),
             jax.ShapeDtypeStruct((4, FEAT, D // 8), jnp.bfloat16),
         ),
         in_specs=[SMEM] + [VMEM] * 12,
-        out_specs=(VMEM, VMEM, VMEM),
+        out_specs=(pl.BlockSpec(memory_space=pltpu.HBM), VMEM, VMEM),
         scratch_shapes=[
+            pltpu.VMEM((GROUP, 3 * FEAT), jnp.bfloat16),
             pltpu.VMEM((GROUP, FEAT), jnp.bfloat16),
-            pltpu.VMEM((HOME, HD), jnp.float32),
-            pltpu.VMEM((HOME, HD), jnp.float32),
+            pltpu.VMEM((HOME, FEAT), jnp.float32),
+            pltpu.VMEM((HOME, FEAT), jnp.float32),
+            pltpu.SemaphoreType.DMA((2,)),
         ],
         compiler_params=PARAMS,
         cost_estimate=pl.CostEstimate(
@@ -387,9 +419,9 @@
             far_a,
             far_c,
             far_a + half,
+            far_b + third,
             far_b,
-            far_b + half,
-            far_c + half,
+            far_c + 2 * third,
             far_d,
             group_id % 2,
         ]
@@ -407,9 +439,9 @@
     padded = jnp.concatenate([qkv, jnp.zeros((MOVE // 2, 3 * FEAT), jnp.bfloat16)], axis=0)
     outgoing = lax.dynamic_slice_in_dim(padded, clip_start[2 * group_id + 1], MOVE, 0)
 
-    got_up = shifted(jnp.concatenate([dy_up[:half], dy_x[:half]]), "head", 2)
-    got_down = shifted(jnp.concatenate([dy_down[half:], dy_x[:half]]), "head", -2)
-    got_x = swapped(jnp.concatenate([dy_down[half:], dy_up[half:]]))
+    got_up = shifted(jnp.concatenate([dy_up[:half], dy_x[: 2 * third]]), "head", 2)
+    got_down = shifted(jnp.concatenate([dy_down[half:], dy_x[third:]]), "head", -2)
+    got_x = swapped(jnp.concatenate([dy_down[:third], dy_up[2 * third :]]))
 
     near_blocks = [out_grad, dy_x, dy_up, dy_down]
     moved, home_att, home_prob, near = lax.switch(
@@ -422,13 +454,12 @@
     last_blocks = [
         shifted(got_up[half : half + third], "head", 2),
         swapped(jnp.concatenate([got_up[third:half], got_down[: 2 * third - half]])),
-        shifted(got_x[half - third : half], "head", -2),
+        shifted(got_down[-third:], "head", -2),
     ]
     far_blocks = [got_up, got_down, got_x]
     att, move_prob = forward_move(meta, moved, home_att)
-    far = grad_att(out_weight, far_blocks)
-    part = grad_weight_part(
-        meta[4:14], att, near_blocks + far_blocks, (ROWS,) * 4 + (half,) * 6
+    far, part = middle(
+        meta[4:14], out_weight, att, near_blocks, far_blocks, (ROWS,) * 4 + FAR_PIECES
     )
     grads, send, keep = backward(
         meta, qkv, moved, att, home_prob, move_prob, near, far, out_weight, last_blocks, part

time: 167 us -> 156 us (0.934)
  waiting for transfers between devices: 61.1 us -> 53 us
  Pallas kernels: 44.8 us -> 40.8 us
    ppermute x1, starting transfers between devices: 5.44 us -> 0.09 us  [summed_over_groups(): got = lax.ppermute(send, 'dp', [(i, i ^ 1) for i in range(16)])]
    pallas_call x2 -> x1, Pallas kernels: 7.74 us -> 4.11 us  [grad_att(): pl.pallas_call(functools.partial(grad_att_kernel, count), grid=(4,), out_...]
    all_to_all x1, waiting for transfers between devices: 9.28 us -> 5.77 us  [local(): lax.all_to_all(packed, 'head', split_axis=1, concat_axis=0, tiled=False)]
    ppermute x1, starting transfers between devices: 0.09 us -> 3.1 us  [summed_over_groups(): got = lax.ppermute(sent, 'dp', [(i, i ^ 2) for i in range(16)])]
    ppermute x1, waiting for transfers between devices: 12.4 us -> 9.75 us  [summed_over_groups(): got = lax.ppermute(sent, 'dp', [(i, i ^ 2) for i in range(16)])]
    ppermute x10, starting transfers between devices: 12.8 us -> 14.9 us  [shifted(): return lax.ppermute(x, axis, [((i - distance) % n, i) for i in range(n)])]
    concatenate x1 -> x3, other arithmetic: 2.11 us -> 3.39 us  [the longest x1 1.27 us: local(): jnp.concatenate([dy_up[:half], dy_x[:2 * third]])]
    unnamed x42 -> x32, local copies, waits for them, and re-layouts: 6.46 us -> 7.02 us
  transfers between devices with their start and end apart: 17 -> 17, of which waited for: 9 -> 10; matrix products, arithmetic and copies ran while one was open for 10% -> 12% of each run, Pallas kernels for 17% -> 17%
where the time goes in v2:
time: 156 us; the launch traced here: 155 us
  waiting for transfers between devices  53 us (34%)
  Pallas kernels  40.8 us (26%)
  starting transfers between devices  33 us (21%)
  local copies, waits for them, and re-layouts  16.6 us (11%)
  other arithmetic  6.93 us (4%)
  between operations  4.28 us (3%)
    ppermute x10, waiting for transfers between devices, shifted(): return lax.ppermute(x, axis, [((i - distance) % n, i) for i in range(n)])  22.4 us
    ppermute x3, waiting for transfers between devices, swapped(): return lax.ppermute(x, 'head', [(i, i ^ 1) for i in range(8)])  15 us
    ppermute x10, starting transfers between devices, shifted(): return lax.ppermute(x, axis, [((i - distance) % n, i) for i in range(n)])  14.9 us
    pallas_call x1, Pallas kernels, backward(): pl.pallas_call(backward_kernel, out_shape=(pltpu.HBM((GROUP, 3 * FEAT), j...  12.3 us
    pallas_call x1, Pallas kernels, forward_home(): pl.pallas_call(forward_home_kernel, out_shape=(jax.ShapeDtypeStruct((HOME...  12.1 us
    ppermute x1, waiting for transfers between devices, summed_over_groups(): got = lax.ppermute(sent, 'dp', [(i, i ^ 2) for i in range(16)])  9.75 us
    unnamed x32, local copies, waits for them, and re-layouts  7.02 us
    ppermute x3, starting transfers between devices, swapped(): return lax.ppermute(x, 'head', [(i, i ^ 1) for i in range(8)])  6.67 us
  transfers between devices with their start and end apart: 17, of which 10 were waited for; matrix products, arithmetic and copies ran while one was open for 12% of the time, Pallas kernels for 17%

profile of v2, /device:TPU:0, one launch (start us, length us, event | category | flops | bytes accessed | tf_op | source)
XLA Modules:
  0.0 154.6 jit_solution(18317045644847825509)
XLA Ops:
  0.6 1.7 %collective-permute-start.8 = (bf16[192,3072]{1,0:T(8,128)(2,1)}, bf16[192,3072]{1,0:T(8,128)(2,1)S(1)}, u32[]{:S(2)}, u32[]{:S(2)}) collective-permute-start(bf16[192,3072]{1,0:T(8,128)(2,1)} %refs_0_.1), channel_id=1, source_target_pairs={{0,1},{1,0},{2,3},{3,2},{4,5},{5,4},{6,7},{7,6},{8,9},{9,8},{10,11... | collective-permute-start | bytes 3538952 | tf_op jit(solution)/shard_map/ppermute | solution.py:63
  3.9 1.7 %collective-permute-start.10 = (bf16[192,3072]{1,0:T(8,128)(2,1)}, bf16[192,3072]{1,0:T(8,128)(2,1)S(1)}, u32[]{:S(2)}, u32[]{:S(2)}) collective-permute-start(bf16[192,3072]{1,0:T(8,128)(2,1)} %refs_0_.1), channel_id=1, source_target_pairs={{2,0},{3,1},{4,2},{5,3},{6,4},{7,5},{0,6},{1,7},{10,8},{11,9},{12,... | collective-permute-start | bytes 3538952 | tf_op jit(solution)/shard_map/ppermute | solution.py:59
  8.6 1.9 %copy.17 = bf16[1,192,8,768]{3,1,0,2:T(8,128)(2,1)} copy(bf16[1,192,8,768]{3,2,1,0:T(8,128)(2,1)S(1)} %maximum_bitcast_fusion) | data formatting | bytes 4718592 | tf_op jit(solution)/shard_map/broadcast_in_dim | solution.py:437
  10.4 4.4 %all-to-all-start = ((bf16[1,192,8,768]{3,1,0,2:T(8,128)(2,1)}), bf16[1,192,8,768]{3,1,0,2:T(8,128)(2,1)}, u32[]{:S(2)}, u32[]{:S(2)}) async-start(bf16[1,192,8,768]{3,1,0,2:T(8,128)(2,1)} %copy.17), calls=%async_computation | async-start | bytes 4718592 | tf_op jit(solution)/shard_map/all_to_all | solution.py:437
  14.8 15.0 %collective-permute-done.8.refs_1_ = bf16[192,3072]{1,0:T(8,128)(2,1)S(1)} collective-permute-done((bf16[192,3072]{1,0:T(8,128)(2,1)}, bf16[192,3072]{1,0:T(8,128)(2,1)S(1)}, u32[]{:S(2)}, u32[]{:S(2)}) %collective-permute-start.8) | collective-permute-done | bytes 1179680 | tf_op jit(solution)/shard_map/ppermute | solution.py:63
  30.0 2.6 %collective-permute-done.9.refs_2_ = bf16[192,3072]{1,0:T(8,128)(2,1)S(1)} collective-permute-done((bf16[192,3072]{1,0:T(8,128)(2,1)}, bf16[192,3072]{1,0:T(8,128)(2,1)S(1)}, u32[]{:S(2)}, u32[]{:S(2)}) %collective-permute-start.9) | collective-permute-done | bytes 1179680 | tf_op jit(solution)/shard_map/ppermute | solution.py:59
  37.6 2.9 %collective-permute-start.12 = (bf16[224,3072]{1,0:T(8,128)(2,1)}, bf16[224,3072]{1,0:T(8,128)(2,1)S(1)}, u32[]{:S(2)}, u32[]{:S(2)}) collective-permute-start(bf16[224,3072]{1,0:T(8,128)(2,1)} %pad_maximum_fusion.1), channel_id=1, source_target_pairs={{2,0},{3,1},{4,2},{5,3},{6,4},{7,5},{0,6},{1,7},{10,8},{11,9},{12,... | collective-permute-start | bytes 4128776 | tf_op jit(solution)/shard_map/ppermute | solution.py:59
  42.4 4.5 %collective-permute-start.13 = (bf16[128,3072]{1,0:T(8,128)(2,1)}, bf16[128,3072]{1,0:T(8,128)(2,1)S(1)}, u32[]{:S(2)}, u32[]{:S(2)}) collective-permute-start(bf16[128,3072]{1,0:T(8,128)(2,1)} %pad_maximum_fusion.2), channel_id=1, source_target_pairs={{0,1},{1,0},{2,3},{3,2},{4,5},{5,4},{6,7},{7,6},{8,9},{9,8},{10,11... | collective-permute-start | bytes 2359304 | tf_op jit(solution)/shard_map/ppermute | solution.py:63
  51.4 2.0 %stack.53.meta_ref = s32[16]{0:T(128)S(1)} concatenate(s32[1]{0:T(128)} %get-tuple-element.266, s32[1]{0:T(128)} %get-tuple-element.271, s32[1]{0:T(128)} %get-tuple-element.272, s32[1]{0:T(128)} %constant.124.clone.1, s32[1]{0:T(128)} %bitcast.1, s32[1]{0:T(128)} %bitcast.2, s32[1]{0:T(128)} %bitcast.3, s32[1]{0:T(128)} %bitcast.4, s32[1]{0:T(128)} %bitcast.5, s32[1]{0:T(128)} %bitcast.6, ...), dimensions={0} | concatenate | bytes 128 | tf_op jit(solution)/shard_map/stack | solution.py:409
  53.5 5.8 %all-to-all-done = bf16[1,192,8,768]{3,1,0,2:T(8,128)(2,1)} async-done(((bf16[1,192,8,768]{3,1,0,2:T(8,128)(2,1)}), bf16[1,192,8,768]{3,1,0,2:T(8,128)(2,1)}, u32[]{:S(2)}, u32[]{:S(2)}) %all-to-all-start) | async-done | bytes 2359328 | tf_op jit(solution)/shard_map/all_to_all | solution.py:437
  61.2 17.2 %conditional.1 = (bf16[512,768]{1,0:T(8,128)(2,1)}, bf16[1024,256]{1,0:T(8,128)(2,1)}, bf16[2,1024,1024]{2,1,0:T(8,128)(2,1)}, bf16[768,256]{1,0:T(8,128)(2,1)S(1)}) conditional(s32[]{:T(128)} %clamp.3, (bf16[512,768]{1,0:T(8,128)(2,1)S(1)}, s32[16]{0:T(128)S(1)}, bf16[1536,768]{1,0:T(8,128)(2,1)}, ...), branch_computations={%region_0.1_spmd, %region_1.2_spmd, %region_2.3_spmd, %region_3.4_... | conditional | flops 6230400000 | bytes 11645000 | solution.py:447
  61.2 4.1 %grad_att.10 = bf16[768,256]{1,0:T(8,128)(2,1)S(1)} custom-call(bf16[256,3072]{1,0:T(8,128)(2,1)S(1)} %get-tuple-element.153.weight_ref, bf16[192,3072]{1,0:T(8,128)(2,1)} %get-tuple-element.154.refs_0_, bf16[192,3072]{1,0:T(8,128)(2,1)S(1)} %get-tuple-element.155.refs_1_, bf16[192,3072]{1,0:T(8,128)(2,1)} %get-tuple-element.156.refs_2_, ...), custom_call_target="tpu_custom_call" | custom-call | flops 230400000 | bytes 499200 | tf_op jit(solution)/shard_map/cond/branch_2_fun/grad_att/pallas_call | solution.py:175
  65.3 12.1 %forward_home.10 = (bf16[1024,256]{1,0:T(8,128)(2,1)}, bf16[2,1024,1024]{2,1,0:T(8,128)(2,1)}) custom-call(s32[16]{0:T(128)S(1)} %get-tuple-element.149.meta_ref, bf16[1536,768]{1,0:T(8,128)(2,1)} %get-tuple-element.150.qkv_ref), custom_call_target="tpu_custom_call" | custom-call | flops 6000000000 | bytes 8000000 | tf_op jit(solution)/shard_map/cond/branch_2_fun/forward_home/pallas_call | solution.py:110
  78.4 7.6 %collective-permute-done.11.refs_4_ = bf16[224,3072]{1,0:T(8,128)(2,1)S(1)} collective-permute-done((bf16[224,3072]{1,0:T(8,128)(2,1)}, bf16[224,3072]{1,0:T(8,128)(2,1)S(1)}, u32[]{:S(2)}, u32[]{:S(2)}) %collective-permute-start.11) | collective-permute-done | bytes 1376288 | tf_op jit(solution)/shard_map/ppermute | solution.py:59
  90.5 1.7 %collective-permute-start.16 = (bf16[64,3072]{1,0:T(8,128)(2,1)}, bf16[64,3072]{1,0:T(8,128)(2,1)}, u32[]{:S(2)}, u32[]{:S(2)}) collective-permute-start(bf16[64,3072]{1,0:T(8,128)(2,1)} %slice.55), channel_id=1, source_target_pairs={{2,0},{3,1},{4,2},{5,3},{6,4},{7,5},{0,6},{1,7},{10,8},{11,9},{12,... | collective-permute-start | bytes 1179656 | tf_op jit(solution)/shard_map/ppermute | solution.py:59
  92.3 4.3 %forward_move.1 = (bf16[1536,256]{1,0:T(8,128)(2,1)S(1)}, bf16[2,512,512]{2,1,0:T(8,128)(2,1)S(1)}) custom-call(s32[16]{0:T(128)S(1)} %stack.53.meta_ref, bf16[512,768]{1,0:T(8,128)(2,1)} %get-tuple-element.231.move_ref, bf16[1024,256]{1,0:T(8,128)(2,1)} %get-tuple-element.232.home_att_ref), custom_call_target="tpu_custom_call" | custom-call | flops 150000000 | bytes 300000 | tf_op jit(solution)/shard_map/forward_move/pallas_call | solution.py:138
  96.7 6.5 %middle.1 = (bf16[576,256]{1,0:T(8,128)(2,1)S(1)}, f32[4,256,768]{2,1,0:T(8,128)S(1)}) custom-call(s32[10]{0:T(128)S(1)} %stack.54.first_ref, bf16[256,3072]{1,0:T(8,128)(2,1)} %weight_ref.3, bf16[1536,256]{1,0:T(8,128)(2,1)S(1)} %get-tuple-element.233.att_ref, bf16[192,3072]{1,0:T(8,128)(2,1)} %refs_0_.1, bf16[192,3072]{1,0:T(8,128)(2,1)} %copy-done.2, ...), custom_call_target="tpu_custom_call" | custom-call | flops 672000000 | bytes 1075200 | tf_op jit(solution)/shard_map/middle/pallas_call | solution.py:226
  103.2 12.3 %backward.1 = (bf16[1536,768]{1,0:T(8,128)(2,1)}, bf16[4,256,384]{2,1,0:T(8,128)(2,1)}, bf16[4,256,384]{2,1,0:T(8,128)(2,1)S(1)}) custom-call(s32[16]{0:T(128)S(1)} %stack.53.meta_ref, bf16[1536,768]{1,0:T(8,128)(2,1)} %bitcast.16.qkv_ref, bf16[512,768]{1,0:T(8,128)(2,1)} %get-tuple-element.231.move_ref, bf16[1536,256]{1,0:T(8,128)(2,1)S(1)} %get-tuple-element.233.att_ref, ...), custom_call_target="tpu_custom_call" | custom-call | flops 10000000000 | bytes 12000000 | tf_op jit(solution)/shard_map/backward/pallas_call | solution.py:347
  115.6 3.9 %all-to-all-start.1 = ((bf16[8,192,768]{2,1,0:T(8,128)(2,1)}), bf16[8,192,768]{2,1,0:T(8,128)(2,1)S(1)}, u32[]{:S(2)}, u32[]{:S(2)}) async-start(bf16[8,192,768]{2,1,0:T(8,128)(2,1)} %bitcast.40), calls=%async_computation.1 | async-start | bytes 4718592 | tf_op jit(solution)/shard_map/all_to_all | solution.py:469
  121.8 4.1 %collective-permute-start.20 = (bf16[256,384]{1,0:T(8,128)(2,1)S(1)}, bf16[256,384]{1,0:T(8,128)(2,1)S(1)}, u32[]{:S(2)}, u32[]{:S(2)}) collective-permute-start(bf16[256,384]{1,0:T(8,128)(2,1)S(1)} %get-tuple-element.263), channel_id=1, source_target_pairs={{32,0},{40,8},{48,16},{56,24},{64,32},{72,40},{80,48},{88,56},{96,... | collective-permute-start | bytes 589832 | tf_op jit(solution)/shard_map/ppermute | solution.py:59
  127.2 7.5 %collective-permute-done.20 = bf16[256,384]{1,0:T(8,128)(2,1)S(1)} collective-permute-done((bf16[256,384]{1,0:T(8,128)(2,1)S(1)}, bf16[256,384]{1,0:T(8,128)(2,1)S(1)}, u32[]{:S(2)}, u32[]{:S(2)}) %collective-permute-start.20) | collective-permute-done | bytes 196640 | tf_op jit(solution)/shard_map/ppermute | solution.py:59
  135.2 2.9 %collective-permute-done.18 = bf16[256,384]{1,0:T(8,128)(2,1)S(1)} collective-permute-done((bf16[256,384]{1,0:T(8,128)(2,1)S(1)}, bf16[256,384]{1,0:T(8,128)(2,1)S(1)}, u32[]{:S(2)}, u32[]{:S(2)}) %collective-permute-start.18) | collective-permute-done | bytes 196640 | tf_op jit(solution)/shard_map/ppermute | solution.py:59
  139.3 3.1 %collective-permute-start.21 = (bf16[256,192]{1,0:T(8,128)(2,1)S(1)}, bf16[256,192]{1,0:T(8,128)(2,1)S(1)}, u32[]{:S(2)}, u32[]{:S(2)}) collective-permute-start(bf16[256,192]{1,0:T(8,128)(2,1)S(1)} %select_convert_fusion), channel_id=1, source_target_pairs={{0,16},{8,24},{16,0},{24,8},{32,48},{40,56},{48,32},{56,40},{64,80... | collective-permute-start | bytes 294920 | tf_op jit(solution)/shard_map/ppermute | solution.py:386
  142.4 9.7 %collective-permute-done.21 = bf16[256,192]{1,0:T(8,128)(2,1)S(1)} collective-permute-done((bf16[256,192]{1,0:T(8,128)(2,1)S(1)}, bf16[256,192]{1,0:T(8,128)(2,1)S(1)}, u32[]{:S(2)}, u32[]{:S(2)}) %collective-permute-start.21) | collective-permute-done | bytes 98336 | tf_op jit(solution)/shard_map/ppermute | solution.py:386
  (75 shorter events, 28.1 us)
Async XLA Ops:
  0.6 7.6 %copy-start.7 = (bf16[192,2048]{1,0:T(8,128)(2,1)S(1)}, bf16[192,2048]{1,0:T(8,128)(2,1)}, u32[]{:S(2)}) copy-start(bf16[192,2048]{1,0:T(8,128)(2,1)} %param.16) | copy-start | bytes 2359300
  0.6 29.2 %collective-permute-start.8 = (bf16[192,3072]{1,0:T(8,128)(2,1)}, bf16[192,3072]{1,0:T(8,128)(2,1)S(1)}, u32[]{:S(2)}, u32[]{:S(2)}) collective-permute-start(bf16[192,3072]{1,0:T(8,128)(2,1)} %refs_0_.1), channel_id=1, source_target_pairs={{0,1},{1,0},{2,3},{3,2},{4,5},{5,4},{6,7},{7,6},{8,9},{9,8},{10,11... | collective-permute-start | bytes 3538952 | tf_op jit(solution)/shard_map/ppermute | solution.py:63
  2.3 30.3 %collective-permute-start.9 = (bf16[192,3072]{1,0:T(8,128)(2,1)}, bf16[192,3072]{1,0:T(8,128)(2,1)S(1)}, u32[]{:S(2)}, u32[]{:S(2)}) collective-permute-start(bf16[192,3072]{1,0:T(8,128)(2,1)} %refs_0_.1), channel_id=1, source_target_pairs={{6,0},{7,1},{0,2},{1,3},{2,4},{3,5},{4,6},{5,7},{14,8},{15,9},{8,1... | collective-permute-start | bytes 3538952 | tf_op jit(solution)/shard_map/ppermute | solution.py:59
  3.9 31.4 %collective-permute-start.10 = (bf16[192,3072]{1,0:T(8,128)(2,1)}, bf16[192,3072]{1,0:T(8,128)(2,1)S(1)}, u32[]{:S(2)}, u32[]{:S(2)}) collective-permute-start(bf16[192,3072]{1,0:T(8,128)(2,1)} %refs_0_.1), channel_id=1, source_target_pairs={{2,0},{3,1},{4,2},{5,3},{6,4},{7,5},{0,6},{1,7},{10,8},{11,9},{12,... | collective-permute-start | bytes 3538952 | tf_op jit(solution)/shard_map/ppermute | solution.py:59
  10.4 48.8 %all-to-all-start = ((bf16[1,192,8,768]{3,1,0,2:T(8,128)(2,1)}), bf16[1,192,8,768]{3,1,0,2:T(8,128)(2,1)}, u32[]{:S(2)}, u32[]{:S(2)}) async-start(bf16[1,192,8,768]{3,1,0,2:T(8,128)(2,1)} %copy.17), calls=%async_computation | async-start | bytes 4718592 | tf_op jit(solution)/shard_map/all_to_all | solution.py:437
  34.9 51.1 %collective-permute-start.11 = (bf16[224,3072]{1,0:T(8,128)(2,1)}, bf16[224,3072]{1,0:T(8,128)(2,1)S(1)}, u32[]{:S(2)}, u32[]{:S(2)}) collective-permute-start(bf16[224,3072]{1,0:T(8,128)(2,1)} %pad_maximum_fusion), channel_id=1, source_target_pairs={{6,0},{7,1},{0,2},{1,3},{2,4},{3,5},{4,6},{5,7},{14,8},{15,9},{8,1... | collective-permute-start | bytes 4128776 | tf_op jit(solution)/shard_map/ppermute | solution.py:59
  36.4 10.5 %copy-start.10 = (s32[32]{0:T(128)S(1)}, s32[32]{0:T(128)}, u32[]{:S(2)}) copy-start(s32[32]{0:T(128)} %param.22) | copy-start | bytes 388
  37.6 11.3 %copy-start.11 = (s32[32]{0:T(128)S(1)}, s32[32]{0:T(128)}, u32[]{:S(2)}) copy-start(s32[32]{0:T(128)} %param.23) | copy-start | bytes 388
  37.6 11.3 %copy-start.12 = (s32[32]{0:T(128)S(1)}, s32[32]{0:T(128)}, u32[]{:S(2)}) copy-start(s32[32]{0:T(128)} %param.21) | copy-start | bytes 388
  37.6 48.7 %collective-permute-start.12 = (bf16[224,3072]{1,0:T(8,128)(2,1)}, bf16[224,3072]{1,0:T(8,128)(2,1)S(1)}, u32[]{:S(2)}, u32[]{:S(2)}) collective-permute-start(bf16[224,3072]{1,0:T(8,128)(2,1)} %pad_maximum_fusion.1), channel_id=1, source_target_pairs={{2,0},{3,1},{4,2},{5,3},{6,4},{7,5},{0,6},{1,7},{10,8},{11,9},{12,... | collective-permute-start | bytes 4128776 | tf_op jit(solution)/shard_map/ppermute | solution.py:59
  42.4 36.0 %collective-permute-start.13 = (bf16[128,3072]{1,0:T(8,128)(2,1)}, bf16[128,3072]{1,0:T(8,128)(2,1)S(1)}, u32[]{:S(2)}, u32[]{:S(2)}) collective-permute-start(bf16[128,3072]{1,0:T(8,128)(2,1)} %pad_maximum_fusion.2), channel_id=1, source_target_pairs={{0,1},{1,0},{2,3},{3,2},{4,5},{5,4},{6,7},{7,6},{8,9},{9,8},{10,11... | collective-permute-start | bytes 2359304 | tf_op jit(solution)/shard_map/ppermute | solution.py:63
  61.2 17.2 %collective-permute-start.2 = (bf16[512,768]{1,0:T(8,128)(2,1)S(1)}, bf16[512,768]{1,0:T(8,128)(2,1)}, u32[]{:S(2)}, u32[]{:S(2)}) collective-permute-start(bf16[512,768]{1,0:T(8,128)(2,1)S(1)} %get-tuple-element.148), channel_id=1, source_target_pairs={{104,0},{112,8},{120,16},{0,24},{8,32},{16,40},{24,48},{32,56},{40... | collective-permute-start | bytes 2359304 | tf_op jit(solution)/shard_map/cond/branch_2_fun/ppermute | solution.py:59
  78.4 12.2 %copy-start.8 = (bf16[768,256]{1,0:T(8,128)(2,1)}, bf16[768,256]{1,0:T(8,128)(2,1)S(1)}, u32[]{:S(2)}) copy-start(bf16[768,256]{1,0:T(8,128)(2,1)S(1)} %get-tuple-element.236.near_ref) | copy-start | bytes 1179652
  87.9 15.3 %collective-permute-start.14 = (bf16[64,3072]{1,0:T(8,128)(2,1)}, bf16[64,3072]{1,0:T(8,128)(2,1)}, u32[]{:S(2)}, u32[]{:S(2)}) collective-permute-start(bf16[64,3072]{1,0:T(8,128)(2,1)} %slice.52), channel_id=1, source_target_pairs={{6,0},{7,1},{0,2},{1,3},{2,4},{3,5},{4,6},{5,7},{14,8},{15,9},{8,1... | collective-permute-start | bytes 1179656 | tf_op jit(solution)/shard_map/ppermute | solution.py:59
  90.0 13.2 %collective-permute-start.15 = (bf16[64,3072]{1,0:T(8,128)(2,1)}, bf16[64,3072]{1,0:T(8,128)(2,1)}, u32[]{:S(2)}, u32[]{:S(2)}) collective-permute-start(bf16[64,3072]{1,0:T(8,128)(2,1)} %pad_maximum_fusion.3), channel_id=1, source_target_pairs={{0,1},{1,0},{2,3},{3,2},{4,5},{5,4},{6,7},{7,6},{8,9},{9,8},{10,11... | collective-permute-start | bytes 1179656 | tf_op jit(solution)/shard_map/ppermute | solution.py:63
  90.5 12.6 %collective-permute-start.16 = (bf16[64,3072]{1,0:T(8,128)(2,1)}, bf16[64,3072]{1,0:T(8,128)(2,1)}, u32[]{:S(2)}, u32[]{:S(2)}) collective-permute-start(bf16[64,3072]{1,0:T(8,128)(2,1)} %slice.55), channel_id=1, source_target_pairs={{2,0},{3,1},{4,2},{5,3},{6,4},{7,5},{0,6},{1,7},{10,8},{11,9},{12,... | collective-permute-start | bytes 1179656 | tf_op jit(solution)/shard_map/ppermute | solution.py:59
  96.6 6.5 %copy-start.1 = (bf16[256,3072]{1,0:T(8,128)(2,1)S(1)}, bf16[256,3072]{1,0:T(8,128)(2,1)}, u32[]{:S(2)}) copy-start(bf16[256,3072]{1,0:T(8,128)(2,1)} %weight_ref.3) | copy-start | bytes 4718596
  96.7 6.5 %copy-start.9 = (bf16[768,256]{1,0:T(8,128)(2,1)S(1)}, bf16[768,256]{1,0:T(8,128)(2,1)}, u32[]{:S(2)}) copy-start(bf16[768,256]{1,0:T(8,128)(2,1)} %copy-done.8) | copy-start | bytes 1179652
  115.5 4.0 %collective-permute-start.17 = (bf16[4,256,384]{2,1,0:T(8,128)(2,1)}, bf16[4,256,384]{2,1,0:T(8,128)(2,1)}, u32[]{:S(2)}, u32[]{:S(2)}) collective-permute-start(bf16[4,256,384]{2,1,0:T(8,128)(2,1)} %get-tuple-element.247), channel_id=1, source_target_pairs={{0,8},{8,0},{16,24},{24,16},{32,40},{40,32},{48,56},{56,48},{64,72... | collective-permute-start | bytes 2359304 | tf_op jit(solution)/shard_map/ppermute | solution.py:378
  115.6 37.4 %all-to-all-start.1 = ((bf16[8,192,768]{2,1,0:T(8,128)(2,1)}), bf16[8,192,768]{2,1,0:T(8,128)(2,1)S(1)}, u32[]{:S(2)}, u32[]{:S(2)}) async-start(bf16[8,192,768]{2,1,0:T(8,128)(2,1)} %bitcast.40), calls=%async_computation.1 | async-start | bytes 4718592 | tf_op jit(solution)/shard_map/all_to_all | solution.py:469
  121.8 12.9 %collective-permute-start.20 = (bf16[256,384]{1,0:T(8,128)(2,1)S(1)}, bf16[256,384]{1,0:T(8,128)(2,1)S(1)}, u32[]{:S(2)}, u32[]{:S(2)}) collective-permute-start(bf16[256,384]{1,0:T(8,128)(2,1)S(1)} %get-tuple-element.263), channel_id=1, source_target_pairs={{32,0},{40,8},{48,16},{56,24},{64,32},{72,40},{80,48},{88,56},{96,... | collective-permute-start | bytes 589832 | tf_op jit(solution)/shard_map/ppermute | solution.py:59
  125.9 9.3 %collective-permute-start.19 = (bf16[256,384]{1,0:T(8,128)(2,1)S(1)}, bf16[256,384]{1,0:T(8,128)(2,1)S(1)}, u32[]{:S(2)}, u32[]{:S(2)}) collective-permute-start(bf16[256,384]{1,0:T(8,128)(2,1)S(1)} %get-tuple-element.264), channel_id=1, source_target_pairs={{64,0},{72,8},{80,16},{88,24},{96,32},{104,40},{112,48},{120,56},{... | collective-permute-start | bytes 589832 | tf_op jit(solution)/shard_map/ppermute | solution.py:59
  125.9 12.2 %collective-permute-start.18 = (bf16[256,384]{1,0:T(8,128)(2,1)S(1)}, bf16[256,384]{1,0:T(8,128)(2,1)S(1)}, u32[]{:S(2)}, u32[]{:S(2)}) collective-permute-start(bf16[256,384]{1,0:T(8,128)(2,1)S(1)} %get-tuple-element.262), channel_id=1, source_target_pairs={{96,0},{104,8},{112,16},{120,24},{0,32},{8,40},{16,48},{24,56},{32... | collective-permute-start | bytes 589832 | tf_op jit(solution)/shard_map/ppermute | solution.py:59
  139.3 12.8 %collective-permute-start.21 = (bf16[256,192]{1,0:T(8,128)(2,1)S(1)}, bf16[256,192]{1,0:T(8,128)(2,1)S(1)}, u32[]{:S(2)}, u32[]{:S(2)}) collective-permute-start(bf16[256,192]{1,0:T(8,128)(2,1)S(1)} %select_convert_fusion), channel_id=1, source_target_pairs={{0,16},{8,24},{16,0},{24,8},{32,48},{40,56},{48,32},{56,40},{64,80... | collective-permute-start | bytes 294920 | tf_op jit(solution)/shard_map/ppermute | solution.py:386
  (8 other events, 22.0 us)

commit v3 on v2

--- a/solution.py
+++ b/solution.py
@@ -123,34 +123,6 @@
     )(meta, qkv)
 
 
-def forward_move_kernel(meta_ref, move_ref, home_att_ref, att_ref, prob_ref):
-    home_len, arrive_len = meta_ref[1], meta_ref[2]
-
-    def read(which, head, first, count):
-        return move_ref[pl.ds(first, count), columns(which, head)]
-
-    att_ref[:HOME, :] = home_att_ref[...]
-    att_ref[HOME:, :] = jnp.zeros((GROUP - HOME, FEAT), jnp.bfloat16)
-    forward_clip(read, arrive_len, MOVE, MOVE_MIN, prob_ref, att_ref, home_len)
-
-
-def forward_move(meta, moved, home_att):
-    return pl.pallas_call(
-        forward_move_kernel,
-        out_shape=(
-            jax.ShapeDtypeStruct((GROUP, FEAT), jnp.bfloat16),
-            jax.ShapeDtypeStruct((2, MOVE, MOVE), jnp.bfloat16),
-        ),
-        in_specs=[SMEM, VMEM, VMEM],
-        out_specs=(VMEM, VMEM),
-        compiler_params=PARAMS,
-        cost_estimate=pl.CostEstimate(
-            flops=150_000_000, bytes_accessed=300_000, transcendentals=50_000
-        ),
-        name="forward_move",
-    )(meta, moved, home_att)
-
-
 def grad_att_kernel(count, weight_ref, *refs):
     blocks = refs[:count]
     out_ref, acc = refs[-2:]
@@ -190,23 +162,24 @@
     )(weight, *blocks)
 
 
-def place_rows(att_ref, first_ref, rows):
-    picked, at = [], 0
-    for count in rows:
-        first = pl.multiple_of(first_ref[at], 32)
-        picked.append(att_ref[pl.ds(first, count), :])
-        at += 1
-    return flip(jnp.concatenate(picked, axis=0))
-
-
-def middle_kernel(pieces, n_far, first_ref, weight_ref, att_ref, *refs):
-    blocks = refs[:-4]
-    grad_att_ref, out_ref, att_t, acc = refs[-4:]
+def middle_kernel(pieces, n_far, meta_ref, move_ref, home_att_ref, weight_ref, *refs):
+    blocks = refs[:-6]
+    att_ref, prob_ref, grad_att_ref, out_ref, att_t, acc = refs[-6:]
     step = pl.program_id(0)
+
+    def read(which, head, first, count):
+        return move_ref[pl.ds(first, count), columns(which, head)]
 
     @pl.when(step == 0)
     def _():
-        att_t[...] = place_rows(att_ref, first_ref, pieces)
+        att_ref[:HOME, :] = home_att_ref[...]
+        att_ref[HOME:, :] = jnp.zeros((GROUP - HOME, FEAT), jnp.bfloat16)
+        forward_clip(read, meta_ref[2], MOVE, MOVE_MIN, prob_ref, att_ref, meta_ref[1])
+        picked = [
+            att_ref[pl.ds(pl.multiple_of(meta_ref[4 + i], 32), count), :]
+            for i, count in enumerate(pieces)
+        ]
+        att_t[...] = flip(jnp.concatenate(picked, axis=0))
         acc[...] = jnp.zeros_like(acc)
 
     dy = [block[...] for block in blocks]
@@ -218,7 +191,7 @@
         grad_att_ref[...] = acc[...].astype(jnp.bfloat16)
 
 
-def middle(firsts, weight, att, near, far, pieces):
+def middle(meta, moved, home_att, weight, near, far, pieces):
     blocks = near + far
     total = sum(pieces)
     far_rows = sum(block.shape[0] for block in far)
@@ -227,16 +200,21 @@
         functools.partial(middle_kernel, pieces, len(far)),
         grid=(4,),
         out_shape=(
+            jax.ShapeDtypeStruct((GROUP, FEAT), jnp.bfloat16),
+            jax.ShapeDtypeStruct((2, MOVE, MOVE), jnp.bfloat16),
             jax.ShapeDtypeStruct((far_rows, FEAT), jnp.bfloat16),
             jax.ShapeDtypeStruct((4, FEAT, wide), jnp.float32),
         ),
         in_specs=[
             SMEM,
+            VMEM,
+            VMEM,
             pl.BlockSpec((FEAT, wide), lambda j: (0, j)),
-            pl.BlockSpec((GROUP, FEAT), lambda j: (0, 0)),
             *[pl.BlockSpec((block.shape[0], wide), lambda j: (0, j)) for block in blocks],
         ],
         out_specs=(
+            VMEM,
+            VMEM,
             pl.BlockSpec((far_rows, FEAT), lambda j: (0, 0)),
             pl.BlockSpec((1, FEAT, wide), lambda j: (j, 0, 0)),
         ),
@@ -246,10 +224,10 @@
         ],
         compiler_params=PARAMS,
         cost_estimate=pl.CostEstimate(
-            flops=total * 500_000, bytes_accessed=total * 800, transcendentals=0
+            flops=total * 600_000, bytes_accessed=total * 1_000, transcendentals=0
         ),
         name="middle",
-    )(firsts, weight, att, *blocks)
+    )(meta, moved, home_att, weight, *blocks)
 
 
 def backward_clip(read, rows, prob_ref, row_first, ga_ref, att_ref, out_ref, key_acc, value_acc):
@@ -457,9 +435,8 @@
         shifted(got_down[-third:], "head", -2),
     ]
     far_blocks = [got_up, got_down, got_x]
-    att, move_prob = forward_move(meta, moved, home_att)
-    far, part = middle(
-        meta[4:14], out_weight, att, near_blocks, far_blocks, (ROWS,) * 4 + FAR_PIECES
+    att, move_prob, far, part = middle(
+        meta, moved, home_att, out_weight, near_blocks, far_blocks, (ROWS,) * 4 + FAR_PIECES
     )
     grads, send, keep = backward(
         meta, qkv, moved, att, home_prob, move_prob, near, far, out_weight, last_blocks, part

time: 156 us -> 159 us (1.019)
  waiting for transfers between devices: 53 us -> 59.8 us
  local copies, waits for them, and re-layouts: 16.6 us -> 15 us
    ppermute x10, waiting for transfers between devices: 22.4 us -> 27.3 us  [shifted(): return lax.ppermute(x, axis, [((i - distance) % n, i) for i in range(n)])]
    pallas_call x1 -> x0, Pallas kernels: 4.34 us -> none  [forward_move(): pl.pallas_call(forward_move_kernel, out_shape=(jax.ShapeDtypeStruct((GROU...]
    pallas_call x1, Pallas kernels: 6.46 us -> 9.62 us  [middle(): pl.pallas_call(functools.partial(middle_kernel, pieces, len(far)), grid=(...]
    unnamed x32 -> x34, local copies, waits for them, and re-layouts: 7.02 us -> 7.02 us
  transfers between devices with their start and end apart: 17 -> 17, of which waited for: 10 -> 9; matrix products, arithmetic and copies ran while one was open for 12% -> 11% of each run, Pallas kernels for 17% -> 16%
where the time goes in v3:
time: 159 us; the launch traced here: 156 us
  waiting for transfers between devices  59.8 us (38%)
  Pallas kernels  39.3 us (25%)
  starting transfers between devices  31.8 us (20%)
  local copies, waits for them, and re-layouts  15 us (9%)
  other arithmetic  6.16 us (4%)
  between operations  4.38 us (3%)
    ppermute x10, waiting for transfers between devices, shifted(): return lax.ppermute(x, axis, [((i - distance) % n, i) for i in range(n)])  27.3 us
    ppermute x10, starting transfers between devices, shifted(): return lax.ppermute(x, axis, [((i - distance) % n, i) for i in range(n)])  15.4 us
    ppermute x3, waiting for transfers between devices, swapped(): return lax.ppermute(x, 'head', [(i, i ^ 1) for i in range(8)])  15 us
    pallas_call x1, Pallas kernels, forward_home(): pl.pallas_call(forward_home_kernel, out_shape=(jax.ShapeDtypeStruct((HOME...  12.1 us
    pallas_call x1, Pallas kernels, backward(): pl.pallas_call(backward_kernel, out_shape=(pltpu.HBM((GROUP, 3 * FEAT), j...  12 us
    ppermute x1, waiting for transfers between devices, summed_over_groups(): got = lax.ppermute(sent, 'dp', [(i, i ^ 2) for i in range(16)])  11 us
    pallas_call x1, Pallas kernels, middle(): pl.pallas_call(functools.partial(middle_kernel, pieces, len(far)), grid=(...  9.62 us
    unnamed x34, local copies, waits for them, and re-layouts  7.02 us
  transfers between devices with their start and end apart: 17, of which 9 were waited for; matrix products, arithmetic and copies ran while one was open for 11% of the time, Pallas kernels for 16%

profile of v3, /device:TPU:0, one launch (start us, length us, event | category | flops | bytes accessed | tf_op | source)
XLA Modules:
  0.0 156.4 jit_solution(18073587227511695409)
XLA Ops:
  0.6 1.7 %collective-permute-start.8 = (bf16[192,3072]{1,0:T(8,128)(2,1)}, bf16[192,3072]{1,0:T(8,128)(2,1)S(1)}, u32[]{:S(2)}, u32[]{:S(2)}) collective-permute-start(bf16[192,3072]{1,0:T(8,128)(2,1)} %refs_0_.1), channel_id=1, source_target_pairs={{0,1},{1,0},{2,3},{3,2},{4,5},{5,4},{6,7},{7,6},{8,9},{9,8},{10,11... | collective-permute-start | bytes 3538952 | tf_op jit(solution)/shard_map/ppermute | solution.py:63
  3.9 1.7 %collective-permute-start.10 = (bf16[192,3072]{1,0:T(8,128)(2,1)}, bf16[192,3072]{1,0:T(8,128)(2,1)S(1)}, u32[]{:S(2)}, u32[]{:S(2)}) collective-permute-start(bf16[192,3072]{1,0:T(8,128)(2,1)} %refs_0_.1), channel_id=1, source_target_pairs={{2,0},{3,1},{4,2},{5,3},{6,4},{7,5},{0,6},{1,7},{10,8},{11,9},{12,... | collective-permute-start | bytes 3538952 | tf_op jit(solution)/shard_map/ppermute | solution.py:59
  8.6 1.9 %copy.17 = bf16[1,192,8,768]{3,1,0,2:T(8,128)(2,1)} copy(bf16[1,192,8,768]{3,2,1,0:T(8,128)(2,1)S(1)} %maximum_bitcast_fusion) | data formatting | bytes 4718592 | tf_op jit(solution)/shard_map/broadcast_in_dim | solution.py:415
  10.4 4.4 %all-to-all-start = ((bf16[1,192,8,768]{3,1,0,2:T(8,128)(2,1)}), bf16[1,192,8,768]{3,1,0,2:T(8,128)(2,1)}, u32[]{:S(2)}, u32[]{:S(2)}) async-start(bf16[1,192,8,768]{3,1,0,2:T(8,128)(2,1)} %copy.17), calls=%async_computation | async-start | bytes 4718592 | tf_op jit(solution)/shard_map/all_to_all | solution.py:415
  14.8 15.0 %collective-permute-done.8.refs_1_ = bf16[192,3072]{1,0:T(8,128)(2,1)S(1)} collective-permute-done((bf16[192,3072]{1,0:T(8,128)(2,1)}, bf16[192,3072]{1,0:T(8,128)(2,1)S(1)}, u32[]{:S(2)}, u32[]{:S(2)}) %collective-permute-start.8) | collective-permute-done | bytes 1179680 | tf_op jit(solution)/shard_map/ppermute | solution.py:63
  30.0 2.6 %collective-permute-done.9.refs_2_ = bf16[192,3072]{1,0:T(8,128)(2,1)S(1)} collective-permute-done((bf16[192,3072]{1,0:T(8,128)(2,1)}, bf16[192,3072]{1,0:T(8,128)(2,1)S(1)}, u32[]{:S(2)}, u32[]{:S(2)}) %collective-permute-start.9) | collective-permute-done | bytes 1179680 | tf_op jit(solution)/shard_map/ppermute | solution.py:59
  37.6 2.9 %collective-permute-start.12 = (bf16[224,3072]{1,0:T(8,128)(2,1)}, bf16[224,3072]{1,0:T(8,128)(2,1)S(1)}, u32[]{:S(2)}, u32[]{:S(2)}) collective-permute-start(bf16[224,3072]{1,0:T(8,128)(2,1)} %pad_maximum_fusion.1), channel_id=1, source_target_pairs={{2,0},{3,1},{4,2},{5,3},{6,4},{7,5},{0,6},{1,7},{10,8},{11,9},{12,... | collective-permute-start | bytes 4128776 | tf_op jit(solution)/shard_map/ppermute | solution.py:59
  42.4 4.5 %collective-permute-start.13 = (bf16[128,3072]{1,0:T(8,128)(2,1)}, bf16[128,3072]{1,0:T(8,128)(2,1)S(1)}, u32[]{:S(2)}, u32[]{:S(2)}) collective-permute-start(bf16[128,3072]{1,0:T(8,128)(2,1)} %pad_maximum_fusion.2), channel_id=1, source_target_pairs={{0,1},{1,0},{2,3},{3,2},{4,5},{5,4},{6,7},{7,6},{8,9},{9,8},{10,11... | collective-permute-start | bytes 2359304 | tf_op jit(solution)/shard_map/ppermute | solution.py:63
  51.5 2.0 %stack.51.meta_ref = s32[16]{0:T(128)S(1)} concatenate(s32[1]{0:T(128)} %get-tuple-element.266, s32[1]{0:T(128)} %get-tuple-element.271, s32[1]{0:T(128)} %get-tuple-element.272, s32[1]{0:T(128)} %constant.124.clone.1, s32[1]{0:T(128)} %bitcast.1, s32[1]{0:T(128)} %bitcast.2, s32[1]{0:T(128)} %bitcast.3, s32[1]{0:T(128)} %bitcast.4, s32[1]{0:T(128)} %bitcast.5, s32[1]{0:T(128)} %bitcast.6, ...), dimensions={0} | concatenate | bytes 128 | tf_op jit(solution)/shard_map/stack | solution.py:387
  53.5 5.8 %all-to-all-done = bf16[1,192,8,768]{3,1,0,2:T(8,128)(2,1)} async-done(((bf16[1,192,8,768]{3,1,0,2:T(8,128)(2,1)}), bf16[1,192,8,768]{3,1,0,2:T(8,128)(2,1)}, u32[]{:S(2)}, u32[]{:S(2)}) %all-to-all-start) | async-done | bytes 2359328 | tf_op jit(solution)/shard_map/all_to_all | solution.py:415
  61.2 32.4 %conditional.1 = (bf16[512,768]{1,0:T(8,128)(2,1)}, bf16[1024,256]{1,0:T(8,128)(2,1)}, bf16[2,1024,1024]{2,1,0:T(8,128)(2,1)}, bf16[768,256]{1,0:T(8,128)(2,1)S(1)}) conditional(s32[]{:T(128)} %clamp.3, (bf16[512,768]{1,0:T(8,128)(2,1)S(1)}, s32[16]{0:T(128)S(1)}, bf16[1536,768]{1,0:T(8,128)(2,1)}, ...), branch_computations={%region_0.1_spmd, %region_1.2_spmd, %region_2.3_spmd, %region_3.4_... | conditional | flops 6230400000 | bytes 11645000 | solution.py:425
  61.2 2.7 %collective-permute-start.1 = (bf16[512,768]{1,0:T(8,128)(2,1)S(1)}, bf16[512,768]{1,0:T(8,128)(2,1)}, u32[]{:S(2)}, u32[]{:S(2)}) collective-permute-start(bf16[512,768]{1,0:T(8,128)(2,1)S(1)} %get-tuple-element.138), channel_id=1, source_target_pairs={{112,0},{120,8},{0,16},{8,24},{16,32},{24,40},{32,48},{40,56},{48,... | collective-permute-start | bytes 2359304 | tf_op jit(solution)/shard_map/cond/branch_1_fun/ppermute | solution.py:59
  63.8 4.1 %grad_att.9 = bf16[768,256]{1,0:T(8,128)(2,1)S(1)} custom-call(bf16[256,3072]{1,0:T(8,128)(2,1)S(1)} %get-tuple-element.143.weight_ref, bf16[192,3072]{1,0:T(8,128)(2,1)} %get-tuple-element.144.refs_0_, bf16[192,3072]{1,0:T(8,128)(2,1)S(1)} %get-tuple-element.145.refs_1_, bf16[192,3072]{1,0:T(8,128)(2,1)} %get-tuple-element.146.refs_2_, ...), custom_call_target="tpu_custom_call" | custom-call | flops 230400000 | bytes 499200 | tf_op jit(solution)/shard_map/cond/branch_1_fun/grad_att/pallas_call | solution.py:147
  67.9 12.1 %forward_home.9 = (bf16[1024,256]{1,0:T(8,128)(2,1)}, bf16[2,1024,1024]{2,1,0:T(8,128)(2,1)}) custom-call(s32[16]{0:T(128)S(1)} %get-tuple-element.139.meta_ref, bf16[1536,768]{1,0:T(8,128)(2,1)} %get-tuple-element.140.qkv_ref), custom_call_target="tpu_custom_call" | custom-call | flops 6000000000 | bytes 8000000 | tf_op jit(solution)/shard_map/cond/branch_1_fun/forward_home/pallas_call | solution.py:110
  80.0 13.6 %collective-permute-done.1 = bf16[512,768]{1,0:T(8,128)(2,1)} collective-permute-done((bf16[512,768]{1,0:T(8,128)(2,1)S(1)}, bf16[512,768]{1,0:T(8,128)(2,1)}, u32[]{:S(2)}, u32[]{:S(2)}) %collective-permute-start.1) | collective-permute-done | bytes 786464 | tf_op jit(solution)/shard_map/cond/branch_1_fun/ppermute | solution.py:59
  95.9 2.5 %collective-permute-start.16 = (bf16[64,3072]{1,0:T(8,128)(2,1)S(1)}, bf16[64,3072]{1,0:T(8,128)(2,1)S(1)}, u32[]{:S(2)}, u32[]{:S(2)}) collective-permute-start(bf16[64,3072]{1,0:T(8,128)(2,1)S(1)} %slice.53), channel_id=1, source_target_pairs={{2,0},{3,1},{4,2},{5,3},{6,4},{7,5},{0,6},{1,7},{10,8},{11,9},{12,... | collective-permute-start | bytes 1179656 | tf_op jit(solution)/shard_map/ppermute | solution.py:59
  98.4 9.6 %middle.1 = (bf16[1536,256]{1,0:T(8,128)(2,1)S(1)}, bf16[2,512,512]{2,1,0:T(8,128)(2,1)S(1)}, bf16[576,256]{1,0:T(8,128)(2,1)S(1)}, f32[4,256,768]{2,1,0:T(8,128)S(1)}) custom-call(s32[16]{0:T(128)S(1)} %stack.51.meta_ref, bf16[512,768]{1,0:T(8,128)(2,1)} %get-tuple-element.231.move_ref, bf16[1024,256]{1,0:T(8,128)(2,1)} %get-tuple-element.232.home_att_ref, ...), custom_call_target="tpu_custom_call" | custom-call | flops 806400000 | bytes 1344000 | tf_op jit(solution)/shard_map/middle/pallas_call | solution.py:199
  108.1 12.0 %backward.1 = (bf16[1536,768]{1,0:T(8,128)(2,1)}, bf16[4,256,384]{2,1,0:T(8,128)(2,1)}, bf16[4,256,384]{2,1,0:T(8,128)(2,1)S(1)}) custom-call(s32[16]{0:T(128)S(1)} %stack.51.meta_ref, bf16[1536,768]{1,0:T(8,128)(2,1)} %bitcast.16.qkv_ref, bf16[512,768]{1,0:T(8,128)(2,1)} %get-tuple-element.231.move_ref, bf16[1536,256]{1,0:T(8,128)(2,1)S(1)} %get-tuple-element.236.att_ref, ...), custom_call_target="tpu_custom_call" | custom-call | flops 10000000000 | bytes 12000000 | tf_op jit(solution)/shard_map/backward/pallas_call | solution.py:325
  120.2 3.6 %all-to-all-start.1 = ((bf16[8,192,768]{2,1,0:T(8,128)(2,1)}), bf16[8,192,768]{2,1,0:T(8,128)(2,1)S(1)}, u32[]{:S(2)}, u32[]{:S(2)}) async-start(bf16[8,192,768]{2,1,0:T(8,128)(2,1)} %bitcast.40), calls=%async_computation.1 | async-start | bytes 4718592 | tf_op jit(solution)/shard_map/all_to_all | solution.py:446
  128.3 5.7 %collective-permute-done.20 = bf16[256,384]{1,0:T(8,128)(2,1)S(1)} collective-permute-done((bf16[256,384]{1,0:T(8,128)(2,1)S(1)}, bf16[256,384]{1,0:T(8,128)(2,1)S(1)}, u32[]{:S(2)}, u32[]{:S(2)}) %collective-permute-start.20) | collective-permute-done | bytes 196640 | tf_op jit(solution)/shard_map/ppermute | solution.py:59
  133.9 2.0 %collective-permute-done.19 = bf16[256,384]{1,0:T(8,128)(2,1)S(1)} collective-permute-done((bf16[256,384]{1,0:T(8,128)(2,1)S(1)}, bf16[256,384]{1,0:T(8,128)(2,1)S(1)}, u32[]{:S(2)}, u32[]{:S(2)}) %collective-permute-start.19) | collective-permute-done | bytes 196640 | tf_op jit(solution)/shard_map/ppermute | solution.py:59
  135.9 3.4 %collective-permute-done.18 = bf16[256,384]{1,0:T(8,128)(2,1)S(1)} collective-permute-done((bf16[256,384]{1,0:T(8,128)(2,1)S(1)}, bf16[256,384]{1,0:T(8,128)(2,1)S(1)}, u32[]{:S(2)}, u32[]{:S(2)}) %collective-permute-start.18) | collective-permute-done | bytes 196640 | tf_op jit(solution)/shard_map/ppermute | solution.py:59
  140.5 1.7 %collective-permute-start.21 = (bf16[256,192]{1,0:T(8,128)(2,1)S(1)}, bf16[256,192]{1,0:T(8,128)(2,1)S(1)}, u32[]{:S(2)}, u32[]{:S(2)}) collective-permute-start(bf16[256,192]{1,0:T(8,128)(2,1)S(1)} %select_convert_fusion), channel_id=1, source_target_pairs={{0,16},{8,24},{16,0},{24,8},{32,48},{40,56},{48,32},{56,40},{64,80... | collective-permute-start | bytes 294920 | tf_op jit(solution)/shard_map/ppermute | solution.py:364
  142.2 11.0 %collective-permute-done.21 = bf16[256,192]{1,0:T(8,128)(2,1)S(1)} collective-permute-done((bf16[256,192]{1,0:T(8,128)(2,1)S(1)}, bf16[256,192]{1,0:T(8,128)(2,1)S(1)}, u32[]{:S(2)}, u32[]{:S(2)}) %collective-permute-start.21) | collective-permute-done | bytes 98336 | tf_op jit(solution)/shard_map/ppermute | solution.py:364
  (75 shorter events, 25.9 us)
Async XLA Ops:
  0.6 7.6 %copy-start.8 = (bf16[192,2048]{1,0:T(8,128)(2,1)S(1)}, bf16[192,2048]{1,0:T(8,128)(2,1)}, u32[]{:S(2)}) copy-start(bf16[192,2048]{1,0:T(8,128)(2,1)} %param.16) | copy-start | bytes 2359300
  0.6 29.2 %collective-permute-start.8 = (bf16[192,3072]{1,0:T(8,128)(2,1)}, bf16[192,3072]{1,0:T(8,128)(2,1)S(1)}, u32[]{:S(2)}, u32[]{:S(2)}) collective-permute-start(bf16[192,3072]{1,0:T(8,128)(2,1)} %refs_0_.1), channel_id=1, source_target_pairs={{0,1},{1,0},{2,3},{3,2},{4,5},{5,4},{6,7},{7,6},{8,9},{9,8},{10,11... | collective-permute-start | bytes 3538952 | tf_op jit(solution)/shard_map/ppermute | solution.py:63
  2.3 30.3 %collective-permute-start.9 = (bf16[192,3072]{1,0:T(8,128)(2,1)}, bf16[192,3072]{1,0:T(8,128)(2,1)S(1)}, u32[]{:S(2)}, u32[]{:S(2)}) collective-permute-start(bf16[192,3072]{1,0:T(8,128)(2,1)} %refs_0_.1), channel_id=1, source_target_pairs={{6,0},{7,1},{0,2},{1,3},{2,4},{3,5},{4,6},{5,7},{14,8},{15,9},{8,1... | collective-permute-start | bytes 3538952 | tf_op jit(solution)/shard_map/ppermute | solution.py:59
  3.9 31.4 %collective-permute-start.10 = (bf16[192,3072]{1,0:T(8,128)(2,1)}, bf16[192,3072]{1,0:T(8,128)(2,1)S(1)}, u32[]{:S(2)}, u32[]{:S(2)}) collective-permute-start(bf16[192,3072]{1,0:T(8,128)(2,1)} %refs_0_.1), channel_id=1, source_target_pairs={{2,0},{3,1},{4,2},{5,3},{6,4},{7,5},{0,6},{1,7},{10,8},{11,9},{12,... | collective-permute-start | bytes 3538952 | tf_op jit(solution)/shard_map/ppermute | solution.py:59
  10.4 48.8 %all-to-all-start = ((bf16[1,192,8,768]{3,1,0,2:T(8,128)(2,1)}), bf16[1,192,8,768]{3,1,0,2:T(8,128)(2,1)}, u32[]{:S(2)}, u32[]{:S(2)}) async-start(bf16[1,192,8,768]{3,1,0,2:T(8,128)(2,1)} %copy.17), calls=%async_computation | async-start | bytes 4718592 | tf_op jit(solution)/shard_map/all_to_all | solution.py:415
  34.9 58.7 %collective-permute-start.11 = (bf16[224,3072]{1,0:T(8,128)(2,1)}, bf16[224,3072]{1,0:T(8,128)(2,1)S(1)}, u32[]{:S(2)}, u32[]{:S(2)}) collective-permute-start(bf16[224,3072]{1,0:T(8,128)(2,1)} %pad_maximum_fusion), channel_id=1, source_target_pairs={{6,0},{7,1},{0,2},{1,3},{2,4},{3,5},{4,6},{5,7},{14,8},{15,9},{8,1... | collective-permute-start | bytes 4128776 | tf_op jit(solution)/shard_map/ppermute | solution.py:59
  35.3 6.1 %slice-start = ((bf16[192,3072]{1,0:T(8,128)(2,1)}), bf16[64,3072]{1,0:T(8,128)(2,1)S(1)}, s32[]{:S(2)}) async-start(bf16[192,3072]{1,0:T(8,128)(2,1)} %copy-done.5), calls=%async_computation.2 | async-start | bytes 786432 | tf_op jit(solution)/shard_map/slice | solution.py:422
  36.4 10.5 %copy-start.11 = (s32[32]{0:T(128)S(1)}, s32[32]{0:T(128)}, u32[]{:S(2)}) copy-start(s32[32]{0:T(128)} %param.22) | copy-start | bytes 388
  37.6 11.3 %copy-start.12 = (s32[32]{0:T(128)S(1)}, s32[32]{0:T(128)}, u32[]{:S(2)}) copy-start(s32[32]{0:T(128)} %param.23) | copy-start | bytes 388
  37.6 11.3 %copy-start.13 = (s32[32]{0:T(128)S(1)}, s32[32]{0:T(128)}, u32[]{:S(2)}) copy-start(s32[32]{0:T(128)} %param.21) | copy-start | bytes 388
  37.6 56.0 %collective-permute-start.12 = (bf16[224,3072]{1,0:T(8,128)(2,1)}, bf16[224,3072]{1,0:T(8,128)(2,1)S(1)}, u32[]{:S(2)}, u32[]{:S(2)}) collective-permute-start(bf16[224,3072]{1,0:T(8,128)(2,1)} %pad_maximum_fusion.1), channel_id=1, source_target_pairs={{2,0},{3,1},{4,2},{5,3},{6,4},{7,5},{0,6},{1,7},{10,8},{11,9},{12,... | collective-permute-start | bytes 4128776 | tf_op jit(solution)/shard_map/ppermute | solution.py:59
  42.4 51.2 %collective-permute-start.13 = (bf16[128,3072]{1,0:T(8,128)(2,1)}, bf16[128,3072]{1,0:T(8,128)(2,1)S(1)}, u32[]{:S(2)}, u32[]{:S(2)}) collective-permute-start(bf16[128,3072]{1,0:T(8,128)(2,1)} %pad_maximum_fusion.2), channel_id=1, source_target_pairs={{0,1},{1,0},{2,3},{3,2},{4,5},{5,4},{6,7},{7,6},{8,9},{9,8},{10,11... | collective-permute-start | bytes 2359304 | tf_op jit(solution)/shard_map/ppermute | solution.py:63
  61.2 32.4 %collective-permute-start.1 = (bf16[512,768]{1,0:T(8,128)(2,1)S(1)}, bf16[512,768]{1,0:T(8,128)(2,1)}, u32[]{:S(2)}, u32[]{:S(2)}) collective-permute-start(bf16[512,768]{1,0:T(8,128)(2,1)S(1)} %get-tuple-element.138), channel_id=1, source_target_pairs={{112,0},{120,8},{0,16},{8,24},{16,32},{24,40},{32,48},{40,56},{48,... | collective-permute-start | bytes 2359304 | tf_op jit(solution)/shard_map/cond/branch_1_fun/ppermute | solution.py:59
  93.7 14.3 %collective-permute-start.14 = (bf16[64,3072]{1,0:T(8,128)(2,1)S(1)}, bf16[64,3072]{1,0:T(8,128)(2,1)S(1)}, u32[]{:S(2)}, u32[]{:S(2)}) collective-permute-start(bf16[64,3072]{1,0:T(8,128)(2,1)S(1)} %slice.50), channel_id=1, source_target_pairs={{6,0},{7,1},{0,2},{1,3},{2,4},{3,5},{4,6},{5,7},{14,8},{15,9},{8,1... | collective-permute-start | bytes 1179656 | tf_op jit(solution)/shard_map/ppermute | solution.py:59
  95.4 12.7 %collective-permute-start.15 = (bf16[64,3072]{1,0:T(8,128)(2,1)S(1)}, bf16[64,3072]{1,0:T(8,128)(2,1)S(1)}, u32[]{:S(2)}, u32[]{:S(2)}) collective-permute-start(bf16[64,3072]{1,0:T(8,128)(2,1)S(1)} %pad_maximum_fusion.3), channel_id=1, source_target_pairs={{0,1},{1,0},{2,3},{3,2},{4,5},{5,4},{6,7},{7,6},{8,9},{9,8},{10,11... | collective-permute-start | bytes 1179656 | tf_op jit(solution)/shard_map/ppermute | solution.py:63
  95.9 12.2 %collective-permute-start.16 = (bf16[64,3072]{1,0:T(8,128)(2,1)S(1)}, bf16[64,3072]{1,0:T(8,128)(2,1)S(1)}, u32[]{:S(2)}, u32[]{:S(2)}) collective-permute-start(bf16[64,3072]{1,0:T(8,128)(2,1)S(1)} %slice.53), channel_id=1, source_target_pairs={{2,0},{3,1},{4,2},{5,3},{6,4},{7,5},{0,6},{1,7},{10,8},{11,9},{12,... | collective-permute-start | bytes 1179656 | tf_op jit(solution)/shard_map/ppermute | solution.py:59
  98.4 9.7 %copy-start.10 = (bf16[768,256]{1,0:T(8,128)(2,1)S(1)}, bf16[768,256]{1,0:T(8,128)(2,1)}, u32[]{:S(2)}) copy-start(bf16[768,256]{1,0:T(8,128)(2,1)} %copy-done.9) | copy-start | bytes 1179652
  98.4 9.7 %copy-start.14 = (bf16[2,1024,1024]{2,1,0:T(8,128)(2,1)S(1)}, bf16[2,1024,1024]{2,1,0:T(8,128)(2,1)}, u32[]{:S(2)}) copy-start(bf16[2,1024,1024]{2,1,0:T(8,128)(2,1)} %get-tuple-element.237.home_prob_ref) | copy-start | bytes 12582916
  120.1 3.8 %collective-permute-start.17 = (bf16[4,256,384]{2,1,0:T(8,128)(2,1)}, bf16[4,256,384]{2,1,0:T(8,128)(2,1)}, u32[]{:S(2)}, u32[]{:S(2)}) collective-permute-start(bf16[4,256,384]{2,1,0:T(8,128)(2,1)} %get-tuple-element.247), channel_id=1, source_target_pairs={{0,8},{8,0},{16,24},{24,16},{32,40},{40,32},{48,56},{56,48},{64,72... | collective-permute-start | bytes 2359304 | tf_op jit(solution)/shard_map/ppermute | solution.py:356
  120.2 34.7 %all-to-all-start.1 = ((bf16[8,192,768]{2,1,0:T(8,128)(2,1)}), bf16[8,192,768]{2,1,0:T(8,128)(2,1)S(1)}, u32[]{:S(2)}, u32[]{:S(2)}) async-start(bf16[8,192,768]{2,1,0:T(8,128)(2,1)} %bitcast.40), calls=%async_computation.1 | async-start | bytes 4718592 | tf_op jit(solution)/shard_map/all_to_all | solution.py:446
  126.2 7.8 %collective-permute-start.20 = (bf16[256,384]{1,0:T(8,128)(2,1)S(1)}, bf16[256,384]{1,0:T(8,128)(2,1)S(1)}, u32[]{:S(2)}, u32[]{:S(2)}) collective-permute-start(bf16[256,384]{1,0:T(8,128)(2,1)S(1)} %get-tuple-element.263), channel_id=1, source_target_pairs={{32,0},{40,8},{48,16},{56,24},{64,32},{72,40},{80,48},{88,56},{96,... | collective-permute-start | bytes 589832 | tf_op jit(solution)/shard_map/ppermute | solution.py:59
  126.7 9.3 %collective-permute-start.19 = (bf16[256,384]{1,0:T(8,128)(2,1)S(1)}, bf16[256,384]{1,0:T(8,128)(2,1)S(1)}, u32[]{:S(2)}, u32[]{:S(2)}) collective-permute-start(bf16[256,384]{1,0:T(8,128)(2,1)S(1)} %get-tuple-element.264), channel_id=1, source_target_pairs={{64,0},{72,8},{80,16},{88,24},{96,32},{104,40},{112,48},{120,56},{... | collective-permute-start | bytes 589832 | tf_op jit(solution)/shard_map/ppermute | solution.py:59
  126.7 12.7 %collective-permute-start.18 = (bf16[256,384]{1,0:T(8,128)(2,1)S(1)}, bf16[256,384]{1,0:T(8,128)(2,1)S(1)}, u32[]{:S(2)}, u32[]{:S(2)}) collective-permute-start(bf16[256,384]{1,0:T(8,128)(2,1)S(1)} %get-tuple-element.262), channel_id=1, source_target_pairs={{96,0},{104,8},{112,16},{120,24},{0,32},{8,40},{16,48},{24,56},{32... | collective-permute-start | bytes 589832 | tf_op jit(solution)/shard_map/ppermute | solution.py:59
  140.5 12.7 %collective-permute-start.21 = (bf16[256,192]{1,0:T(8,128)(2,1)S(1)}, bf16[256,192]{1,0:T(8,128)(2,1)S(1)}, u32[]{:S(2)}, u32[]{:S(2)}) collective-permute-start(bf16[256,192]{1,0:T(8,128)(2,1)S(1)} %select_convert_fusion), channel_id=1, source_target_pairs={{0,16},{8,24},{16,0},{24,8},{32,48},{40,56},{48,32},{56,40},{64,80... | collective-permute-start | bytes 294920 | tf_op jit(solution)/shard_map/ppermute | solution.py:364
  (9 other events, 20.9 us)

commit v4 on v3

--- a/solution.py
+++ b/solution.py
@@ -18,6 +18,7 @@
 MOVE_MIN = 256
 FAR_PIECES = (96, 128, 96, 128, 64, 64)
 QB = 256
+BQ = 512
 SCALE = HD ** (-0.5)
 EXP2_SCALE = SCALE * 1.4426950408889634
 NEG_BIG = -1e30
@@ -25,6 +26,7 @@
 NT = (((1,), (1,)), ((), ()))
 VMEM = pl.BlockSpec(memory_space=pltpu.VMEM)
 SMEM = pl.BlockSpec(memory_space=pltpu.SMEM)
+HBM = pl.BlockSpec(memory_space=pltpu.HBM)
 PARAMS = pltpu.CompilerParams(vmem_limit_bytes=32 * 1024 * 1024)
 
 
@@ -236,13 +238,13 @@
     value_acc[:rows, :] = jnp.zeros((rows, FEAT), jnp.float32)
 
     def block(step, _):
-        first = pl.multiple_of(step * QB, QB)
-        there = pl.ds(pl.multiple_of(row_first + first, 128), QB)
+        first = pl.multiple_of(step * BQ, BQ)
+        there = pl.ds(pl.multiple_of(row_first + first, 128), BQ)
         for head in range(2):
             side = slice(head * HD, (head + 1) * HD)
-            q = read(0, head, first, QB)
+            q = read(0, head, first, BQ)
             v = read(2, head, 0, rows)
-            prob = prob_ref[head, :, pl.ds(first, QB)]
+            prob = prob_ref[head, :, pl.ds(first, BQ)]
             grad_att = ga_ref[there, side]
             product = grad_att.astype(jnp.float32) * att_ref[there, side].astype(jnp.float32)
             row_dot = jnp.sum(product.T, axis=0, keepdims=True)
@@ -254,7 +256,7 @@
             out_ref[there, side] = grad_query
         return 0
 
-    lax.fori_loop(0, rows // QB, block, 0)
+    lax.fori_loop(0, rows // BQ, block, 0)
     whole = pl.ds(pl.multiple_of(row_first, 128), rows)
     out_ref[whole, FEAT : 2 * FEAT] = (key_acc[:rows, :] * SCALE).astype(jnp.bfloat16)
     out_ref[whole, 2 * FEAT :] = value_acc[:rows, :].astype(jnp.bfloat16)
@@ -263,7 +265,7 @@
 def backward_kernel(
     meta_ref, qkv_ref, move_ref, att_ref, home_prob_ref, move_prob_ref,
     near_ref, far_ref, weight_ref, last_a, last_b, last_c, sum_ref,
-    grads_ref, send_ref, keep_ref, out_ref, ga_ref, key_acc, value_acc, done,
+    grads_ref, send_ref, keep_ref, out_ref, ga_ref, key_acc, value_acc, sent_ref, done,
 ):
     home_first, home_len = meta_ref[0], meta_ref[1]
     half = ROWS // 2
@@ -293,7 +295,9 @@
         ]
         first_core = meta_ref[15] == 0
         keep_ref[z] = jnp.where(first_core, by_core[0], by_core[1])
-        send_ref[z] = jnp.where(first_core, by_core[1], by_core[0])
+        sent_ref[z] = jnp.where(first_core, by_core[1], by_core[0])
+    put_sent = pltpu.make_async_copy(sent_ref, send_ref, done.at[2])
+    put_sent.start()
 
     def read_home(which, head, first, count):
         start = pl.multiple_of(home_first + first, 128)
@@ -319,6 +323,7 @@
     end.start()
     start.wait()
     end.wait()
+    put_sent.wait()
 
 
 def backward(meta, qkv, moved, att, home_prob, move_prob, near, far, weight, last_blocks, part):
@@ -326,17 +331,18 @@
         backward_kernel,
         out_shape=(
             pltpu.HBM((GROUP, 3 * FEAT), jnp.bfloat16),
+            pltpu.HBM((4, FEAT, D // 8), jnp.bfloat16),
             jax.ShapeDtypeStruct((4, FEAT, D // 8), jnp.bfloat16),
-            jax.ShapeDtypeStruct((4, FEAT, D // 8), jnp.bfloat16),
         ),
         in_specs=[SMEM] + [VMEM] * 12,
-        out_specs=(pl.BlockSpec(memory_space=pltpu.HBM), VMEM, VMEM),
+        out_specs=(HBM, HBM, VMEM),
         scratch_shapes=[
             pltpu.VMEM((GROUP, 3 * FEAT), jnp.bfloat16),
             pltpu.VMEM((GROUP, FEAT), jnp.bfloat16),
             pltpu.VMEM((HOME, FEAT), jnp.float32),
             pltpu.VMEM((HOME, FEAT), jnp.float32),
-            pltpu.SemaphoreType.DMA((2,)),
+            pltpu.VMEM((4, FEAT, D // 8), jnp.bfloat16),
+            pltpu.SemaphoreType.DMA((3,)),
         ],
         compiler_params=PARAMS,
         cost_estimate=pl.CostEstimate(
@@ -348,16 +354,34 @@
 
 def pick(x, index):
     return lax.dynamic_index_in_dim(x, index, 0, keepdims=False)
+
+
+def both_cores_kernel(z_ref, keep_ref, got_ref, *outs):
+    for distance, out in enumerate(outs):
+        at = lax.rem(z_ref[0] + distance, 4)
+        both = keep_ref[at].astype(jnp.float32) + got_ref[at].astype(jnp.float32)
+        out[...] = both.astype(jnp.bfloat16)
+
+
+def both_cores(z, keep, got):
+    return pl.pallas_call(
+        both_cores_kernel,
+        out_shape=(jax.ShapeDtypeStruct((FEAT, D // 8), jnp.bfloat16),) * 4,
+        in_specs=[SMEM, VMEM, VMEM],
+        out_specs=(VMEM,) * 4,
+        compiler_params=PARAMS,
+        cost_estimate=pl.CostEstimate(flops=0, bytes_accessed=3_000_000, transcendentals=0),
+        name="both_cores",
+    )(z.reshape(1).astype(jnp.int32), keep, got)
 
 
 def summed_over_groups(send, keep):
     group_id = lax.axis_index("dp")
     z, xh = group_id // 4, group_id // 2 % 2
     got = lax.ppermute(send, "dp", [(i, i ^ 1) for i in range(16)])
-    both = (keep.astype(jnp.float32) + got.astype(jnp.float32)).astype(jnp.bfloat16)
-    total = pick(both, z).astype(jnp.float32)
-    for distance in (1, 2, 3):
-        sent = pick(both, (z + distance) % 4)
+    mine, *rest = both_cores(z, keep, got)
+    total = mine.astype(jnp.float32)
+    for distance, sent in enumerate(rest, 1):
         total = total + shifted(sent, "dp", 4 * distance).astype(jnp.float32)
     low, high = total[:, : D // 16], total[:, D // 16 :]
     sent = jnp.where(xh == 0, high, low).astype(jnp.bfloat16)

time: 159 us -> 147 us (0.925); the launches traced: 156 us -> 146 us
  waiting for transfers between devices: 59.8 us -> 52.3 us
  other arithmetic: 6.16 us -> 3.92 us
  local copies, waits for them, and re-layouts: 15 us -> 13.2 us
    ppermute x10, waiting for transfers between devices: 27.3 us -> 21.8 us  [shifted(): return lax.ppermute(x, axis, [((i - distance) % n, i) for i in range(n)])]
    ppermute x1, waiting for transfers between devices: 11 us -> 6.2 us  [summed_over_groups(): got = lax.ppermute(sent, 'dp', [(i, i ^ 2) for i in range(16)])]
    ppermute x1, waiting for transfers between devices: 0.01 us -> 2.6 us  [summed_over_groups(): got = lax.ppermute(send, 'dp', [(i, i ^ 1) for i in range(16)])]
    pallas_call x1, Pallas kernels: 12 us -> 9.98 us  [backward(): pl.pallas_call(backward_kernel, out_shape=(pltpu.HBM((GROUP, 3 * FEAT), j...]
    pallas_call x0 -> x1, Pallas kernels: none -> 1.96 us  [both_cores(): pl.pallas_call(both_cores_kernel, out_shape=(jax.ShapeDtypeStruct((FEAT,...]
    unnamed x34 -> x32, local copies, waits for them, and re-layouts: 7.02 us -> 6.18 us
  transfers between devices with their start and end apart: 17 -> 17, of which waited for: 9 -> 11; matrix products, arithmetic and copies ran while one was open for 11% -> 10% of each run, Pallas kernels for 16% -> 19%
where the time goes in v4:
time: 147 us; the launch traced here: 146 us
  waiting for transfers between devices  52.3 us (36%)
  Pallas kernels  39.3 us (27%)
  starting transfers between devices  33.3 us (23%)
  local copies, waits for them, and re-layouts  13.2 us (9%)
  between operations  4.28 us (3%)
  other arithmetic  3.92 us (3%)
    ppermute x10, waiting for transfers between devices, shifted(): return lax.ppermute(x, axis, [((i - distance) % n, i) for i in range(n)])  21.8 us
    ppermute x10, starting transfers between devices, shifted(): return lax.ppermute(x, axis, [((i - distance) % n, i) for i in range(n)])  15.3 us
    ppermute x3, waiting for transfers between devices, swapped(): return lax.ppermute(x, 'head', [(i, i ^ 1) for i in range(8)])  15 us
    pallas_call x1, Pallas kernels, forward_home(): pl.pallas_call(forward_home_kernel, out_shape=(jax.ShapeDtypeStruct((HOME...  12.1 us
    pallas_call x1, Pallas kernels, backward(): pl.pallas_call(backward_kernel, out_shape=(pltpu.HBM((GROUP, 3 * FEAT), j...  9.98 us
    pallas_call x1, Pallas kernels, middle(): pl.pallas_call(functools.partial(middle_kernel, pieces, len(far)), grid=(...  9.62 us
    ppermute x3, starting transfers between devices, swapped(): return lax.ppermute(x, 'head', [(i, i ^ 1) for i in range(8)])  6.74 us
    all_to_all x1, waiting for transfers between devices, local(): lax.all_to_all(packed, 'head', split_axis=1, concat_axis=0, tiled=False)  6.7 us
  transfers between devices with their start and end apart: 17, of which 11 were waited for; matrix products, arithmetic and copies ran while one was open for 10% of the time, Pallas kernels for 19%

profile of v4, /device:TPU:0, one launch (start us, length us, event | category | flops | bytes accessed | tf_op | source)
XLA Modules:
  0.0 146.2 jit_solution(1864288777411384655)
XLA Ops:
  3.9 1.7 %collective-permute-start.10 = (bf16[192,3072]{1,0:T(8,128)(2,1)}, bf16[192,3072]{1,0:T(8,128)(2,1)S(1)}, u32[]{:S(2)}, u32[]{:S(2)}) collective-permute-start(bf16[192,3072]{1,0:T(8,128)(2,1)} %refs_0_.1), channel_id=1, source_target_pairs={{2,0},{3,1},{4,2},{5,3},{6,4},{7,5},{0,6},{1,7},{10,8},{11,9},{12,... | collective-permute-start | bytes 3538952 | tf_op jit(solution)/shard_map/ppermute | solution.py:61
  8.6 1.9 %copy.17 = bf16[1,192,8,768]{3,1,0,2:T(8,128)(2,1)} copy(bf16[1,192,8,768]{3,2,1,0:T(8,128)(2,1)S(1)} %maximum_bitcast_fusion) | data formatting | bytes 4718592 | tf_op jit(solution)/shard_map/broadcast_in_dim | solution.py:439
  10.4 4.4 %all-to-all-start = ((bf16[1,192,8,768]{3,1,0,2:T(8,128)(2,1)}), bf16[1,192,8,768]{3,1,0,2:T(8,128)(2,1)}, u32[]{:S(2)}, u32[]{:S(2)}) async-start(bf16[1,192,8,768]{3,1,0,2:T(8,128)(2,1)} %copy.17), calls=%async_computation | async-start | bytes 4718592 | tf_op jit(solution)/shard_map/all_to_all | solution.py:439
  14.8 15.0 %collective-permute-done.8.refs_1_ = bf16[192,3072]{1,0:T(8,128)(2,1)S(1)} collective-permute-done((bf16[192,3072]{1,0:T(8,128)(2,1)}, bf16[192,3072]{1,0:T(8,128)(2,1)S(1)}, u32[]{:S(2)}, u32[]{:S(2)}) %collective-permute-start.8) | collective-permute-done | bytes 1179680 | tf_op jit(solution)/shard_map/ppermute | solution.py:65
  30.0 2.6 %collective-permute-done.9.refs_2_ = bf16[192,3072]{1,0:T(8,128)(2,1)S(1)} collective-permute-done((bf16[192,3072]{1,0:T(8,128)(2,1)}, bf16[192,3072]{1,0:T(8,128)(2,1)S(1)}, u32[]{:S(2)}, u32[]{:S(2)}) %collective-permute-start.9) | collective-permute-done | bytes 1179680 | tf_op jit(solution)/shard_map/ppermute | solution.py:61
  37.6 2.9 %collective-permute-start.12 = (bf16[224,3072]{1,0:T(8,128)(2,1)}, bf16[224,3072]{1,0:T(8,128)(2,1)S(1)}, u32[]{:S(2)}, u32[]{:S(2)}) collective-permute-start(bf16[224,3072]{1,0:T(8,128)(2,1)} %pad_maximum_fusion.1), channel_id=1, source_target_pairs={{2,0},{3,1},{4,2},{5,3},{6,4},{7,5},{0,6},{1,7},{10,8},{11,9},{12,... | collective-permute-start | bytes 4128776 | tf_op jit(solution)/shard_map/ppermute | solution.py:61
  41.4 4.5 %collective-permute-start.13 = (bf16[128,3072]{1,0:T(8,128)(2,1)}, bf16[128,3072]{1,0:T(8,128)(2,1)S(1)}, u32[]{:S(2)}, u32[]{:S(2)}) collective-permute-start(bf16[128,3072]{1,0:T(8,128)(2,1)} %pad_maximum_fusion.2), channel_id=1, source_target_pairs={{0,1},{1,0},{2,3},{3,2},{4,5},{5,4},{6,7},{7,6},{8,9},{9,8},{10,11... | collective-permute-start | bytes 2359304 | tf_op jit(solution)/shard_map/ppermute | solution.py:65
  50.5 2.0 %stack.51.meta_ref = s32[16]{0:T(128)S(1)} concatenate(s32[1]{0:T(128)} %get-tuple-element.271, s32[1]{0:T(128)} %get-tuple-element.276, s32[1]{0:T(128)} %get-tuple-element.277, s32[1]{0:T(128)} %constant.98.clone.1, s32[1]{0:T(128)} %bitcast.1, s32[1]{0:T(128)} %bitcast.2, s32[1]{0:T(128)} %bitcast.3, s32[1]{0:T(128)} %bitcast.4, s32[1]{0:T(128)} %bitcast.5, s32[1]{0:T(128)} %bitcast.6, ...), dimensions={0} | concatenate | bytes 128 | tf_op jit(solution)/shard_map/stack | solution.py:411
  52.5 6.7 %all-to-all-done = bf16[1,192,8,768]{3,1,0,2:T(8,128)(2,1)} async-done(((bf16[1,192,8,768]{3,1,0,2:T(8,128)(2,1)}), bf16[1,192,8,768]{3,1,0,2:T(8,128)(2,1)}, u32[]{:S(2)}, u32[]{:S(2)}) %all-to-all-start) | async-done | bytes 2359328 | tf_op jit(solution)/shard_map/all_to_all | solution.py:439
  61.2 17.2 %conditional.1 = (bf16[512,768]{1,0:T(8,128)(2,1)}, bf16[1024,256]{1,0:T(8,128)(2,1)}, bf16[2,1024,1024]{2,1,0:T(8,128)(2,1)}, bf16[768,256]{1,0:T(8,128)(2,1)S(1)}) conditional(s32[]{:T(128)} %clamp.3, (bf16[512,768]{1,0:T(8,128)(2,1)S(1)}, s32[16]{0:T(128)S(1)}, bf16[1536,768]{1,0:T(8,128)(2,1)}, ...), branch_computations={%region_0.1_spmd, %region_1.2_spmd, %region_2.3_spmd, %region_3.4_... | conditional | flops 6230400000 | bytes 11645000 | solution.py:449
  61.7 4.1 %grad_att.14 = bf16[768,256]{1,0:T(8,128)(2,1)S(1)} custom-call(bf16[256,3072]{1,0:T(8,128)(2,1)S(1)} %get-tuple-element.193.weight_ref, bf16[192,3072]{1,0:T(8,128)(2,1)} %get-tuple-element.194.refs_0_, bf16[192,3072]{1,0:T(8,128)(2,1)S(1)} %get-tuple-element.195.refs_1_, bf16[192,3072]{1,0:T(8,128)(2,1)} %get-tuple-element.196.refs_2_, ...), custom_call_target="tpu_custom_call" | custom-call | flops 230400000 | bytes 499200 | tf_op jit(solution)/shard_map/cond/branch_6_fun/grad_att/pallas_call | solution.py:149
  65.8 12.1 %forward_home.14 = (bf16[1024,256]{1,0:T(8,128)(2,1)}, bf16[2,1024,1024]{2,1,0:T(8,128)(2,1)}) custom-call(s32[16]{0:T(128)S(1)} %get-tuple-element.189.meta_ref, bf16[1536,768]{1,0:T(8,128)(2,1)} %get-tuple-element.190.qkv_ref), custom_call_target="tpu_custom_call" | custom-call | flops 6000000000 | bytes 8000000 | tf_op jit(solution)/shard_map/cond/branch_6_fun/forward_home/pallas_call | solution.py:112
  78.4 7.6 %collective-permute-done.11.refs_4_ = bf16[224,3072]{1,0:T(8,128)(2,1)S(1)} collective-permute-done((bf16[224,3072]{1,0:T(8,128)(2,1)}, bf16[224,3072]{1,0:T(8,128)(2,1)S(1)}, u32[]{:S(2)}, u32[]{:S(2)}) %collective-permute-start.11) | collective-permute-done | bytes 1376288 | tf_op jit(solution)/shard_map/ppermute | solution.py:61
  88.4 1.7 %collective-permute-start.16 = (bf16[64,3072]{1,0:T(8,128)(2,1)S(1)}, bf16[64,3072]{1,0:T(8,128)(2,1)S(1)}, u32[]{:S(2)}, u32[]{:S(2)}) collective-permute-start(bf16[64,3072]{1,0:T(8,128)(2,1)S(1)} %slice.53), channel_id=1, source_target_pairs={{2,0},{3,1},{4,2},{5,3},{6,4},{7,5},{0,6},{1,7},{10,8},{11,9},{12,... | collective-permute-start | bytes 1179656 | tf_op jit(solution)/shard_map/ppermute | solution.py:61
  90.1 9.6 %middle.1 = (bf16[1536,256]{1,0:T(8,128)(2,1)S(1)}, bf16[2,512,512]{2,1,0:T(8,128)(2,1)S(1)}, bf16[576,256]{1,0:T(8,128)(2,1)S(1)}, f32[4,256,768]{2,1,0:T(8,128)S(1)}) custom-call(s32[16]{0:T(128)S(1)} %stack.51.meta_ref, bf16[512,768]{1,0:T(8,128)(2,1)} %get-tuple-element.235.move_ref, bf16[1024,256]{1,0:T(8,128)(2,1)} %get-tuple-element.236.home_att_ref, ...), custom_call_target="tpu_custom_call" | custom-call | flops 806400000 | bytes 1344000 | tf_op jit(solution)/shard_map/middle/pallas_call | solution.py:201
  99.8 10.0 %backward.1 = (bf16[1536,768]{1,0:T(8,128)(2,1)}, bf16[4,256,384]{2,1,0:T(8,128)(2,1)}, bf16[4,256,384]{2,1,0:T(8,128)(2,1)S(1)}) custom-call(s32[16]{0:T(128)S(1)} %stack.51.meta_ref, bf16[1536,768]{1,0:T(8,128)(2,1)} %bitcast.16.qkv_ref, bf16[512,768]{1,0:T(8,128)(2,1)} %get-tuple-element.235.move_ref, bf16[1536,256]{1,0:T(8,128)(2,1)S(1)} %get-tuple-element.240.att_ref, ...), custom_call_target="tpu_custom_call" | custom-call | flops 10000000000 | bytes 12000000 | tf_op jit(solution)/shard_map/backward/pallas_call | solution.py:330
  109.8 3.9 %all-to-all-start.1 = ((bf16[8,192,768]{2,1,0:T(8,128)(2,1)}), bf16[8,192,768]{2,1,0:T(8,128)(2,1)S(1)}, u32[]{:S(2)}, u32[]{:S(2)}) async-start(bf16[8,192,768]{2,1,0:T(8,128)(2,1)} %bitcast.32), calls=%async_computation.1 | async-start | bytes 4718592 | tf_op jit(solution)/shard_map/all_to_all | solution.py:470
  113.7 2.6 %collective-permute-done.17.got_ref = bf16[4,256,384]{2,1,0:T(8,128)(2,1)} collective-permute-done((bf16[4,256,384]{2,1,0:T(8,128)(2,1)}, bf16[4,256,384]{2,1,0:T(8,128)(2,1)}, u32[]{:S(2)}, u32[]{:S(2)}) %collective-permute-start.17) | collective-permute-done | bytes 786464 | tf_op jit(solution)/shard_map/ppermute | solution.py:381
  116.3 2.0 %both_cores.1 = (bf16[256,384]{1,0:T(8,128)(2,1)S(1)}, bf16[256,384]{1,0:T(8,128)(2,1)S(1)}, bf16[256,384]{1,0:T(8,128)(2,1)}, bf16[256,384]{1,0:T(8,128)(2,1)}) custom-call(s32[1]{0:T(128)} %bitcast.21.z_ref, bf16[4,256,384]{2,1,0:T(8,128)(2,1)S(1)} %get-tuple-element.250.keep_ref, bf16[4,256,384]{2,1,0:T(8,128)(2,1)} %collective-permute-done.17.got_ref), custom_call_target="tpu_custom_call" | custom-call | bytes 3000000 | tf_op jit(solution)/shard_map/both_cores/pallas_call | solution.py:367
  118.3 4.0 %collective-permute-start.20 = (bf16[256,384]{1,0:T(8,128)(2,1)}, bf16[256,384]{1,0:T(8,128)(2,1)S(1)}, u32[]{:S(2)}, u32[]{:S(2)}) collective-permute-start(bf16[256,384]{1,0:T(8,128)(2,1)} %get-tuple-element.255), channel_id=1, source_target_pairs={{32,0},{40,8},{48,16},{56,24},{64,32},{72,40},{80,48},{88,56},{96,... | collective-permute-start | bytes 589832 | tf_op jit(solution)/shard_map/ppermute | solution.py:61
  123.6 7.7 %collective-permute-done.20 = bf16[256,384]{1,0:T(8,128)(2,1)S(1)} collective-permute-done((bf16[256,384]{1,0:T(8,128)(2,1)}, bf16[256,384]{1,0:T(8,128)(2,1)S(1)}, u32[]{:S(2)}, u32[]{:S(2)}) %collective-permute-start.20) | collective-permute-done | bytes 196640 | tf_op jit(solution)/shard_map/ppermute | solution.py:61
  131.8 2.6 %collective-permute-done.18 = bf16[256,384]{1,0:T(8,128)(2,1)S(1)} collective-permute-done((bf16[256,384]{1,0:T(8,128)(2,1)S(1)}, bf16[256,384]{1,0:T(8,128)(2,1)S(1)}, u32[]{:S(2)}, u32[]{:S(2)}) %collective-permute-start.18) | collective-permute-done | bytes 196640 | tf_op jit(solution)/shard_map/ppermute | solution.py:61
  134.6 2.9 %collective-permute-start.21 = (bf16[256,192]{1,0:T(8,128)(2,1)S(1)}, bf16[256,192]{1,0:T(8,128)(2,1)S(1)}, u32[]{:S(2)}, u32[]{:S(2)}) collective-permute-start(bf16[256,192]{1,0:T(8,128)(2,1)S(1)} %select_convert_fusion), channel_id=1, source_target_pairs={{0,16},{8,24},{16,0},{24,8},{32,48},{40,56},{48,32},{56,40},{64,80... | collective-permute-start | bytes 294920 | tf_op jit(solution)/shard_map/ppermute | solution.py:388
  137.5 6.2 %collective-permute-done.21 = bf16[256,192]{1,0:T(8,128)(2,1)S(1)} collective-permute-done((bf16[256,192]{1,0:T(8,128)(2,1)S(1)}, bf16[256,192]{1,0:T(8,128)(2,1)S(1)}, u32[]{:S(2)}, u32[]{:S(2)}) %collective-permute-start.21) | collective-permute-done | bytes 98336 | tf_op jit(solution)/shard_map/ppermute | solution.py:388
  (73 shorter events, 23.4 us)
Async XLA Ops:
  0.6 29.2 %collective-permute-start.8 = (bf16[192,3072]{1,0:T(8,128)(2,1)}, bf16[192,3072]{1,0:T(8,128)(2,1)S(1)}, u32[]{:S(2)}, u32[]{:S(2)}) collective-permute-start(bf16[192,3072]{1,0:T(8,128)(2,1)} %refs_0_.1), channel_id=1, source_target_pairs={{0,1},{1,0},{2,3},{3,2},{4,5},{5,4},{6,7},{7,6},{8,9},{9,8},{10,11... | collective-permute-start | bytes 3538952 | tf_op jit(solution)/shard_map/ppermute | solution.py:65
  2.3 30.3 %collective-permute-start.9 = (bf16[192,3072]{1,0:T(8,128)(2,1)}, bf16[192,3072]{1,0:T(8,128)(2,1)S(1)}, u32[]{:S(2)}, u32[]{:S(2)}) collective-permute-start(bf16[192,3072]{1,0:T(8,128)(2,1)} %refs_0_.1), channel_id=1, source_target_pairs={{6,0},{7,1},{0,2},{1,3},{2,4},{3,5},{4,6},{5,7},{14,8},{15,9},{8,1... | collective-permute-start | bytes 3538952 | tf_op jit(solution)/shard_map/ppermute | solution.py:61
  3.9 31.4 %collective-permute-start.10 = (bf16[192,3072]{1,0:T(8,128)(2,1)}, bf16[192,3072]{1,0:T(8,128)(2,1)S(1)}, u32[]{:S(2)}, u32[]{:S(2)}) collective-permute-start(bf16[192,3072]{1,0:T(8,128)(2,1)} %refs_0_.1), channel_id=1, source_target_pairs={{2,0},{3,1},{4,2},{5,3},{6,4},{7,5},{0,6},{1,7},{10,8},{11,9},{12,... | collective-permute-start | bytes 3538952 | tf_op jit(solution)/shard_map/ppermute | solution.py:61
  10.4 48.8 %all-to-all-start = ((bf16[1,192,8,768]{3,1,0,2:T(8,128)(2,1)}), bf16[1,192,8,768]{3,1,0,2:T(8,128)(2,1)}, u32[]{:S(2)}, u32[]{:S(2)}) async-start(bf16[1,192,8,768]{3,1,0,2:T(8,128)(2,1)} %copy.17), calls=%async_computation | async-start | bytes 4718592 | tf_op jit(solution)/shard_map/all_to_all | solution.py:439
  34.9 51.1 %collective-permute-start.11 = (bf16[224,3072]{1,0:T(8,128)(2,1)}, bf16[224,3072]{1,0:T(8,128)(2,1)S(1)}, u32[]{:S(2)}, u32[]{:S(2)}) collective-permute-start(bf16[224,3072]{1,0:T(8,128)(2,1)} %pad_maximum_fusion), channel_id=1, source_target_pairs={{6,0},{7,1},{0,2},{1,3},{2,4},{3,5},{4,6},{5,7},{14,8},{15,9},{8,1... | collective-permute-start | bytes 4128776 | tf_op jit(solution)/shard_map/ppermute | solution.py:61
  36.4 9.5 %copy-start.10 = (s32[32]{0:T(128)S(1)}, s32[32]{0:T(128)}, u32[]{:S(2)}) copy-start(s32[32]{0:T(128)} %param.22) | copy-start | bytes 388
  37.6 10.2 %copy-start.11 = (s32[32]{0:T(128)S(1)}, s32[32]{0:T(128)}, u32[]{:S(2)}) copy-start(s32[32]{0:T(128)} %param.23) | copy-start | bytes 388
  37.6 10.3 %copy-start.12 = (s32[32]{0:T(128)S(1)}, s32[32]{0:T(128)}, u32[]{:S(2)}) copy-start(s32[32]{0:T(128)} %param.21) | copy-start | bytes 388
  37.6 48.6 %collective-permute-start.12 = (bf16[224,3072]{1,0:T(8,128)(2,1)}, bf16[224,3072]{1,0:T(8,128)(2,1)S(1)}, u32[]{:S(2)}, u32[]{:S(2)}) collective-permute-start(bf16[224,3072]{1,0:T(8,128)(2,1)} %pad_maximum_fusion.1), channel_id=1, source_target_pairs={{2,0},{3,1},{4,2},{5,3},{6,4},{7,5},{0,6},{1,7},{10,8},{11,9},{12,... | collective-permute-start | bytes 4128776 | tf_op jit(solution)/shard_map/ppermute | solution.py:61
  41.4 37.0 %collective-permute-start.13 = (bf16[128,3072]{1,0:T(8,128)(2,1)}, bf16[128,3072]{1,0:T(8,128)(2,1)S(1)}, u32[]{:S(2)}, u32[]{:S(2)}) collective-permute-start(bf16[128,3072]{1,0:T(8,128)(2,1)} %pad_maximum_fusion.2), channel_id=1, source_target_pairs={{0,1},{1,0},{2,3},{3,2},{4,5},{5,4},{6,7},{7,6},{8,9},{9,8},{10,11... | collective-permute-start | bytes 2359304 | tf_op jit(solution)/shard_map/ppermute | solution.py:65
  61.2 17.2 %collective-permute-start.6 = (bf16[512,768]{1,0:T(8,128)(2,1)S(1)}, bf16[512,768]{1,0:T(8,128)(2,1)}, u32[]{:S(2)}, u32[]{:S(2)}) collective-permute-start(bf16[512,768]{1,0:T(8,128)(2,1)S(1)} %get-tuple-element.188), channel_id=1, source_target_pairs={{72,0},{80,8},{88,16},{96,24},{104,32},{112,40},{120,48},{0,56},{8... | collective-permute-start | bytes 2359304 | tf_op jit(solution)/shard_map/cond/branch_6_fun/ppermute | solution.py:61
  78.4 11.7 %copy-start.1 = (bf16[256,3072]{1,0:T(8,128)(2,1)S(1)}, bf16[256,3072]{1,0:T(8,128)(2,1)}, u32[]{:S(2)}) copy-start(bf16[256,3072]{1,0:T(8,128)(2,1)} %weight_ref.3) | copy-start | bytes 4718596
  78.4 11.7 %copy-start.4 = (bf16[192,3072]{1,0:T(8,128)(2,1)S(1)}, bf16[192,3072]{1,0:T(8,128)(2,1)}, u32[]{:S(2)}) copy-start(bf16[192,3072]{1,0:T(8,128)(2,1)} %copy-done.2) | copy-start | bytes 3538948
  86.4 13.4 %collective-permute-start.14 = (bf16[64,3072]{1,0:T(8,128)(2,1)S(1)}, bf16[64,3072]{1,0:T(8,128)(2,1)S(1)}, u32[]{:S(2)}, u32[]{:S(2)}) collective-permute-start(bf16[64,3072]{1,0:T(8,128)(2,1)S(1)} %slice.50), channel_id=1, source_target_pairs={{6,0},{7,1},{0,2},{1,3},{2,4},{3,5},{4,6},{5,7},{14,8},{15,9},{8,1... | collective-permute-start | bytes 1179656 | tf_op jit(solution)/shard_map/ppermute | solution.py:61
  87.8 11.9 %collective-permute-start.15 = (bf16[64,3072]{1,0:T(8,128)(2,1)S(1)}, bf16[64,3072]{1,0:T(8,128)(2,1)S(1)}, u32[]{:S(2)}, u32[]{:S(2)}) collective-permute-start(bf16[64,3072]{1,0:T(8,128)(2,1)S(1)} %pad_maximum_fusion.3), channel_id=1, source_target_pairs={{0,1},{1,0},{2,3},{3,2},{4,5},{5,4},{6,7},{7,6},{8,9},{9,8},{10,11... | collective-permute-start | bytes 1179656 | tf_op jit(solution)/shard_map/ppermute | solution.py:65
  88.4 11.3 %collective-permute-start.16 = (bf16[64,3072]{1,0:T(8,128)(2,1)S(1)}, bf16[64,3072]{1,0:T(8,128)(2,1)S(1)}, u32[]{:S(2)}, u32[]{:S(2)}) collective-permute-start(bf16[64,3072]{1,0:T(8,128)(2,1)S(1)} %slice.53), channel_id=1, source_target_pairs={{2,0},{3,1},{4,2},{5,3},{6,4},{7,5},{0,6},{1,7},{10,8},{11,9},{12,... | collective-permute-start | bytes 1179656 | tf_op jit(solution)/shard_map/ppermute | solution.py:61
  90.1 9.7 %copy-start.9 = (bf16[768,256]{1,0:T(8,128)(2,1)S(1)}, bf16[768,256]{1,0:T(8,128)(2,1)}, u32[]{:S(2)}) copy-start(bf16[768,256]{1,0:T(8,128)(2,1)} %copy-done.8) | copy-start | bytes 1179652
  90.1 9.7 %copy-start.13 = (bf16[2,1024,1024]{2,1,0:T(8,128)(2,1)S(1)}, bf16[2,1024,1024]{2,1,0:T(8,128)(2,1)}, u32[]{:S(2)}) copy-start(bf16[2,1024,1024]{2,1,0:T(8,128)(2,1)} %get-tuple-element.241.home_prob_ref) | copy-start | bytes 12582916
  109.8 34.9 %all-to-all-start.1 = ((bf16[8,192,768]{2,1,0:T(8,128)(2,1)}), bf16[8,192,768]{2,1,0:T(8,128)(2,1)S(1)}, u32[]{:S(2)}, u32[]{:S(2)}) async-start(bf16[8,192,768]{2,1,0:T(8,128)(2,1)} %bitcast.32), calls=%async_computation.1 | async-start | bytes 4718592 | tf_op jit(solution)/shard_map/all_to_all | solution.py:470
  113.7 2.6 %collective-permute-start.17 = (bf16[4,256,384]{2,1,0:T(8,128)(2,1)}, bf16[4,256,384]{2,1,0:T(8,128)(2,1)}, u32[]{:S(2)}, u32[]{:S(2)}) collective-permute-start(bf16[4,256,384]{2,1,0:T(8,128)(2,1)} %get-tuple-element.251), channel_id=1, source_target_pairs={{0,8},{8,0},{16,24},{24,16},{32,40},{40,32},{48,56},{56,48},{64,72... | collective-permute-start | bytes 2359304 | tf_op jit(solution)/shard_map/ppermute | solution.py:381
  118.3 13.0 %collective-permute-start.20 = (bf16[256,384]{1,0:T(8,128)(2,1)}, bf16[256,384]{1,0:T(8,128)(2,1)S(1)}, u32[]{:S(2)}, u32[]{:S(2)}) collective-permute-start(bf16[256,384]{1,0:T(8,128)(2,1)} %get-tuple-element.255), channel_id=1, source_target_pairs={{32,0},{40,8},{48,16},{56,24},{64,32},{72,40},{80,48},{88,56},{96,... | collective-permute-start | bytes 589832 | tf_op jit(solution)/shard_map/ppermute | solution.py:61
  122.3 9.5 %collective-permute-start.19 = (bf16[256,384]{1,0:T(8,128)(2,1)}, bf16[256,384]{1,0:T(8,128)(2,1)S(1)}, u32[]{:S(2)}, u32[]{:S(2)}) collective-permute-start(bf16[256,384]{1,0:T(8,128)(2,1)} %get-tuple-element.254), channel_id=1, source_target_pairs={{64,0},{72,8},{80,16},{88,24},{96,32},{104,40},{112,48},{120,56},{... | collective-permute-start | bytes 589832 | tf_op jit(solution)/shard_map/ppermute | solution.py:61
  122.3 12.1 %collective-permute-start.18 = (bf16[256,384]{1,0:T(8,128)(2,1)S(1)}, bf16[256,384]{1,0:T(8,128)(2,1)S(1)}, u32[]{:S(2)}, u32[]{:S(2)}) collective-permute-start(bf16[256,384]{1,0:T(8,128)(2,1)S(1)} %get-tuple-element.253), channel_id=1, source_target_pairs={{96,0},{104,8},{112,16},{120,24},{0,32},{8,40},{16,48},{24,56},{32... | collective-permute-start | bytes 589832 | tf_op jit(solution)/shard_map/ppermute | solution.py:61
  134.6 9.1 %collective-permute-start.21 = (bf16[256,192]{1,0:T(8,128)(2,1)S(1)}, bf16[256,192]{1,0:T(8,128)(2,1)S(1)}, u32[]{:S(2)}, u32[]{:S(2)}) collective-permute-start(bf16[256,192]{1,0:T(8,128)(2,1)S(1)} %select_convert_fusion), channel_id=1, source_target_pairs={{0,16},{8,24},{16,0},{24,8},{32,48},{40,56},{48,32},{56,40},{64,80... | collective-permute-start | bytes 294920 | tf_op jit(solution)/shard_map/ppermute | solution.py:388
  (9 other events, 33.7 us)

commit v5 on v4

--- a/solution.py
+++ b/solution.py
@@ -18,7 +18,7 @@
 MOVE_MIN = 256
 FAR_PIECES = (96, 128, 96, 128, 64, 64)
 QB = 256
-BQ = 512
+BQ = 1024
 SCALE = HD ** (-0.5)
 EXP2_SCALE = SCALE * 1.4426950408889634
 NEG_BIG = -1e30
@@ -69,31 +69,31 @@
     return pl.ds(pl.multiple_of(which * FEAT + head * HD, HD), HD)
 
 
-def forward_clip(read, length, rows, sure, prob_ref, att_ref, att_first):
+def forward_clip(read, length, rows, sure, prob_ref, att_ref, att_first, step_rows):
     def one_head(head, _):
         k = read(1, head, 0, rows)
         v_t = flip(read(2, head, 0, rows))
 
         def block(step, _):
-            first = pl.multiple_of(step * QB, QB)
-            q = read(0, head, first, QB)
+            first = pl.multiple_of(step * step_rows, step_rows)
+            q = read(0, head, first, step_rows)
             scores = dot(k, q, NT)
-            key = lax.broadcasted_iota(jnp.int32, (rows - sure, QB), 0) + sure
+            key = lax.broadcasted_iota(jnp.int32, (rows - sure, step_rows), 0) + sure
             scores = jnp.concatenate(
                 [scores[:sure], jnp.where(key < length, scores[sure:], NEG_BIG)], axis=0
             )
             peak = jnp.max(scores, axis=0, keepdims=True)
             unnorm = jnp.exp2((scores - peak) * EXP2_SCALE)
             total = jnp.sum(unnorm, axis=0, keepdims=True)
-            query = lax.broadcasted_iota(jnp.int32, (1, QB), 1) + first
+            query = lax.broadcasted_iota(jnp.int32, (1, step_rows), 1) + first
             prob = (unnorm * jnp.where(query < length, 1.0 / total, 0.0)).astype(jnp.bfloat16)
-            prob_ref[head, :, pl.ds(first, QB)] = prob
+            prob_ref[head, :, pl.ds(first, step_rows)] = prob
             att = dot(v_t, prob).T.astype(jnp.bfloat16)
-            there = pl.ds(pl.multiple_of(att_first + first, 128), QB)
+            there = pl.ds(pl.multiple_of(att_first + first, 128), step_rows)
             att_ref[there, columns(0, head)] = att
             return 0
 
-        return lax.fori_loop(0, rows // QB, block, 0)
+        return lax.fori_loop(0, rows // step_rows, block, 0)
 
     lax.fori_loop(0, 2, one_head, 0)
 
@@ -105,7 +105,7 @@
         start = pl.multiple_of(home_first + first, 128)
         return qkv_ref[pl.ds(start, count), columns(which, head)]
 
-    forward_clip(read, home_len, HOME, HOME_MIN, prob_ref, att_ref, 0)
+    forward_clip(read, home_len, HOME, HOME_MIN, prob_ref, att_ref, 0, QB)
 
 
 def forward_home(meta, qkv):
@@ -176,7 +176,7 @@
     def _():
         att_ref[:HOME, :] = home_att_ref[...]
         att_ref[HOME:, :] = jnp.zeros((GROUP - HOME, FEAT), jnp.bfloat16)
-        forward_clip(read, meta_ref[2], MOVE, MOVE_MIN, prob_ref, att_ref, meta_ref[1])
+        forward_clip(read, meta_ref[2], MOVE, MOVE_MIN, prob_ref, att_ref, meta_ref[1], MOVE)
         picked = [
             att_ref[pl.ds(pl.multiple_of(meta_ref[4 + i], 32), count), :]
             for i, count in enumerate(pieces)
@@ -233,18 +233,19 @@
 
 
 def backward_clip(read, rows, prob_ref, row_first, ga_ref, att_ref, out_ref, key_acc, value_acc):
+    block_rows = min(rows, BQ)
     k_t = [flip(read(1, head, 0, rows)) for head in range(2)]
     key_acc[:rows, :] = jnp.zeros((rows, FEAT), jnp.float32)
     value_acc[:rows, :] = jnp.zeros((rows, FEAT), jnp.float32)
 
     def block(step, _):
-        first = pl.multiple_of(step * BQ, BQ)
-        there = pl.ds(pl.multiple_of(row_first + first, 128), BQ)
+        first = pl.multiple_of(step * block_rows, block_rows)
+        there = pl.ds(pl.multiple_of(row_first + first, 128), block_rows)
         for head in range(2):
             side = slice(head * HD, (head + 1) * HD)
-            q = read(0, head, first, BQ)
+            q = read(0, head, first, block_rows)
             v = read(2, head, 0, rows)
-            prob = prob_ref[head, :, pl.ds(first, BQ)]
+            prob = prob_ref[head, :, pl.ds(first, block_rows)]
             grad_att = ga_ref[there, side]
             product = grad_att.astype(jnp.float32) * att_ref[there, side].astype(jnp.float32)
             row_dot = jnp.sum(product.T, axis=0, keepdims=True)
@@ -256,7 +257,7 @@
             out_ref[there, side] = grad_query
         return 0
 
-    lax.fori_loop(0, rows // BQ, block, 0)
+    lax.fori_loop(0, rows // block_rows, block, 0)
     whole = pl.ds(pl.multiple_of(row_first, 128), rows)
     out_ref[whole, FEAT : 2 * FEAT] = (key_acc[:rows, :] * SCALE).astype(jnp.bfloat16)
     out_ref[whole, 2 * FEAT :] = value_acc[:rows, :].astype(jnp.bfloat16)
@@ -360,13 +361,13 @@
     for distance, out in enumerate(outs):
         at = lax.rem(z_ref[0] + distance, 4)
         both = keep_ref[at].astype(jnp.float32) + got_ref[at].astype(jnp.float32)
-        out[...] = both.astype(jnp.bfloat16)
+        out[...] = both.T.astype(jnp.bfloat16)
 
 
 def both_cores(z, keep, got):
     return pl.pallas_call(
         both_cores_kernel,
-        out_shape=(jax.ShapeDtypeStruct((FEAT, D // 8), jnp.bfloat16),) * 4,
+        out_shape=(jax.ShapeDtypeStruct((D // 8, FEAT), jnp.bfloat16),) * 4,
         in_specs=[SMEM, VMEM, VMEM],
         out_specs=(VMEM,) * 4,
         compiler_params=PARAMS,
@@ -383,10 +384,10 @@
     total = mine.astype(jnp.float32)
     for distance, sent in enumerate(rest, 1):
         total = total + shifted(sent, "dp", 4 * distance).astype(jnp.float32)
-    low, high = total[:, : D // 16], total[:, D // 16 :]
+    low, high = total[: D // 16], total[D // 16 :]
     sent = jnp.where(xh == 0, high, low).astype(jnp.bfloat16)
     got = lax.ppermute(sent, "dp", [(i, i ^ 2) for i in range(16)])
-    return jnp.where(xh == 0, low, high) + got.astype(jnp.float32)
+    return (jnp.where(xh == 0, low, high) + got.astype(jnp.float32)).T
 
 
 def arriving(distance, outgoing, qkv, meta, weight, *blocks):

time: 147 us -> 144 us (0.980)
  waiting for transfers between devices: 52.3 us -> 46.9 us
  starting transfers between devices: 33.3 us -> 37.1 us
  Pallas kernels: 39.3 us -> 37.7 us
    ppermute x10, starting transfers between devices: 15.3 us -> 18.8 us  [shifted(): return lax.ppermute(x, axis, [((i - distance) % n, i) for i in range(n)])]
    ppermute x10, waiting for transfers between devices: 21.8 us -> 18.4 us  [shifted(): return lax.ppermute(x, axis, [((i - distance) % n, i) for i in range(n)])]
    unnamed x32 -> x31, local copies, waits for them, and re-layouts: 6.18 us -> 5.37 us
  transfers between devices with their start and end apart: 17 -> 17, of which waited for: 11 -> 10; matrix products, arithmetic and copies ran while one was open for 10% -> 10% of each run, Pallas kernels for 19% -> 19%
where the time goes in v5:
time: 144 us; the launch traced here: 143 us
  waiting for transfers between devices  46.9 us (33%)
  Pallas kernels  37.7 us (26%)
  starting transfers between devices  37.1 us (26%)
  local copies, waits for them, and re-layouts  13.1 us (9%)
  other arithmetic  4.4 us (3%)
  between operations  4.28 us (3%)
    ppermute x10, starting transfers between devices, shifted(): return lax.ppermute(x, axis, [((i - distance) % n, i) for i in range(n)])  18.8 us
    ppermute x10, waiting for transfers between devices, shifted(): return lax.ppermute(x, axis, [((i - distance) % n, i) for i in range(n)])  18.4 us
    ppermute x3, waiting for transfers between devices, swapped(): return lax.ppermute(x, 'head', [(i, i ^ 1) for i in range(8)])  15 us
    pallas_call x1, Pallas kernels, forward_home(): pl.pallas_call(forward_home_kernel, out_shape=(jax.ShapeDtypeStruct((HOME...  12.1 us
    pallas_call x1, Pallas kernels, backward(): pl.pallas_call(backward_kernel, out_shape=(pltpu.HBM((GROUP, 3 * FEAT), j...  9.42 us
    pallas_call x1, Pallas kernels, middle(): pl.pallas_call(functools.partial(middle_kernel, pieces, len(far)), grid=(...  8.39 us
    ppermute x3, starting transfers between devices, swapped(): return lax.ppermute(x, 'head', [(i, i ^ 1) for i in range(8)])  6.74 us
    all_to_all x1, waiting for transfers between devices, local(): lax.all_to_all(packed, 'head', split_axis=1, concat_axis=0, tiled=False)  5.85 us
  transfers between devices with their start and end apart: 17, of which 10 were waited for; matrix products, arithmetic and copies ran while one was open for 10% of the time, Pallas kernels for 19%

profile of v5, /device:TPU:0, one launch (start us, length us, event | category | flops | bytes accessed | tf_op | source)
XLA Modules:
  0.0 143.5 jit_solution(14356508995862345930)
XLA Ops:
  8.6 1.9 %copy.15 = bf16[1,192,8,768]{3,1,0,2:T(8,128)(2,1)} copy(bf16[1,192,8,768]{3,2,1,0:T(8,128)(2,1)S(1)} %maximum_bitcast_fusion) | data formatting | bytes 4718592 | tf_op jit(solution)/shard_map/broadcast_in_dim | solution.py:440
  10.4 4.4 %all-to-all-start = ((bf16[1,192,8,768]{3,1,0,2:T(8,128)(2,1)}), bf16[1,192,8,768]{3,1,0,2:T(8,128)(2,1)}, u32[]{:S(2)}, u32[]{:S(2)}) async-start(bf16[1,192,8,768]{3,1,0,2:T(8,128)(2,1)} %copy.15), calls=%async_computation | async-start | bytes 4718592 | tf_op jit(solution)/shard_map/all_to_all | solution.py:440
  14.8 15.0 %collective-permute-done.8.refs_1_ = bf16[192,3072]{1,0:T(8,128)(2,1)S(1)} collective-permute-done((bf16[192,3072]{1,0:T(8,128)(2,1)}, bf16[192,3072]{1,0:T(8,128)(2,1)S(1)}, u32[]{:S(2)}, u32[]{:S(2)}) %collective-permute-start.8) | collective-permute-done | bytes 1179680 | tf_op jit(solution)/shard_map/ppermute | solution.py:65
  30.0 2.6 %collective-permute-done.9.refs_2_ = bf16[192,3072]{1,0:T(8,128)(2,1)S(1)} collective-permute-done((bf16[192,3072]{1,0:T(8,128)(2,1)}, bf16[192,3072]{1,0:T(8,128)(2,1)S(1)}, u32[]{:S(2)}, u32[]{:S(2)}) %collective-permute-start.9) | collective-permute-done | bytes 1179680 | tf_op jit(solution)/shard_map/ppermute | solution.py:61
  37.6 2.9 %collective-permute-start.12 = (bf16[224,3072]{1,0:T(8,128)(2,1)}, bf16[224,3072]{1,0:T(8,128)(2,1)S(1)}, u32[]{:S(2)}, u32[]{:S(2)}) collective-permute-start(bf16[224,3072]{1,0:T(8,128)(2,1)} %pad_maximum_fusion.1), channel_id=1, source_target_pairs={{2,0},{3,1},{4,2},{5,3},{6,4},{7,5},{0,6},{1,7},{10,8},{11,9},{12,... | collective-permute-start | bytes 4128776 | tf_op jit(solution)/shard_map/ppermute | solution.py:61
  42.4 4.5 %collective-permute-start.13 = (bf16[128,3072]{1,0:T(8,128)(2,1)}, bf16[128,3072]{1,0:T(8,128)(2,1)S(1)}, u32[]{:S(2)}, u32[]{:S(2)}) collective-permute-start(bf16[128,3072]{1,0:T(8,128)(2,1)} %pad_maximum_fusion.2), channel_id=1, source_target_pairs={{0,1},{1,0},{2,3},{3,2},{4,5},{5,4},{6,7},{7,6},{8,9},{9,8},{10,11... | collective-permute-start | bytes 2359304 | tf_op jit(solution)/shard_map/ppermute | solution.py:65
  51.4 1.9 %stack.51.meta_ref = s32[16]{0:T(128)S(1)} concatenate(s32[1]{0:T(128)} %get-tuple-element.259, s32[1]{0:T(128)} %get-tuple-element.264, s32[1]{0:T(128)} %get-tuple-element.265, s32[1]{0:T(128)} %constant.98.clone.1, s32[1]{0:T(128)} %bitcast.1, s32[1]{0:T(128)} %bitcast.2, s32[1]{0:T(128)} %bitcast.3, s32[1]{0:T(128)} %bitcast.4, s32[1]{0:T(128)} %bitcast.5, s32[1]{0:T(128)} %bitcast.6, ...), dimensions={0} | concatenate | bytes 128 | tf_op jit(solution)/shard_map/stack | solution.py:412
  53.4 5.8 %all-to-all-done = bf16[1,192,8,768]{3,1,0,2:T(8,128)(2,1)} async-done(((bf16[1,192,8,768]{3,1,0,2:T(8,128)(2,1)}), bf16[1,192,8,768]{3,1,0,2:T(8,128)(2,1)}, u32[]{:S(2)}, u32[]{:S(2)}) %all-to-all-start) | async-done | bytes 2359328 | tf_op jit(solution)/shard_map/all_to_all | solution.py:440
  61.1 20.2 %conditional.1 = (bf16[512,768]{1,0:T(8,128)(2,1)}, bf16[1024,256]{1,0:T(8,128)(2,1)}, bf16[2,1024,1024]{2,1,0:T(8,128)(2,1)}, bf16[768,256]{1,0:T(8,128)(2,1)S(1)}) conditional(s32[]{:T(128)} %clamp.3, (bf16[512,768]{1,0:T(8,128)(2,1)S(1)}, s32[16]{0:T(128)S(1)}, bf16[1536,768]{1,0:T(8,128)(2,1)}, ...), branch_computations={%region_0.1_spmd, %region_1.2_spmd, %region_2.3_spmd, %region_3.4_... | conditional | flops 6230400000 | bytes 11645000 | solution.py:450
  61.1 4.0 %collective-permute-start.7 = (bf16[512,768]{1,0:T(8,128)(2,1)S(1)}, bf16[512,768]{1,0:T(8,128)(2,1)}, u32[]{:S(2)}, u32[]{:S(2)}) collective-permute-start(bf16[512,768]{1,0:T(8,128)(2,1)S(1)} %get-tuple-element.198), channel_id=1, source_target_pairs={{64,0},{72,8},{80,16},{88,24},{96,32},{104,40},{112,48},{120,56},{... | collective-permute-start | bytes 2359304 | tf_op jit(solution)/shard_map/cond/branch_7_fun/ppermute | solution.py:61
  65.1 4.1 %grad_att.15 = bf16[768,256]{1,0:T(8,128)(2,1)S(1)} custom-call(bf16[256,3072]{1,0:T(8,128)(2,1)S(1)} %get-tuple-element.203.weight_ref, bf16[192,3072]{1,0:T(8,128)(2,1)} %get-tuple-element.204.refs_0_, bf16[192,3072]{1,0:T(8,128)(2,1)S(1)} %get-tuple-element.205.refs_1_, bf16[192,3072]{1,0:T(8,128)(2,1)} %get-tuple-element.206.refs_2_, ...), custom_call_target="tpu_custom_call" | custom-call | flops 230400000 | bytes 499200 | tf_op jit(solution)/shard_map/cond/branch_7_fun/grad_att/pallas_call | solution.py:149
  69.2 12.1 %forward_home.15 = (bf16[1024,256]{1,0:T(8,128)(2,1)}, bf16[2,1024,1024]{2,1,0:T(8,128)(2,1)}) custom-call(s32[16]{0:T(128)S(1)} %get-tuple-element.199.meta_ref, bf16[1536,768]{1,0:T(8,128)(2,1)} %get-tuple-element.200.qkv_ref), custom_call_target="tpu_custom_call" | custom-call | flops 6000000000 | bytes 8000000 | tf_op jit(solution)/shard_map/cond/branch_7_fun/forward_home/pallas_call | solution.py:112
  81.3 4.7 %collective-permute-done.11.refs_4_ = bf16[224,3072]{1,0:T(8,128)(2,1)S(1)} collective-permute-done((bf16[224,3072]{1,0:T(8,128)(2,1)}, bf16[224,3072]{1,0:T(8,128)(2,1)S(1)}, u32[]{:S(2)}, u32[]{:S(2)}) %collective-permute-start.11) | collective-permute-done | bytes 1376288 | tf_op jit(solution)/shard_map/ppermute | solution.py:61
  88.4 1.7 %collective-permute-start.16 = (bf16[64,3072]{1,0:T(8,128)(2,1)S(1)}, bf16[64,3072]{1,0:T(8,128)(2,1)S(1)}, u32[]{:S(2)}, u32[]{:S(2)}) collective-permute-start(bf16[64,3072]{1,0:T(8,128)(2,1)S(1)} %slice.53), channel_id=1, source_target_pairs={{2,0},{3,1},{4,2},{5,3},{6,4},{7,5},{0,6},{1,7},{10,8},{11,9},{12,... | collective-permute-start | bytes 1179656 | tf_op jit(solution)/shard_map/ppermute | solution.py:61
  90.1 8.4 %middle.1 = (bf16[1536,256]{1,0:T(8,128)(2,1)S(1)}, bf16[2,512,512]{2,1,0:T(8,128)(2,1)S(1)}, bf16[576,256]{1,0:T(8,128)(2,1)S(1)}, f32[4,256,768]{2,1,0:T(8,128)S(1)}) custom-call(s32[16]{0:T(128)S(1)} %stack.51.meta_ref, bf16[512,768]{1,0:T(8,128)(2,1)} %get-tuple-element.235.move_ref, bf16[1024,256]{1,0:T(8,128)(2,1)} %get-tuple-element.236.home_att_ref, ...), custom_call_target="tpu_custom_call" | custom-call | flops 806400000 | bytes 1344000 | tf_op jit(solution)/shard_map/middle/pallas_call | solution.py:201
  98.5 9.4 %backward.1 = (bf16[1536,768]{1,0:T(8,128)(2,1)}, bf16[4,256,384]{2,1,0:T(8,128)(2,1)}, bf16[4,256,384]{2,1,0:T(8,128)(2,1)S(1)}) custom-call(s32[16]{0:T(128)S(1)} %stack.51.meta_ref, bf16[1536,768]{1,0:T(8,128)(2,1)} %bitcast.16.qkv_ref, bf16[512,768]{1,0:T(8,128)(2,1)} %get-tuple-element.235.move_ref, bf16[1536,256]{1,0:T(8,128)(2,1)S(1)} %get-tuple-element.240.att_ref, ...), custom_call_target="tpu_custom_call" | custom-call | flops 10000000000 | bytes 12000000 | tf_op jit(solution)/shard_map/backward/pallas_call | solution.py:331
  108.0 4.4 %all-to-all-start.1 = ((bf16[8,192,768]{2,1,0:T(8,128)(2,1)}), bf16[8,192,768]{2,1,0:T(8,128)(2,1)S(1)}, u32[]{:S(2)}, u32[]{:S(2)}) async-start(bf16[8,192,768]{2,1,0:T(8,128)(2,1)} %bitcast.34), calls=%async_computation.1 | async-start | bytes 4718592 | tf_op jit(solution)/shard_map/all_to_all | solution.py:471
  112.4 2.6 %collective-permute-done.17.got_ref = bf16[4,256,384]{2,1,0:T(8,128)(2,1)} collective-permute-done((bf16[4,256,384]{2,1,0:T(8,128)(2,1)}, bf16[4,256,384]{2,1,0:T(8,128)(2,1)}, u32[]{:S(2)}, u32[]{:S(2)}) %collective-permute-start.17) | collective-permute-done | bytes 786464 | tf_op jit(solution)/shard_map/ppermute | solution.py:382
  115.0 2.1 %both_cores.1 = (bf16[384,256]{1,0:T(8,128)(2,1)S(1)}, bf16[384,256]{1,0:T(8,128)(2,1)S(1)}, bf16[384,256]{1,0:T(8,128)(2,1)}, bf16[384,256]{1,0:T(8,128)(2,1)}) custom-call(s32[1]{0:T(128)} %bitcast.21.z_ref, bf16[4,256,384]{2,1,0:T(8,128)(2,1)S(1)} %get-tuple-element.250.keep_ref, bf16[4,256,384]{2,1,0:T(8,128)(2,1)} %collective-permute-done.17.got_ref), custom_call_target="tpu_custom_call" | custom-call | bytes 3000000 | tf_op jit(solution)/shard_map/both_cores/pallas_call | solution.py:368
  117.1 4.0 %collective-permute-start.20 = (bf16[384,256]{1,0:T(8,128)(2,1)}, bf16[384,256]{1,0:T(8,128)(2,1)S(1)}, u32[]{:S(2)}, u32[]{:S(2)}) collective-permute-start(bf16[384,256]{1,0:T(8,128)(2,1)} %get-tuple-element.255), channel_id=1, source_target_pairs={{32,0},{40,8},{48,16},{56,24},{64,32},{72,40},{80,48},{88,56},{96,... | collective-permute-start | bytes 589832 | tf_op jit(solution)/shard_map/ppermute | solution.py:61
  122.4 7.7 %collective-permute-done.20 = bf16[384,256]{1,0:T(8,128)(2,1)S(1)} collective-permute-done((bf16[384,256]{1,0:T(8,128)(2,1)}, bf16[384,256]{1,0:T(8,128)(2,1)S(1)}, u32[]{:S(2)}, u32[]{:S(2)}) %collective-permute-start.20) | collective-permute-done | bytes 196640 | tf_op jit(solution)/shard_map/ppermute | solution.py:61
  130.7 2.6 %collective-permute-done.18 = bf16[384,256]{1,0:T(8,128)(2,1)S(1)} collective-permute-done((bf16[384,256]{1,0:T(8,128)(2,1)S(1)}, bf16[384,256]{1,0:T(8,128)(2,1)S(1)}, u32[]{:S(2)}, u32[]{:S(2)}) %collective-permute-start.18) | collective-permute-done | bytes 196640 | tf_op jit(solution)/shard_map/ppermute | solution.py:61
  133.4 2.8 %collective-permute-start.21 = (bf16[192,256]{1,0:T(8,128)(2,1)S(1)}, bf16[192,256]{1,0:T(8,128)(2,1)S(1)}, u32[]{:S(2)}, u32[]{:S(2)}) collective-permute-start(bf16[192,256]{1,0:T(8,128)(2,1)S(1)} %select_convert_fusion), channel_id=1, source_target_pairs={{0,16},{8,24},{16,0},{24,8},{32,48},{40,56},{48,32},{56,40},{64,80... | collective-permute-start | bytes 294920 | tf_op jit(solution)/shard_map/ppermute | solution.py:389
  136.2 5.0 %collective-permute-done.21 = bf16[192,256]{1,0:T(8,128)(2,1)S(1)} collective-permute-done((bf16[192,256]{1,0:T(8,128)(2,1)S(1)}, bf16[192,256]{1,0:T(8,128)(2,1)S(1)}, u32[]{:S(2)}, u32[]{:S(2)}) %collective-permute-start.21) | collective-permute-done | bytes 98336 | tf_op jit(solution)/shard_map/ppermute | solution.py:389
  (71 shorter events, 24.5 us)
Async XLA Ops:
  0.6 29.2 %collective-permute-start.8 = (bf16[192,3072]{1,0:T(8,128)(2,1)}, bf16[192,3072]{1,0:T(8,128)(2,1)S(1)}, u32[]{:S(2)}, u32[]{:S(2)}) collective-permute-start(bf16[192,3072]{1,0:T(8,128)(2,1)} %refs_0_.1), channel_id=1, source_target_pairs={{0,1},{1,0},{2,3},{3,2},{4,5},{5,4},{6,7},{7,6},{8,9},{9,8},{10,11... | collective-permute-start | bytes 3538952 | tf_op jit(solution)/shard_map/ppermute | solution.py:65
  2.3 30.3 %collective-permute-start.9 = (bf16[192,3072]{1,0:T(8,128)(2,1)}, bf16[192,3072]{1,0:T(8,128)(2,1)S(1)}, u32[]{:S(2)}, u32[]{:S(2)}) collective-permute-start(bf16[192,3072]{1,0:T(8,128)(2,1)} %refs_0_.1), channel_id=1, source_target_pairs={{6,0},{7,1},{0,2},{1,3},{2,4},{3,5},{4,6},{5,7},{14,8},{15,9},{8,1... | collective-permute-start | bytes 3538952 | tf_op jit(solution)/shard_map/ppermute | solution.py:61
  3.9 31.4 %collective-permute-start.10 = (bf16[192,3072]{1,0:T(8,128)(2,1)}, bf16[192,3072]{1,0:T(8,128)(2,1)S(1)}, u32[]{:S(2)}, u32[]{:S(2)}) collective-permute-start(bf16[192,3072]{1,0:T(8,128)(2,1)} %refs_0_.1), channel_id=1, source_target_pairs={{2,0},{3,1},{4,2},{5,3},{6,4},{7,5},{0,6},{1,7},{10,8},{11,9},{12,... | collective-permute-start | bytes 3538952 | tf_op jit(solution)/shard_map/ppermute | solution.py:61
  10.4 48.8 %all-to-all-start = ((bf16[1,192,8,768]{3,1,0,2:T(8,128)(2,1)}), bf16[1,192,8,768]{3,1,0,2:T(8,128)(2,1)}, u32[]{:S(2)}, u32[]{:S(2)}) async-start(bf16[1,192,8,768]{3,1,0,2:T(8,128)(2,1)} %copy.15), calls=%async_computation | async-start | bytes 4718592 | tf_op jit(solution)/shard_map/all_to_all | solution.py:440
  34.9 51.1 %collective-permute-start.11 = (bf16[224,3072]{1,0:T(8,128)(2,1)}, bf16[224,3072]{1,0:T(8,128)(2,1)S(1)}, u32[]{:S(2)}, u32[]{:S(2)}) collective-permute-start(bf16[224,3072]{1,0:T(8,128)(2,1)} %pad_maximum_fusion), channel_id=1, source_target_pairs={{6,0},{7,1},{0,2},{1,3},{2,4},{3,5},{4,6},{5,7},{14,8},{15,9},{8,1... | collective-permute-start | bytes 4128776 | tf_op jit(solution)/shard_map/ppermute | solution.py:61
  36.4 10.5 %copy-start.10 = (s32[32]{0:T(128)S(1)}, s32[32]{0:T(128)}, u32[]{:S(2)}) copy-start(s32[32]{0:T(128)} %param.22) | copy-start | bytes 388
  37.6 11.3 %copy-start.11 = (s32[32]{0:T(128)S(1)}, s32[32]{0:T(128)}, u32[]{:S(2)}) copy-start(s32[32]{0:T(128)} %param.23) | copy-start | bytes 388
  37.6 11.3 %copy-start.12 = (s32[32]{0:T(128)S(1)}, s32[32]{0:T(128)}, u32[]{:S(2)}) copy-start(s32[32]{0:T(128)} %param.21) | copy-start | bytes 388
  37.6 48.7 %collective-permute-start.12 = (bf16[224,3072]{1,0:T(8,128)(2,1)}, bf16[224,3072]{1,0:T(8,128)(2,1)S(1)}, u32[]{:S(2)}, u32[]{:S(2)}) collective-permute-start(bf16[224,3072]{1,0:T(8,128)(2,1)} %pad_maximum_fusion.1), channel_id=1, source_target_pairs={{2,0},{3,1},{4,2},{5,3},{6,4},{7,5},{0,6},{1,7},{10,8},{11,9},{12,... | collective-permute-start | bytes 4128776 | tf_op jit(solution)/shard_map/ppermute | solution.py:61
  42.4 38.9 %collective-permute-start.13 = (bf16[128,3072]{1,0:T(8,128)(2,1)}, bf16[128,3072]{1,0:T(8,128)(2,1)S(1)}, u32[]{:S(2)}, u32[]{:S(2)}) collective-permute-start(bf16[128,3072]{1,0:T(8,128)(2,1)} %pad_maximum_fusion.2), channel_id=1, source_target_pairs={{0,1},{1,0},{2,3},{3,2},{4,5},{5,4},{6,7},{7,6},{8,9},{9,8},{10,11... | collective-permute-start | bytes 2359304 | tf_op jit(solution)/shard_map/ppermute | solution.py:65
  61.1 20.2 %collective-permute-start.7 = (bf16[512,768]{1,0:T(8,128)(2,1)S(1)}, bf16[512,768]{1,0:T(8,128)(2,1)}, u32[]{:S(2)}, u32[]{:S(2)}) collective-permute-start(bf16[512,768]{1,0:T(8,128)(2,1)S(1)} %get-tuple-element.198), channel_id=1, source_target_pairs={{64,0},{72,8},{80,16},{88,24},{96,32},{104,40},{112,48},{120,56},{... | collective-permute-start | bytes 2359304 | tf_op jit(solution)/shard_map/cond/branch_7_fun/ppermute | solution.py:61
  81.3 8.8 %copy-start.1 = (bf16[256,3072]{1,0:T(8,128)(2,1)S(1)}, bf16[256,3072]{1,0:T(8,128)(2,1)}, u32[]{:S(2)}) copy-start(bf16[256,3072]{1,0:T(8,128)(2,1)} %weight_ref.3) | copy-start | bytes 4718596
  81.3 8.8 %copy-start.4 = (bf16[192,3072]{1,0:T(8,128)(2,1)S(1)}, bf16[192,3072]{1,0:T(8,128)(2,1)}, u32[]{:S(2)}) copy-start(bf16[192,3072]{1,0:T(8,128)(2,1)} %copy-done.2) | copy-start | bytes 3538948
  86.4 12.1 %collective-permute-start.14 = (bf16[64,3072]{1,0:T(8,128)(2,1)S(1)}, bf16[64,3072]{1,0:T(8,128)(2,1)S(1)}, u32[]{:S(2)}, u32[]{:S(2)}) collective-permute-start(bf16[64,3072]{1,0:T(8,128)(2,1)S(1)} %slice.50), channel_id=1, source_target_pairs={{6,0},{7,1},{0,2},{1,3},{2,4},{3,5},{4,6},{5,7},{14,8},{15,9},{8,1... | collective-permute-start | bytes 1179656 | tf_op jit(solution)/shard_map/ppermute | solution.py:61
  87.8 10.7 %collective-permute-start.15 = (bf16[64,3072]{1,0:T(8,128)(2,1)S(1)}, bf16[64,3072]{1,0:T(8,128)(2,1)S(1)}, u32[]{:S(2)}, u32[]{:S(2)}) collective-permute-start(bf16[64,3072]{1,0:T(8,128)(2,1)S(1)} %pad_maximum_fusion.3), channel_id=1, source_target_pairs={{0,1},{1,0},{2,3},{3,2},{4,5},{5,4},{6,7},{7,6},{8,9},{9,8},{10,11... | collective-permute-start | bytes 1179656 | tf_op jit(solution)/shard_map/ppermute | solution.py:65
  88.4 10.1 %collective-permute-start.16 = (bf16[64,3072]{1,0:T(8,128)(2,1)S(1)}, bf16[64,3072]{1,0:T(8,128)(2,1)S(1)}, u32[]{:S(2)}, u32[]{:S(2)}) collective-permute-start(bf16[64,3072]{1,0:T(8,128)(2,1)S(1)} %slice.53), channel_id=1, source_target_pairs={{2,0},{3,1},{4,2},{5,3},{6,4},{7,5},{0,6},{1,7},{10,8},{11,9},{12,... | collective-permute-start | bytes 1179656 | tf_op jit(solution)/shard_map/ppermute | solution.py:61
  90.1 8.4 %copy-start.9 = (bf16[768,256]{1,0:T(8,128)(2,1)S(1)}, bf16[768,256]{1,0:T(8,128)(2,1)}, u32[]{:S(2)}) copy-start(bf16[768,256]{1,0:T(8,128)(2,1)} %copy-done.8) | copy-start | bytes 1179652
  90.1 8.4 %copy-start.13 = (bf16[2,1024,1024]{2,1,0:T(8,128)(2,1)S(1)}, bf16[2,1024,1024]{2,1,0:T(8,128)(2,1)}, u32[]{:S(2)}) copy-start(bf16[2,1024,1024]{2,1,0:T(8,128)(2,1)} %get-tuple-element.241.home_prob_ref) | copy-start | bytes 12582916
  108.0 34.0 %all-to-all-start.1 = ((bf16[8,192,768]{2,1,0:T(8,128)(2,1)}), bf16[8,192,768]{2,1,0:T(8,128)(2,1)S(1)}, u32[]{:S(2)}, u32[]{:S(2)}) async-start(bf16[8,192,768]{2,1,0:T(8,128)(2,1)} %bitcast.34), calls=%async_computation.1 | async-start | bytes 4718592 | tf_op jit(solution)/shard_map/all_to_all | solution.py:471
  112.3 2.6 %collective-permute-start.17 = (bf16[4,256,384]{2,1,0:T(8,128)(2,1)}, bf16[4,256,384]{2,1,0:T(8,128)(2,1)}, u32[]{:S(2)}, u32[]{:S(2)}) collective-permute-start(bf16[4,256,384]{2,1,0:T(8,128)(2,1)} %get-tuple-element.251), channel_id=1, source_target_pairs={{0,8},{8,0},{16,24},{24,16},{32,40},{40,32},{48,56},{56,48},{64,72... | collective-permute-start | bytes 2359304 | tf_op jit(solution)/shard_map/ppermute | solution.py:382
  117.1 13.0 %collective-permute-start.20 = (bf16[384,256]{1,0:T(8,128)(2,1)}, bf16[384,256]{1,0:T(8,128)(2,1)S(1)}, u32[]{:S(2)}, u32[]{:S(2)}) collective-permute-start(bf16[384,256]{1,0:T(8,128)(2,1)} %get-tuple-element.255), channel_id=1, source_target_pairs={{32,0},{40,8},{48,16},{56,24},{64,32},{72,40},{80,48},{88,56},{96,... | collective-permute-start | bytes 589832 | tf_op jit(solution)/shard_map/ppermute | solution.py:61
  121.2 9.5 %collective-permute-start.19 = (bf16[384,256]{1,0:T(8,128)(2,1)}, bf16[384,256]{1,0:T(8,128)(2,1)S(1)}, u32[]{:S(2)}, u32[]{:S(2)}) collective-permute-start(bf16[384,256]{1,0:T(8,128)(2,1)} %get-tuple-element.254), channel_id=1, source_target_pairs={{64,0},{72,8},{80,16},{88,24},{96,32},{104,40},{112,48},{120,56},{... | collective-permute-start | bytes 589832 | tf_op jit(solution)/shard_map/ppermute | solution.py:61
  121.2 12.1 %collective-permute-start.18 = (bf16[384,256]{1,0:T(8,128)(2,1)S(1)}, bf16[384,256]{1,0:T(8,128)(2,1)S(1)}, u32[]{:S(2)}, u32[]{:S(2)}) collective-permute-start(bf16[384,256]{1,0:T(8,128)(2,1)S(1)} %get-tuple-element.253), channel_id=1, source_target_pairs={{96,0},{104,8},{112,16},{120,24},{0,32},{8,40},{16,48},{24,56},{32... | collective-permute-start | bytes 589832 | tf_op jit(solution)/shard_map/ppermute | solution.py:61
  133.4 7.8 %collective-permute-start.21 = (bf16[192,256]{1,0:T(8,128)(2,1)S(1)}, bf16[192,256]{1,0:T(8,128)(2,1)S(1)}, u32[]{:S(2)}, u32[]{:S(2)}) collective-permute-start(bf16[192,256]{1,0:T(8,128)(2,1)S(1)} %select_convert_fusion), channel_id=1, source_target_pairs={{0,16},{8,24},{16,0},{24,8},{32,48},{40,56},{48,32},{56,40},{64,80... | collective-permute-start | bytes 294920 | tf_op jit(solution)/shard_map/ppermute | solution.py:389
  (8 other events, 28.5 us)

commit v6 on v5

--- a/solution.py
+++ b/solution.py
@@ -18,7 +18,6 @@
 MOVE_MIN = 256
 FAR_PIECES = (96, 128, 96, 128, 64, 64)
 QB = 256
-BQ = 1024
 SCALE = HD ** (-0.5)
 EXP2_SCALE = SCALE * 1.4426950408889634
 NEG_BIG = -1e30
@@ -35,7 +34,7 @@
 
 
 def flip(x):
-    return x.astype(jnp.float32).T.astype(x.dtype)
+    return x.T
 
 
 def apart_kernel(packed_ref, *outs):
@@ -232,41 +231,29 @@
     )(meta, moved, home_att, weight, *blocks)
 
 
-def backward_clip(read, rows, prob_ref, row_first, ga_ref, att_ref, out_ref, key_acc, value_acc):
-    block_rows = min(rows, BQ)
-    k_t = [flip(read(1, head, 0, rows)) for head in range(2)]
-    key_acc[:rows, :] = jnp.zeros((rows, FEAT), jnp.float32)
-    value_acc[:rows, :] = jnp.zeros((rows, FEAT), jnp.float32)
-
-    def block(step, _):
-        first = pl.multiple_of(step * block_rows, block_rows)
-        there = pl.ds(pl.multiple_of(row_first + first, 128), block_rows)
-        for head in range(2):
-            side = slice(head * HD, (head + 1) * HD)
-            q = read(0, head, first, block_rows)
-            v = read(2, head, 0, rows)
-            prob = prob_ref[head, :, pl.ds(first, block_rows)]
-            grad_att = ga_ref[there, side]
-            product = grad_att.astype(jnp.float32) * att_ref[there, side].astype(jnp.float32)
-            row_dot = jnp.sum(product.T, axis=0, keepdims=True)
-            grad_prob = dot(v, grad_att, NT)
-            grad_score = (prob.astype(jnp.float32) * (grad_prob - row_dot)).astype(jnp.bfloat16)
-            value_acc[:rows, side] += dot(prob, grad_att)
-            key_acc[:rows, side] += dot(grad_score, q)
-            grad_query = (dot(k_t[head], grad_score) * SCALE).T.astype(jnp.bfloat16)
-            out_ref[there, side] = grad_query
-        return 0
-
-    lax.fori_loop(0, rows // block_rows, block, 0)
-    whole = pl.ds(pl.multiple_of(row_first, 128), rows)
-    out_ref[whole, FEAT : 2 * FEAT] = (key_acc[:rows, :] * SCALE).astype(jnp.bfloat16)
-    out_ref[whole, 2 * FEAT :] = value_acc[:rows, :].astype(jnp.bfloat16)
+def backward_clip(read, rows, prob_ref, row_first, ga_ref, att_ref, out_ref):
+    there = pl.ds(pl.multiple_of(row_first, 128), rows)
+    for head in range(2):
+        side = slice(head * HD, (head + 1) * HD)
+        k_t = flip(read(1, head, 0, rows))
+        prob = prob_ref[head]
+        grad_att = ga_ref[there, side]
+        product = grad_att.astype(jnp.float32) * att_ref[there, side].astype(jnp.float32)
+        row_dot = jnp.sum(product.T, axis=0, keepdims=True)
+        grad_prob = dot(read(2, head, 0, rows), grad_att, NT)
+        grad_score = (prob.astype(jnp.float32) * (grad_prob - row_dot)).astype(jnp.bfloat16)
+        grad_value = dot(prob, grad_att)
+        grad_key = dot(grad_score, read(0, head, 0, rows)) * SCALE
+        grad_query = (dot(k_t, grad_score) * SCALE).T
+        out_ref[there, columns(0, head)] = grad_query.astype(jnp.bfloat16)
+        out_ref[there, columns(1, head)] = grad_key.astype(jnp.bfloat16)
+        out_ref[there, columns(2, head)] = grad_value.astype(jnp.bfloat16)
 
 
 def backward_kernel(
     meta_ref, qkv_ref, move_ref, att_ref, home_prob_ref, move_prob_ref,
     near_ref, far_ref, weight_ref, last_a, last_b, last_c, sum_ref,
-    grads_ref, send_ref, keep_ref, out_ref, ga_ref, key_acc, value_acc, sent_ref, done,
+    grads_ref, send_ref, keep_ref, out_ref, ga_ref, sent_ref, done,
 ):
     home_first, home_len = meta_ref[0], meta_ref[1]
     half = ROWS // 2
@@ -309,14 +296,14 @@
 
     out_ref[HOME:, :] = jnp.zeros((GROUP - HOME, 3 * FEAT), jnp.bfloat16)
     backward_clip(
-        read_home, HOME, home_prob_ref, 0, ga_ref, att_ref, out_ref, key_acc, value_acc
+        read_home, HOME, home_prob_ref, 0, ga_ref, att_ref, out_ref
     )
     start = pltpu.make_async_copy(
         out_ref.at[:HOME_MIN, :], grads_ref.at[:HOME_MIN, :], done.at[0]
     )
     start.start()
     backward_clip(
-        read_move, MOVE, move_prob_ref, home_len, ga_ref, att_ref, out_ref, key_acc, value_acc
+        read_move, MOVE, move_prob_ref, home_len, ga_ref, att_ref, out_ref
     )
     end = pltpu.make_async_copy(
         out_ref.at[HOME_MIN:, :], grads_ref.at[HOME_MIN:, :], done.at[1]
@@ -340,8 +327,6 @@
         scratch_shapes=[
             pltpu.VMEM((GROUP, 3 * FEAT), jnp.bfloat16),
             pltpu.VMEM((GROUP, FEAT), jnp.bfloat16),
-            pltpu.VMEM((HOME, FEAT), jnp.float32),
-            pltpu.VMEM((HOME, FEAT), jnp.float32),
             pltpu.VMEM((4, FEAT, D // 8), jnp.bfloat16),
             pltpu.SemaphoreType.DMA((3,)),
         ],
@@ -416,9 +401,9 @@
             clip_len[2 * source_group + 1],
             jnp.int32(0),
             me * ROWS,
-            (me ^ 1) * ROWS,
             up,
             down,
+            (me ^ 1) * ROWS,
             far_a,
             far_c,
             far_a + half,
@@ -430,9 +415,9 @@
         ]
     ).astype(jnp.int32)
 
-    dy_x = swapped(out_grad)
     dy_up = shifted(out_grad, "head", 2)
     dy_down = shifted(out_grad, "head", -2)
+    dy_x = swapped(out_grad)
 
     packed = jnp.concatenate(
         [x.reshape(ROWS, 8, FEAT) for x in (query_rows, key_rows, value_rows)], axis=2
@@ -446,7 +431,7 @@
     got_down = shifted(jnp.concatenate([dy_down[half:], dy_x[third:]]), "head", -2)
     got_x = swapped(jnp.concatenate([dy_down[:third], dy_up[2 * third :]]))
 
-    near_blocks = [out_grad, dy_x, dy_up, dy_down]
+    near_blocks = [out_grad, dy_up, dy_down, dy_x]
     moved, home_att, home_prob, near = lax.switch(
         rotate_by - 1,
         [functools.partial(arriving, d) for d in range(1, groups // 2 + 1)],

time: 144 us -> 144 us (level)
  starting transfers between devices: 37.1 us -> 33.2 us
  waiting for transfers between devices: 46.9 us -> 50.7 us
    ppermute x10, starting transfers between devices: 18.8 us -> 14.7 us  [shifted(): return lax.ppermute(x, axis, [((i - distance) % n, i) for i in range(n)])]
    ppermute x10, waiting for transfers between devices: 18.4 us -> 22.3 us  [shifted(): return lax.ppermute(x, axis, [((i - distance) % n, i) for i in range(n)])]
  transfers between devices with their start and end apart: 17 -> 17, of which waited for: 10 -> 11; matrix products, arithmetic and copies ran while one was open for 10% -> 10% of each run, Pallas kernels for 19% -> 19%
where the time goes in v6:
time: 144 us; the launch traced here: 143 us
  waiting for transfers between devices  50.7 us (35%)
  Pallas kernels  37.5 us (26%)
  starting transfers between devices  33.2 us (23%)
  local copies, waits for them, and re-layouts  13.2 us (9%)
  other arithmetic  4.4 us (3%)
  between operations  4.27 us (3%)
    ppermute x10, waiting for transfers between devices, shifted(): return lax.ppermute(x, axis, [((i - distance) % n, i) for i in range(n)])  22.3 us
    ppermute x3, waiting for transfers between devices, swapped(): return lax.ppermute(x, 'head', [(i, i ^ 1) for i in range(8)])  15 us
    ppermute x10, starting transfers between devices, shifted(): return lax.ppermute(x, axis, [((i - distance) % n, i) for i in range(n)])  14.7 us
    pallas_call x1, Pallas kernels, forward_home(): pl.pallas_call(forward_home_kernel, out_shape=(jax.ShapeDtypeStruct((HOME...  12 us
    pallas_call x1, Pallas kernels, backward(): pl.pallas_call(backward_kernel, out_shape=(pltpu.HBM((GROUP, 3 * FEAT), j...  9.44 us
    pallas_call x1, Pallas kernels, middle(): pl.pallas_call(functools.partial(middle_kernel, pieces, len(far)), grid=(...  8.31 us
    ppermute x3, starting transfers between devices, swapped(): return lax.ppermute(x, 'head', [(i, i ^ 1) for i in range(8)])  6.77 us
    all_to_all x1, waiting for transfers between devices, local(): lax.all_to_all(packed, 'head', split_axis=1, concat_axis=0, tiled=False)  5.85 us
  transfers between devices with their start and end apart: 17, of which 11 were waited for; matrix products, arithmetic and copies ran while one was open for 10% of the time, Pallas kernels for 19%

profile of v6, /device:TPU:0, one launch (start us, length us, event | category | flops | bytes accessed | tf_op | source)
XLA Modules:
  0.0 143.3 jit_solution(11364864120049607992)
XLA Ops:
  3.9 1.7 %collective-permute-start.9 = (bf16[192,3072]{1,0:T(8,128)(2,1)}, bf16[192,3072]{1,0:T(8,128)(2,1)S(1)}, u32[]{:S(2)}, u32[]{:S(2)}) collective-permute-start(bf16[192,3072]{1,0:T(8,128)(2,1)} %refs_0_.1), channel_id=1, source_target_pairs={{2,0},{3,1},{4,2},{5,3},{6,4},{7,5},{0,6},{1,7},{10,8},{11,9},{12,... | collective-permute-start | bytes 3538952 | tf_op jit(solution)/shard_map/ppermute | solution.py:60
  8.6 1.9 %copy.15 = bf16[1,192,8,768]{3,1,0,2:T(8,128)(2,1)} copy(bf16[1,192,8,768]{3,2,1,0:T(8,128)(2,1)S(1)} %maximum_bitcast_fusion) | data formatting | bytes 4718592 | tf_op jit(solution)/shard_map/broadcast_in_dim | solution.py:425
  10.4 4.4 %all-to-all-start = ((bf16[1,192,8,768]{3,1,0,2:T(8,128)(2,1)}), bf16[1,192,8,768]{3,1,0,2:T(8,128)(2,1)}, u32[]{:S(2)}, u32[]{:S(2)}) async-start(bf16[1,192,8,768]{3,1,0,2:T(8,128)(2,1)} %copy.15), calls=%async_computation | async-start | bytes 4718592 | tf_op jit(solution)/shard_map/all_to_all | solution.py:425
  14.8 15.0 %collective-permute-done.10.refs_3_ = bf16[192,3072]{1,0:T(8,128)(2,1)S(1)} collective-permute-done((bf16[192,3072]{1,0:T(8,128)(2,1)}, bf16[192,3072]{1,0:T(8,128)(2,1)S(1)}, u32[]{:S(2)}, u32[]{:S(2)}) %collective-permute-start.10) | collective-permute-done | bytes 1179680 | tf_op jit(solution)/shard_map/ppermute | solution.py:64
  30.0 2.6 %collective-permute-done.8.refs_1_ = bf16[192,3072]{1,0:T(8,128)(2,1)S(1)} collective-permute-done((bf16[192,3072]{1,0:T(8,128)(2,1)}, bf16[192,3072]{1,0:T(8,128)(2,1)S(1)}, u32[]{:S(2)}, u32[]{:S(2)}) %collective-permute-start.8) | collective-permute-done | bytes 1179680 | tf_op jit(solution)/shard_map/ppermute | solution.py:60
  37.5 2.9 %collective-permute-start.12 = (bf16[224,3072]{1,0:T(8,128)(2,1)}, bf16[224,3072]{1,0:T(8,128)(2,1)S(1)}, u32[]{:S(2)}, u32[]{:S(2)}) collective-permute-start(bf16[224,3072]{1,0:T(8,128)(2,1)} %pad_maximum_fusion.1), channel_id=1, source_target_pairs={{2,0},{3,1},{4,2},{5,3},{6,4},{7,5},{0,6},{1,7},{10,8},{11,9},{12,... | collective-permute-start | bytes 4128776 | tf_op jit(solution)/shard_map/ppermute | solution.py:60
  42.4 4.5 %collective-permute-start.13 = (bf16[128,3072]{1,0:T(8,128)(2,1)}, bf16[128,3072]{1,0:T(8,128)(2,1)S(1)}, u32[]{:S(2)}, u32[]{:S(2)}) collective-permute-start(bf16[128,3072]{1,0:T(8,128)(2,1)} %pad_maximum_fusion.2), channel_id=1, source_target_pairs={{0,1},{1,0},{2,3},{3,2},{4,5},{5,4},{6,7},{7,6},{8,9},{9,8},{10,11... | collective-permute-start | bytes 2359304 | tf_op jit(solution)/shard_map/ppermute | solution.py:64
  51.4 2.0 %stack.51.meta_ref = s32[16]{0:T(128)S(1)} concatenate(s32[1]{0:T(128)} %get-tuple-element.259, s32[1]{0:T(128)} %get-tuple-element.264, s32[1]{0:T(128)} %get-tuple-element.265, s32[1]{0:T(128)} %constant.98.clone.1, s32[1]{0:T(128)} %bitcast.1, s32[1]{0:T(128)} %bitcast.2, s32[1]{0:T(128)} %bitcast.3, s32[1]{0:T(128)} %bitcast.4, s32[1]{0:T(128)} %bitcast.5, s32[1]{0:T(128)} %bitcast.6, ...), dimensions={0} | concatenate | bytes 128 | tf_op jit(solution)/shard_map/stack | solution.py:397
  53.4 5.8 %all-to-all-done = bf16[1,192,8,768]{3,1,0,2:T(8,128)(2,1)} async-done(((bf16[1,192,8,768]{3,1,0,2:T(8,128)(2,1)}), bf16[1,192,8,768]{3,1,0,2:T(8,128)(2,1)}, u32[]{:S(2)}, u32[]{:S(2)}) %all-to-all-start) | async-done | bytes 2359328 | tf_op jit(solution)/shard_map/all_to_all | solution.py:425
  61.2 23.9 %conditional.1 = (bf16[512,768]{1,0:T(8,128)(2,1)}, bf16[1024,256]{1,0:T(8,128)(2,1)}, bf16[2,1024,1024]{2,1,0:T(8,128)(2,1)}, bf16[768,256]{1,0:T(8,128)(2,1)S(1)}) conditional(s32[]{:T(128)} %clamp.3, (bf16[512,768]{1,0:T(8,128)(2,1)S(1)}, s32[16]{0:T(128)S(1)}, bf16[1536,768]{1,0:T(8,128)(2,1)}, ...), branch_computations={%region_0.1_spmd, %region_1.2_spmd, %region_2.3_spmd, %region_3.4_... | conditional | flops 6230400000 | bytes 11645000 | solution.py:435
  61.2 4.1 %grad_att.8 = bf16[768,256]{1,0:T(8,128)(2,1)S(1)} custom-call(bf16[256,3072]{1,0:T(8,128)(2,1)S(1)} %get-tuple-element.133.weight_ref, bf16[192,3072]{1,0:T(8,128)(2,1)} %get-tuple-element.134.refs_0_, bf16[192,3072]{1,0:T(8,128)(2,1)} %get-tuple-element.135.refs_1_, bf16[192,3072]{1,0:T(8,128)(2,1)} %get-tuple-element.136.refs_2_, ...), custom_call_target="tpu_custom_call" | custom-call | flops 230400000 | bytes 499200 | tf_op jit(solution)/shard_map/cond/branch_0_fun/grad_att/pallas_call | solution.py:148
  65.3 12.0 %forward_home.8 = (bf16[1024,256]{1,0:T(8,128)(2,1)}, bf16[2,1024,1024]{2,1,0:T(8,128)(2,1)}) custom-call(s32[16]{0:T(128)S(1)} %get-tuple-element.129.meta_ref, bf16[1536,768]{1,0:T(8,128)(2,1)} %get-tuple-element.130.qkv_ref), custom_call_target="tpu_custom_call" | custom-call | flops 6000000000 | bytes 8000000 | tf_op jit(solution)/shard_map/cond/branch_0_fun/forward_home/pallas_call | solution.py:111
  77.3 7.8 %collective-permute-done = bf16[512,768]{1,0:T(8,128)(2,1)} collective-permute-done((bf16[512,768]{1,0:T(8,128)(2,1)S(1)}, bf16[512,768]{1,0:T(8,128)(2,1)}, u32[]{:S(2)}, u32[]{:S(2)}) %collective-permute-start) | collective-permute-done | bytes 786464 | tf_op jit(solution)/shard_map/cond/branch_0_fun/ppermute | solution.py:60
  88.4 1.7 %collective-permute-start.16 = (bf16[64,3072]{1,0:T(8,128)(2,1)S(1)}, bf16[64,3072]{1,0:T(8,128)(2,1)S(1)}, u32[]{:S(2)}, u32[]{:S(2)}) collective-permute-start(bf16[64,3072]{1,0:T(8,128)(2,1)S(1)} %slice.53), channel_id=1, source_target_pairs={{2,0},{3,1},{4,2},{5,3},{6,4},{7,5},{0,6},{1,7},{10,8},{11,9},{12,... | collective-permute-start | bytes 1179656 | tf_op jit(solution)/shard_map/ppermute | solution.py:60
  90.1 8.3 %middle.1 = (bf16[1536,256]{1,0:T(8,128)(2,1)S(1)}, bf16[2,512,512]{2,1,0:T(8,128)(2,1)S(1)}, bf16[576,256]{1,0:T(8,128)(2,1)S(1)}, f32[4,256,768]{2,1,0:T(8,128)S(1)}) custom-call(s32[16]{0:T(128)S(1)} %stack.51.meta_ref, bf16[512,768]{1,0:T(8,128)(2,1)} %get-tuple-element.235.move_ref, bf16[1024,256]{1,0:T(8,128)(2,1)} %get-tuple-element.236.home_att_ref, ...), custom_call_target="tpu_custom_call" | custom-call | flops 806400000 | bytes 1344000 | tf_op jit(solution)/shard_map/middle/pallas_call | solution.py:200
  98.5 9.4 %backward.1 = (bf16[1536,768]{1,0:T(8,128)(2,1)}, bf16[4,256,384]{2,1,0:T(8,128)(2,1)}, bf16[4,256,384]{2,1,0:T(8,128)(2,1)S(1)}) custom-call(s32[16]{0:T(128)S(1)} %stack.51.meta_ref, bf16[1536,768]{1,0:T(8,128)(2,1)} %bitcast.16.qkv_ref, bf16[512,768]{1,0:T(8,128)(2,1)} %get-tuple-element.235.move_ref, bf16[1536,256]{1,0:T(8,128)(2,1)S(1)} %get-tuple-element.240.att_ref, ...), custom_call_target="tpu_custom_call" | custom-call | flops 10000000000 | bytes 12000000 | tf_op jit(solution)/shard_map/backward/pallas_call | solution.py:318
  107.9 4.5 %all-to-all-start.1 = ((bf16[8,192,768]{2,1,0:T(8,128)(2,1)}), bf16[8,192,768]{2,1,0:T(8,128)(2,1)S(1)}, u32[]{:S(2)}, u32[]{:S(2)}) async-start(bf16[8,192,768]{2,1,0:T(8,128)(2,1)} %bitcast.34), calls=%async_computation.1 | async-start | bytes 4718592 | tf_op jit(solution)/shard_map/all_to_all | solution.py:456
  112.5 2.6 %collective-permute-done.17.got_ref = bf16[4,256,384]{2,1,0:T(8,128)(2,1)} collective-permute-done((bf16[4,256,384]{2,1,0:T(8,128)(2,1)}, bf16[4,256,384]{2,1,0:T(8,128)(2,1)}, u32[]{:S(2)}, u32[]{:S(2)}) %collective-permute-start.17) | collective-permute-done | bytes 786464 | tf_op jit(solution)/shard_map/ppermute | solution.py:367
  115.1 2.1 %both_cores.1 = (bf16[384,256]{1,0:T(8,128)(2,1)S(1)}, bf16[384,256]{1,0:T(8,128)(2,1)S(1)}, bf16[384,256]{1,0:T(8,128)(2,1)}, bf16[384,256]{1,0:T(8,128)(2,1)}) custom-call(s32[1]{0:T(128)} %bitcast.21.z_ref, bf16[4,256,384]{2,1,0:T(8,128)(2,1)S(1)} %get-tuple-element.250.keep_ref, bf16[4,256,384]{2,1,0:T(8,128)(2,1)} %collective-permute-done.17.got_ref), custom_call_target="tpu_custom_call" | custom-call | bytes 3000000 | tf_op jit(solution)/shard_map/both_cores/pallas_call | solution.py:353
  117.2 3.9 %collective-permute-start.20 = (bf16[384,256]{1,0:T(8,128)(2,1)}, bf16[384,256]{1,0:T(8,128)(2,1)S(1)}, u32[]{:S(2)}, u32[]{:S(2)}) collective-permute-start(bf16[384,256]{1,0:T(8,128)(2,1)} %get-tuple-element.255), channel_id=1, source_target_pairs={{32,0},{40,8},{48,16},{56,24},{64,32},{72,40},{80,48},{88,56},{96,... | collective-permute-start | bytes 589832 | tf_op jit(solution)/shard_map/ppermute | solution.py:60
  122.4 7.7 %collective-permute-done.20 = bf16[384,256]{1,0:T(8,128)(2,1)S(1)} collective-permute-done((bf16[384,256]{1,0:T(8,128)(2,1)}, bf16[384,256]{1,0:T(8,128)(2,1)S(1)}, u32[]{:S(2)}, u32[]{:S(2)}) %collective-permute-start.20) | collective-permute-done | bytes 196640 | tf_op jit(solution)/shard_map/ppermute | solution.py:60
  130.6 2.6 %collective-permute-done.18 = bf16[384,256]{1,0:T(8,128)(2,1)S(1)} collective-permute-done((bf16[384,256]{1,0:T(8,128)(2,1)S(1)}, bf16[384,256]{1,0:T(8,128)(2,1)S(1)}, u32[]{:S(2)}, u32[]{:S(2)}) %collective-permute-start.18) | collective-permute-done | bytes 196640 | tf_op jit(solution)/shard_map/ppermute | solution.py:60
  133.4 2.8 %collective-permute-start.21 = (bf16[192,256]{1,0:T(8,128)(2,1)S(1)}, bf16[192,256]{1,0:T(8,128)(2,1)S(1)}, u32[]{:S(2)}, u32[]{:S(2)}) collective-permute-start(bf16[192,256]{1,0:T(8,128)(2,1)S(1)} %select_convert_fusion), channel_id=1, source_target_pairs={{0,16},{8,24},{16,0},{24,8},{32,48},{40,56},{48,32},{56,40},{64,80... | collective-permute-start | bytes 294920 | tf_op jit(solution)/shard_map/ppermute | solution.py:374
  136.2 4.9 %collective-permute-done.21 = bf16[192,256]{1,0:T(8,128)(2,1)S(1)} collective-permute-done((bf16[192,256]{1,0:T(8,128)(2,1)S(1)}, bf16[192,256]{1,0:T(8,128)(2,1)S(1)}, u32[]{:S(2)}, u32[]{:S(2)}) %collective-permute-start.21) | collective-permute-done | bytes 98336 | tf_op jit(solution)/shard_map/ppermute | solution.py:374
  (71 shorter events, 23.8 us)
Async XLA Ops:
  0.6 7.6 %copy-start.7 = (bf16[192,2048]{1,0:T(8,128)(2,1)S(1)}, bf16[192,2048]{1,0:T(8,128)(2,1)}, u32[]{:S(2)}) copy-start(bf16[192,2048]{1,0:T(8,128)(2,1)} %param.16) | copy-start | bytes 2359300
  0.6 29.2 %collective-permute-start.10 = (bf16[192,3072]{1,0:T(8,128)(2,1)}, bf16[192,3072]{1,0:T(8,128)(2,1)S(1)}, u32[]{:S(2)}, u32[]{:S(2)}) collective-permute-start(bf16[192,3072]{1,0:T(8,128)(2,1)} %refs_0_.1), channel_id=1, source_target_pairs={{0,1},{1,0},{2,3},{3,2},{4,5},{5,4},{6,7},{7,6},{8,9},{9,8},{10,11... | collective-permute-start | bytes 3538952 | tf_op jit(solution)/shard_map/ppermute | solution.py:64
  2.3 30.3 %collective-permute-start.8 = (bf16[192,3072]{1,0:T(8,128)(2,1)}, bf16[192,3072]{1,0:T(8,128)(2,1)S(1)}, u32[]{:S(2)}, u32[]{:S(2)}) collective-permute-start(bf16[192,3072]{1,0:T(8,128)(2,1)} %refs_0_.1), channel_id=1, source_target_pairs={{6,0},{7,1},{0,2},{1,3},{2,4},{3,5},{4,6},{5,7},{14,8},{15,9},{8,1... | collective-permute-start | bytes 3538952 | tf_op jit(solution)/shard_map/ppermute | solution.py:60
  3.9 31.4 %collective-permute-start.9 = (bf16[192,3072]{1,0:T(8,128)(2,1)}, bf16[192,3072]{1,0:T(8,128)(2,1)S(1)}, u32[]{:S(2)}, u32[]{:S(2)}) collective-permute-start(bf16[192,3072]{1,0:T(8,128)(2,1)} %refs_0_.1), channel_id=1, source_target_pairs={{2,0},{3,1},{4,2},{5,3},{6,4},{7,5},{0,6},{1,7},{10,8},{11,9},{12,... | collective-permute-start | bytes 3538952 | tf_op jit(solution)/shard_map/ppermute | solution.py:60
  10.4 48.8 %all-to-all-start = ((bf16[1,192,8,768]{3,1,0,2:T(8,128)(2,1)}), bf16[1,192,8,768]{3,1,0,2:T(8,128)(2,1)}, u32[]{:S(2)}, u32[]{:S(2)}) async-start(bf16[1,192,8,768]{3,1,0,2:T(8,128)(2,1)} %copy.15), calls=%async_computation | async-start | bytes 4718592 | tf_op jit(solution)/shard_map/all_to_all | solution.py:425
  34.9 51.1 %collective-permute-start.11 = (bf16[224,3072]{1,0:T(8,128)(2,1)}, bf16[224,3072]{1,0:T(8,128)(2,1)S(1)}, u32[]{:S(2)}, u32[]{:S(2)}) collective-permute-start(bf16[224,3072]{1,0:T(8,128)(2,1)} %pad_maximum_fusion), channel_id=1, source_target_pairs={{6,0},{7,1},{0,2},{1,3},{2,4},{3,5},{4,6},{5,7},{14,8},{15,9},{8,1... | collective-permute-start | bytes 4128776 | tf_op jit(solution)/shard_map/ppermute | solution.py:60
  35.3 6.1 %slice-start = ((bf16[192,3072]{1,0:T(8,128)(2,1)}), bf16[64,3072]{1,0:T(8,128)(2,1)S(1)}, s32[]{:S(2)}) async-start(bf16[192,3072]{1,0:T(8,128)(2,1)} %copy-done.5), calls=%async_computation.2 | async-start | bytes 786432 | tf_op jit(solution)/shard_map/slice | solution.py:432
  36.3 10.5 %copy-start.10 = (s32[32]{0:T(128)S(1)}, s32[32]{0:T(128)}, u32[]{:S(2)}) copy-start(s32[32]{0:T(128)} %param.22) | copy-start | bytes 388
  37.5 11.3 %copy-start.11 = (s32[32]{0:T(128)S(1)}, s32[32]{0:T(128)}, u32[]{:S(2)}) copy-start(s32[32]{0:T(128)} %param.23) | copy-start | bytes 388
  37.5 11.3 %copy-start.12 = (s32[32]{0:T(128)S(1)}, s32[32]{0:T(128)}, u32[]{:S(2)}) copy-start(s32[32]{0:T(128)} %param.21) | copy-start | bytes 388
  37.5 48.7 %collective-permute-start.12 = (bf16[224,3072]{1,0:T(8,128)(2,1)}, bf16[224,3072]{1,0:T(8,128)(2,1)S(1)}, u32[]{:S(2)}, u32[]{:S(2)}) collective-permute-start(bf16[224,3072]{1,0:T(8,128)(2,1)} %pad_maximum_fusion.1), channel_id=1, source_target_pairs={{2,0},{3,1},{4,2},{5,3},{6,4},{7,5},{0,6},{1,7},{10,8},{11,9},{12,... | collective-permute-start | bytes 4128776 | tf_op jit(solution)/shard_map/ppermute | solution.py:60
  42.4 42.8 %collective-permute-start.13 = (bf16[128,3072]{1,0:T(8,128)(2,1)}, bf16[128,3072]{1,0:T(8,128)(2,1)S(1)}, u32[]{:S(2)}, u32[]{:S(2)}) collective-permute-start(bf16[128,3072]{1,0:T(8,128)(2,1)} %pad_maximum_fusion.2), channel_id=1, source_target_pairs={{0,1},{1,0},{2,3},{3,2},{4,5},{5,4},{6,7},{7,6},{8,9},{9,8},{10,11... | collective-permute-start | bytes 2359304 | tf_op jit(solution)/shard_map/ppermute | solution.py:64
  61.2 23.9 %collective-permute-start = (bf16[512,768]{1,0:T(8,128)(2,1)S(1)}, bf16[512,768]{1,0:T(8,128)(2,1)}, u32[]{:S(2)}, u32[]{:S(2)}) collective-permute-start(bf16[512,768]{1,0:T(8,128)(2,1)S(1)} %get-tuple-element.128), channel_id=1, source_target_pairs={{120,0},{0,8},{8,16},{16,24},{24,32},{32,40},{40,48},{48,56},{56,6... | collective-permute-start | bytes 2359304 | tf_op jit(solution)/shard_map/cond/branch_0_fun/ppermute | solution.py:60
  86.4 12.1 %collective-permute-start.14 = (bf16[64,3072]{1,0:T(8,128)(2,1)S(1)}, bf16[64,3072]{1,0:T(8,128)(2,1)S(1)}, u32[]{:S(2)}, u32[]{:S(2)}) collective-permute-start(bf16[64,3072]{1,0:T(8,128)(2,1)S(1)} %slice.50), channel_id=1, source_target_pairs={{6,0},{7,1},{0,2},{1,3},{2,4},{3,5},{4,6},{5,7},{14,8},{15,9},{8,1... | collective-permute-start | bytes 1179656 | tf_op jit(solution)/shard_map/ppermute | solution.py:60
  87.8 10.6 %collective-permute-start.15 = (bf16[64,3072]{1,0:T(8,128)(2,1)S(1)}, bf16[64,3072]{1,0:T(8,128)(2,1)S(1)}, u32[]{:S(2)}, u32[]{:S(2)}) collective-permute-start(bf16[64,3072]{1,0:T(8,128)(2,1)S(1)} %pad_maximum_fusion.3), channel_id=1, source_target_pairs={{0,1},{1,0},{2,3},{3,2},{4,5},{5,4},{6,7},{7,6},{8,9},{9,8},{10,11... | collective-permute-start | bytes 1179656 | tf_op jit(solution)/shard_map/ppermute | solution.py:64
  88.4 10.0 %collective-permute-start.16 = (bf16[64,3072]{1,0:T(8,128)(2,1)S(1)}, bf16[64,3072]{1,0:T(8,128)(2,1)S(1)}, u32[]{:S(2)}, u32[]{:S(2)}) collective-permute-start(bf16[64,3072]{1,0:T(8,128)(2,1)S(1)} %slice.53), channel_id=1, source_target_pairs={{2,0},{3,1},{4,2},{5,3},{6,4},{7,5},{0,6},{1,7},{10,8},{11,9},{12,... | collective-permute-start | bytes 1179656 | tf_op jit(solution)/shard_map/ppermute | solution.py:60
  90.1 8.4 %copy-start.9 = (bf16[768,256]{1,0:T(8,128)(2,1)S(1)}, bf16[768,256]{1,0:T(8,128)(2,1)}, u32[]{:S(2)}) copy-start(bf16[768,256]{1,0:T(8,128)(2,1)} %copy-done.8) | copy-start | bytes 1179652
  90.1 8.4 %copy-start.13 = (bf16[2,1024,1024]{2,1,0:T(8,128)(2,1)S(1)}, bf16[2,1024,1024]{2,1,0:T(8,128)(2,1)}, u32[]{:S(2)}) copy-start(bf16[2,1024,1024]{2,1,0:T(8,128)(2,1)} %get-tuple-element.241.home_prob_ref) | copy-start | bytes 12582916
  107.9 33.9 %all-to-all-start.1 = ((bf16[8,192,768]{2,1,0:T(8,128)(2,1)}), bf16[8,192,768]{2,1,0:T(8,128)(2,1)S(1)}, u32[]{:S(2)}, u32[]{:S(2)}) async-start(bf16[8,192,768]{2,1,0:T(8,128)(2,1)} %bitcast.34), calls=%async_computation.1 | async-start | bytes 4718592 | tf_op jit(solution)/shard_map/all_to_all | solution.py:456
  112.4 2.6 %collective-permute-start.17 = (bf16[4,256,384]{2,1,0:T(8,128)(2,1)}, bf16[4,256,384]{2,1,0:T(8,128)(2,1)}, u32[]{:S(2)}, u32[]{:S(2)}) collective-permute-start(bf16[4,256,384]{2,1,0:T(8,128)(2,1)} %get-tuple-element.251), channel_id=1, source_target_pairs={{0,8},{8,0},{16,24},{24,16},{32,40},{40,32},{48,56},{56,48},{64,72... | collective-permute-start | bytes 2359304 | tf_op jit(solution)/shard_map/ppermute | solution.py:367
  117.2 12.9 %collective-permute-start.20 = (bf16[384,256]{1,0:T(8,128)(2,1)}, bf16[384,256]{1,0:T(8,128)(2,1)S(1)}, u32[]{:S(2)}, u32[]{:S(2)}) collective-permute-start(bf16[384,256]{1,0:T(8,128)(2,1)} %get-tuple-element.255), channel_id=1, source_target_pairs={{32,0},{40,8},{48,16},{56,24},{64,32},{72,40},{80,48},{88,56},{96,... | collective-permute-start | bytes 589832 | tf_op jit(solution)/shard_map/ppermute | solution.py:60
  121.1 9.5 %collective-permute-start.19 = (bf16[384,256]{1,0:T(8,128)(2,1)}, bf16[384,256]{1,0:T(8,128)(2,1)S(1)}, u32[]{:S(2)}, u32[]{:S(2)}) collective-permute-start(bf16[384,256]{1,0:T(8,128)(2,1)} %get-tuple-element.254), channel_id=1, source_target_pairs={{64,0},{72,8},{80,16},{88,24},{96,32},{104,40},{112,48},{120,56},{... | collective-permute-start | bytes 589832 | tf_op jit(solution)/shard_map/ppermute | solution.py:60
  121.1 12.1 %collective-permute-start.18 = (bf16[384,256]{1,0:T(8,128)(2,1)S(1)}, bf16[384,256]{1,0:T(8,128)(2,1)S(1)}, u32[]{:S(2)}, u32[]{:S(2)}) collective-permute-start(bf16[384,256]{1,0:T(8,128)(2,1)S(1)} %get-tuple-element.253), channel_id=1, source_target_pairs={{96,0},{104,8},{112,16},{120,24},{0,32},{8,40},{16,48},{24,56},{32... | collective-permute-start | bytes 589832 | tf_op jit(solution)/shard_map/ppermute | solution.py:60
  133.4 7.7 %collective-permute-start.21 = (bf16[192,256]{1,0:T(8,128)(2,1)S(1)}, bf16[192,256]{1,0:T(8,128)(2,1)S(1)}, u32[]{:S(2)}, u32[]{:S(2)}) collective-permute-start(bf16[192,256]{1,0:T(8,128)(2,1)S(1)} %select_convert_fusion), channel_id=1, source_target_pairs={{0,16},{8,24},{16,0},{24,8},{32,48},{40,56},{48,32},{56,40},{64,80... | collective-permute-start | bytes 294920 | tf_op jit(solution)/shard_map/ppermute | solution.py:374
  (8 other events, 21.0 us)
